TPU v7x, 32 devices: a whole 2x2x4 slice. The times are simulated.
32 devices in a mesh: dp: 32 (over z, y, x, core).
Axes of the slice: x: 2, y: 2, z: 4, core: 2. Of those that a mesh axis runs over, the one named last changes fastest.
Arguments:
- images: bfloat16 [512, 14, 14, 384], P('dp'), may hold values from -6 to 6
- mix_weight: float32 [512], P('dp'), may hold values from 0.5 to 1
- partner: int32 [512], P('dp'), may hold values from 0 to 511, as said below
- keep_mask: int32 [512], P('dp'), may hold values 0 or 1
- cotangent: bfloat16 [512, 7, 7, 768], P('dp'), may hold values from -6 to 6
- weight_in: float32 [1536, 384], P('dp')
- weight_out: float32 [1536, 384], P('dp')
- weight_down: float32 [1536, 768], P('dp'), may hold values from -0.15625 to 0.15625
- small_params: float32 [23808], P('dp')
- first_in: float32 [1536, 384], P('dp'), may hold values from -0.0009765625 to 0.0009765625
- second_in: float32 [1536, 384], P('dp'), may hold values from 4.196208e-10 to 1.6784832e-09
- first_out: float32 [1536, 384], P('dp'), may hold values from -0.0009765625 to 0.0009765625
- second_out: float32 [1536, 384], P('dp'), may hold values from 4.196208e-10 to 1.6784832e-09
- first_down: float32 [1536, 768], P('dp'), may hold values from -0.0009765625 to 0.0009765625
- second_down: float32 [1536, 768], P('dp'), may hold values from 4.196208e-10 to 1.6784832e-09
- first_small: float32 [23808], P('dp'), may hold values from -0.0009765625 to 0.0009765625
- second_small: float32 [23808], P('dp'), may hold values from 4.196208e-10 to 1.6784832e-09
Outputs:
- output: bfloat16 [512, 7, 7, 768], P('dp')
- images_grad: float32 [512, 14, 14, 384], P('dp')
- grad_norm: float32 [], replicated
- new_first_in: float32 [1536, 384], P('dp')
- new_second_in: float32 [1536, 384], P('dp')
- new_weight_in: float32 [1536, 384], P('dp')
- new_first_out: float32 [1536, 384], P('dp')
- new_second_out: float32 [1536, 384], P('dp')
- new_weight_out: float32 [1536, 384], P('dp')
- new_first_down: float32 [1536, 768], P('dp')
- new_second_down: float32 [1536, 768], P('dp')
- new_weight_down: float32 [1536, 768], P('dp')
- new_first_small: float32 [23808], P('dp')
- new_second_small: float32 [23808], P('dp')
- new_small_params: float32 [23808], P('dp')
Inputs may be any that keep to these rules, and one draw needn't show every extreme that they name: The partner of each image lies in the same aligned block of 16 images (one device's), and within each block the partners are a permutation of its images.
All inputs are finite; a program needn't handle non-finite values. No bound on the sum of `keep_mask` on one device may be relied on, other than what follows from the above.
Results may differ from a plain program's by a relative error of at most 0.0089.
Values may be sent and summed in bfloat16 or wider, within the bound.
No kernel may reach another device: no remote copies, remote signals or barrier semaphores. Data moves between devices by JAX's collectives and lax.ppermute only.
A program may use at most 192 MiB of HBM per device.

v0:
```python
import jax
import jax.numpy as jnp
from jax import lax
from jax.sharding import PartitionSpec as P

D = 384
FF = 1536
STEP = 10


LN_EPS = 1e-06
DROP_RATE = 0.2
RATE_MATRIX = 0.05
RATE_VECTOR = 0.3
LAYER_DECAY = 0.8
BETA_ONE = 0.9
BETA_TWO = 0.999
ADAM_EPS = 1e-08
WEIGHT_DECAY = 0.05
CLIP_NORM = 1.0
PRECISE = lax.Precision.HIGHEST
ROW_CONTRACT = (((0,), (0,)), ((), ()))
COL_CONTRACT = (((1,), (1,)), ((), ()))


def split_small(small_vec):
    sizes_list = [49 * D, D, D, D, FF, D, D, D, D, 2 * D]
    pieces = []
    begin_at = 0
    for length in sizes_list:
        pieces.append(small_vec[begin_at : begin_at + length])
        begin_at = begin_at + length
    pieces[0] = pieces[0].reshape(49, D)
    return pieces


def norm_parts(values, gain_vec, bias_vec):
    average = jnp.mean(values, axis=-1, keepdims=True)
    centred = values - average
    variance = jnp.mean(centred * centred, axis=-1, keepdims=True)
    inverse = lax.rsqrt(variance + LN_EPS)
    unit_vals = centred * inverse
    return (unit_vals * gain_vec + bias_vec, unit_vals, inverse)


def norm_back(back_vals, unit_vals, inverse, gain_vec):
    scaled_back = back_vals * gain_vec
    mean_one = jnp.mean(scaled_back, axis=-1, keepdims=True)
    mean_two = jnp.mean(scaled_back * unit_vals, axis=-1, keepdims=True)
    return inverse * (scaled_back - mean_one - unit_vals * mean_two)


def gelu_exact(values):
    return jax.nn.gelu(values, approximate=False)


def forward(gathered, mixed_in, keep_scale):
    weight_in, weight_out, weight_down, small_vec = gathered
    (
        depth_kernel,
        depth_bias,
        gain_one,
        bias_one,
        hidden_bias,
        out_bias,
        layer_scale,
        gain_two,
        bias_two,
        down_bias,
    ) = split_small(small_vec.astype(jnp.float32))
    images_dev, side_len = (mixed_in.shape[0], mixed_in.shape[1])
    half_len = side_len // 2
    pixels = images_dev * side_len * side_len
    padded = jnp.pad(mixed_in, ((0, 0), (3, 3), (3, 3), (0, 0)))
    conv_out = jnp.zeros_like(mixed_in) + depth_bias
    for row_off in range(7):
        for col_off in range(7):
            conv_out = (
                conv_out
                + padded[:, row_off : row_off + side_len, col_off : col_off + side_len, :]
                * depth_kernel[row_off * 7 + col_off]
            )
    normed_full, unit_one, inverse_one = norm_parts(conv_out, gain_one, bias_one)
    normed_one = normed_full.astype(jnp.bfloat16).reshape(pixels, D)
    hidden_pre = (
        lax.dot_general(normed_one, weight_in, COL_CONTRACT, preferred_element_type=jnp.float32)
        + hidden_bias
    )
    hidden_act = gelu_exact(hidden_pre).astype(jnp.bfloat16)
    branch = jnp.dot(hidden_act, weight_out, preferred_element_type=jnp.float32) + out_bias
    keep_col = keep_scale[:, None, None, None]
    residual = mixed_in + keep_col * layer_scale * branch.reshape(mixed_in.shape)
    normed_full_two, unit_two, inverse_two = norm_parts(residual, gain_two, bias_two)
    normed_two = normed_full_two.astype(jnp.bfloat16)
    patches = (
        normed_two.reshape(images_dev, half_len, 2, half_len, 2, D)
        .transpose(0, 1, 3, 5, 2, 4)
        .reshape(images_dev * half_len * half_len, 4 * D)
    )
    result = jnp.dot(patches, weight_down, preferred_element_type=jnp.float32) + down_bias
    result = result.reshape(images_dev, half_len, half_len, 2 * D)
    return (
        padded,
        unit_one,
        inverse_one,
        normed_one,
        hidden_pre,
        hidden_act,
        branch,
        unit_two,
        inverse_two,
        patches,
        result,
    )


def backward(gathered, kept_values, cotangent, keep_scale):
    weight_in, weight_out, weight_down, small_vec = gathered
    (
        depth_kernel,
        depth_bias,
        gain_one,
        bias_one,
        hidden_bias,
        out_bias,
        layer_scale,
        gain_two,
        bias_two,
        down_bias,
    ) = split_small(small_vec.astype(jnp.float32))
    (
        padded,
        unit_one,
        inverse_one,
        normed_one,
        hidden_pre,
        hidden_act,
        branch,
        unit_two,
        inverse_two,
        patches,
        result,
    ) = kept_values
    images_dev, side_len = (unit_one.shape[0], unit_one.shape[1])
    half_len = side_len // 2
    cot_rows = cotangent.reshape(images_dev * half_len * half_len, 2 * D)
    grad_down = lax.dot_general(patches, cot_rows, ROW_CONTRACT, preferred_element_type=jnp.float32)
    grad_down_bias = jnp.sum(cot_rows.astype(jnp.float32), axis=0)
    back_patch = lax.dot_general(
        cot_rows, weight_down, COL_CONTRACT, preferred_element_type=jnp.float32
    )
    back_two = (
        back_patch.reshape(images_dev, half_len, half_len, D, 2, 2)
        .transpose(0, 1, 4, 2, 5, 3)
        .reshape(images_dev, side_len, side_len, D)
    )
    grad_gain_two = jnp.sum(back_two * unit_two, axis=(0, 1, 2))
    grad_bias_two = jnp.sum(back_two, axis=(0, 1, 2))
    back_res = norm_back(back_two, unit_two, inverse_two, gain_two)
    keep_col = keep_scale[:, None, None, None]
    grad_layer = jnp.sum(back_res * keep_col * branch.reshape(back_res.shape), axis=(0, 1, 2))
    back_branch = (back_res * (keep_col * layer_scale)).astype(jnp.bfloat16).reshape(-1, D)
    grad_out_bias = jnp.sum(back_branch.astype(jnp.float32), axis=0)
    grad_out = lax.dot_general(
        hidden_act, back_branch, ROW_CONTRACT, preferred_element_type=jnp.float32
    )
    back_act = lax.dot_general(
        back_branch, weight_out, COL_CONTRACT, preferred_element_type=jnp.float32
    )
    _, gelu_pull = jax.vjp(gelu_exact, hidden_pre)
    back_pre = gelu_pull(back_act)[0].astype(jnp.bfloat16)
    grad_hidden_bias = jnp.sum(back_pre.astype(jnp.float32), axis=0)
    grad_in = lax.dot_general(
        back_pre, normed_one, ROW_CONTRACT, preferred_element_type=jnp.float32
    )
    back_one = jnp.dot(back_pre, weight_in, preferred_element_type=jnp.float32).reshape(
        images_dev, side_len, side_len, D
    )
    grad_gain_one = jnp.sum(back_one * unit_one, axis=(0, 1, 2))
    grad_bias_one = jnp.sum(back_one, axis=(0, 1, 2))
    back_conv = norm_back(back_one, unit_one, inverse_one, gain_one)
    grad_depth_bias = jnp.sum(back_conv, axis=(0, 1, 2))
    back_padded = jnp.pad(back_conv, ((0, 0), (3, 3), (3, 3), (0, 0)))
    kernel_rows = []
    back_mixed = back_res
    for row_off in range(7):
        for col_off in range(7):
            window = padded[:, row_off : row_off + side_len, col_off : col_off + side_len, :]
            kernel_rows.append(jnp.sum(window * back_conv, axis=(0, 1, 2)))
            back_mixed = (
                back_mixed
                + back_padded[
                    :, 6 - row_off : 6 - row_off + side_len, 6 - col_off : 6 - col_off + side_len, :
                ]
                * depth_kernel[row_off * 7 + col_off]
            )
    padding = jnp.zeros((small_vec.shape[0] - 58 * D - FF,), jnp.float32)
    grad_small = jnp.concatenate(
        [
            jnp.stack(kernel_rows).reshape(-1),
            grad_depth_bias,
            grad_gain_one,
            grad_bias_one,
            grad_hidden_bias,
            grad_out_bias,
            grad_layer,
            grad_gain_two,
            grad_bias_two,
            grad_down_bias,
            padding,
        ]
    )
    return (back_mixed, (grad_in, grad_out, grad_down, grad_small))


def adamw_step(weight, first_mom, second, gradient, step_rate, decay_rate):
    first_mom = BETA_ONE * first_mom + (1.0 - BETA_ONE) * gradient
    second = BETA_TWO * second + (1.0 - BETA_TWO) * gradient * gradient
    first_hat = first_mom / (1.0 - BETA_ONE**STEP)
    second_hat = second / (1.0 - BETA_TWO**STEP)
    weight = weight - step_rate * (
        first_hat / (jnp.sqrt(second_hat) + ADAM_EPS) + decay_rate * weight
    )
    return (first_mom, second, weight)


def local(
    images,
    mix_weight,
    partner,
    keep_mask,
    cotangent,
    weight_in,
    weight_out,
    weight_down,
    small_params,
    first_in,
    second_in,
    first_out,
    second_out,
    first_down,
    second_down,
    first_small,
    second_small,
):
    images_dev = images.shape[0]
    lowered = (
        weight_in.astype(jnp.bfloat16),
        weight_out.astype(jnp.bfloat16),
        weight_down.astype(jnp.bfloat16),
        small_params.astype(jnp.bfloat16),
    )
    gathered = (
        lax.all_gather(lowered[0], "dp", axis=0, tiled=True),
        lax.all_gather(lowered[1], "dp", axis=0, tiled=True),
        lax.all_gather(lowered[2], "dp", axis=0, tiled=True),
        lax.all_gather(lowered[3], "dp", axis=0, tiled=True),
    )
    first_image = lax.axis_index("dp") * images_dev
    local_partner = partner - first_image
    selector = local_partner[:, None] == jnp.arange(images_dev, dtype=jnp.int32)[None, :]
    flat_images = images.reshape(images_dev, -1)
    partner_rows = jnp.dot(
        selector.astype(jnp.bfloat16), flat_images, preferred_element_type=jnp.float32
    ).reshape(images.shape)
    mix_col = mix_weight[:, None, None, None]
    mixed_in = mix_col * images.astype(jnp.float32) + (1.0 - mix_col) * partner_rows
    keep_scale = keep_mask.astype(jnp.float32) / (1.0 - DROP_RATE)
    kept_values = forward(gathered, mixed_in, keep_scale)
    result = kept_values[-1]
    regathered = (
        lax.all_gather(lowered[0], "dp", axis=0, tiled=True),
        lax.all_gather(lowered[1], "dp", axis=0, tiled=True),
        lax.all_gather(lowered[2], "dp", axis=0, tiled=True),
        lax.all_gather(lowered[3], "dp", axis=0, tiled=True),
    )
    kept_values = forward(regathered, mixed_in, keep_scale)
    gathered = regathered
    back_mixed, gradients = backward(gathered, kept_values, cotangent, keep_scale)
    spread = ((1.0 - mix_col) * back_mixed).reshape(images_dev, -1)
    images_grad = mix_col * back_mixed + jnp.dot(
        selector.astype(jnp.float32).T,
        spread,
        precision=PRECISE,
        preferred_element_type=jnp.float32,
    ).reshape(images.shape)
    shards = (
        lax.psum_scatter(gradients[0], "dp", scatter_dimension=0, tiled=True),
        lax.psum_scatter(gradients[1], "dp", scatter_dimension=0, tiled=True),
        lax.psum_scatter(gradients[2], "dp", scatter_dimension=0, tiled=True),
        lax.psum_scatter(gradients[3], "dp", scatter_dimension=0, tiled=True),
    )
    squares = sum((jnp.sum(shard_piece * shard_piece) for shard_piece in shards))
    squares_sum = lax.psum(squares, "dp")
    grad_norm = jnp.sqrt(squares_sum)
    factor = CLIP_NORM / jnp.maximum(grad_norm, CLIP_NORM)
    grad_in, grad_out, grad_down, grad_small = shards
    shard_len = grad_small.shape[0]
    position = lax.axis_index("dp") * shard_len + jnp.arange(shard_len, dtype=jnp.int32)
    small_rate = jnp.where(position < 54 * D + FF, LAYER_DECAY * RATE_VECTOR, RATE_VECTOR)
    small_decay = jnp.where(position < 49 * D, WEIGHT_DECAY, 0.0)
    new_in = adamw_step(
        weight_in, first_in, second_in, grad_in * factor, LAYER_DECAY * RATE_MATRIX, WEIGHT_DECAY
    )
    new_out = adamw_step(
        weight_out,
        first_out,
        second_out,
        grad_out * factor,
        LAYER_DECAY * RATE_MATRIX,
        WEIGHT_DECAY,
    )
    new_down = adamw_step(
        weight_down, first_down, second_down, grad_down * factor, RATE_MATRIX, WEIGHT_DECAY
    )
    new_small = adamw_step(
        small_params, first_small, second_small, grad_small * factor, small_rate, small_decay
    )
    return (
        result.astype(jnp.bfloat16),
        images_grad,
        grad_norm,
        new_in[0],
        new_in[1],
        new_in[2],
        new_out[0],
        new_out[1],
        new_out[2],
        new_down[0],
        new_down[1],
        new_down[2],
        new_small[0],
        new_small[1],
        new_small[2],
    )


def solution(mesh):
    return jax.shard_map(
        local,
        mesh=mesh,
        in_specs=(
            P("dp", None, None, None),
            P("dp"),
            P("dp"),
            P("dp"),
            P("dp", None, None, None),
            P("dp", None),
            P("dp", None),
            P("dp", None),
            P("dp"),
            P("dp", None),
            P("dp", None),
            P("dp", None),
            P("dp", None),
            P("dp", None),
            P("dp", None),
            P("dp"),
            P("dp"),
        ),
        out_specs=(
            P("dp", None, None, None),
            P("dp", None, None, None),
            P(),
            P("dp", None),
            P("dp", None),
            P("dp", None),
            P("dp", None),
            P("dp", None),
            P("dp", None),
            P("dp", None),
            P("dp", None),
            P("dp", None),
            P("dp"),
            P("dp"),
            P("dp"),
        ),
        check_vma=False,
    )
```

profile of v0, /device:TPU:0, one launch (start us, length us, event | category | flops | bytes accessed | tf_op | source)
XLA Modules:
  0.0 832.9 jit_solution(2070850569453749640)
XLA Ops:
  10.4 1.6 convert_element_type.73
  12.9 42.4 %all-reduce.2 = bf16[23808]{0:T(1024)(128)(2,1)S(1)} all-reduce(bf16[23808]{0:T(1024)(128)(2,1)S(1)} %dynamic-update-slice), channel_id=1, replica_groups=mesh['dp'=32] {'dp'}, use_global_device_ids=true, to_apply=%add.2 | all-reduce | flops 23808 | bytes 95232
  59.4 2.1 convert_reduce_fusion.2
  61.5 2.3 copy.69
  63.8 2.8 reshape.321
  66.6 3.5 dot_general.46
  70.1 2.9 multiply_add_fusion.3
  73.4 55.1 %fusion.133 = (f32[16,14,14]{0,2,1:T(8,128)S(1)}, f32[16,14,14,384]{3,0,2,1:T(8,128)S(1)}) fusion(f32[384]{0:T(512)S(1)} %get-tuple-element.212, f32[384]{0:T(512)S(1)} %get-tuple-element.211, f32[384]{0:T(512)S(1)} %get-tuple-element.210, f32[384]{0:T(512)S(1)} %get-tuple-element.209, f32[384]{0:T(512)S(1)} %get-tuple-element.208, ...), kind=kLoop, calls=%fused_computation.343 | loop fusion | flops 119215040 | bytes 9723136 | tf_op jit(solution)/shard_map/reduce_sum | solution.py:38
  132.5 2.4 reshape.322
  136.2 47.9 %multiply_convert_fusion = (bf16[3136,1536]{1,0:T(8,128)(2,1)}, f32[3136,1536]{1,0:T(8,128)}, f32[3136,1536]{1,0:T(8,128)}) fusion(f32[1536]{0:T(1024)S(1)} %slice.979, bf16[3136,384]{1,0:T(8,128)(2,1)} %reshape.322, bf16[1536,384]{1,0:T(8,128)(2,1)} %all-gather.4.cloned.1.call-done), kind=kOutput, calls=%fused_computation.100 | convolution fusion | flops 4017291264 | bytes 51763200 | tf_op jit(solution)/shard_map/dot_general | solution.py:86
  184.2 9.5 %convolution_add_fusion = f32[3136,384]{1,0:T(8,128)} fusion(bf16[3136,1536]{1,0:T(8,128)(2,1)} %get-tuple-element.152, bf16[1536,384]{1,0:T(8,128)(2,1)} %all-gather.6.cloned.1.call-done, f32[384]{0:T(512)S(1)} %copy-done.109), kind=kOutput, calls=%fused_computation.114 | convolution fusion | flops 3700580352 | bytes 15631872 | tf_op jit(solution)/shard_map/dot_general | solution.py:90
  193.7 6.2 reshape.323
  199.9 7.0 fusion.131
  206.9 2.1 copy-done.2
  210.6 5.9 dot_general.51
  216.6 6.0 multiply_reduce_fusion.55
  222.8 2.9 copy.76
  226.5 2.1 multiply_reduce_fusion
  228.8 5.9 multiply_reduce_fusion.1
  234.7 2.2 copy-done.3
  238.3 2.3 reshape.327
  240.6 20.9 %convert_reduce_fusion = (f32[1536]{0:T(1024)S(1)}, bf16[3136,1536]{1,0:T(8,128)(2,1)S(1)}) fusion(f32[3136,1536]{1,0:T(8,128)} %get-tuple-element.153, bf16[3136,384]{1,0:T(8,128)(2,1)} %reshape.327, bf16[1536,384]{1,0:T(8,128)(2,1)} %all-gather.6.cloned.1.call-done, f32[3136,1536]{1,0:T(8,128)} %get-tuple-element.213, f32[1536]{0:T(1024)S(1)} %slice.979), kind=kOutput, calls=%fused_computation.98 | convolution fusion | flops 3781261824 | bytes 51769344 | tf_op jit(solution)/shard_map/dot_general | solution.py:167
  261.5 7.3 fusion.125
  269.2 6.3 reshape.328
  275.5 6.0 multiply_reduce_fusion.2
  281.5 21.3 %multiply_reduce_fusion.3 = (f32[384]{0:T(512)S(1)}, f32[384]{0:T(512)S(1)}, f32[384]{0:T(512)S(1)}, f32[384]{0:T(512)S(1)}, f32[384]{0:T(512)S(1)}, /*index=5*/...) fusion(f32[16,14,14,384]{3,0,2,1:T(8,128)S(1)} %bitcast.48, ...), kind=kLoop, calls=%fused_computation.218 | loop fusion | flops 51774720 | bytes 19346944 | tf_op jit(solution)/shard_map/reduce_sum | solution.py:189
  302.9 13.9 %multiply_reduce_fusion.39 = (f32[384]{0:T(512)S(1)}, f32[384]{0:T(512)S(1)}, f32[384]{0:T(512)S(1)}, f32[384]{0:T(512)S(1)}, f32[384]{0:T(512)S(1)}, /*index=5*...) fusion(f32[16,14,14,384]{3,0,2,1:T(8,128)} %get-tuple-element.1, ...), kind=kLoop, calls=%fused_computation.254 | loop fusion | flops 32508672 | bytes 9655296 | tf_op jit(solution)/shard_map/reduce_sum | solution.py:189
  316.7 12.4 %multiply_reduce_fusion.21 = (f32[384]{0:T(512)S(1)}, f32[384]{0:T(512)S(1)}, f32[384]{0:T(512)S(1)}, f32[384]{0:T(512)S(1)}, f32[384]{0:T(512)S(1)}, /*index=5*...) fusion(f32[16,14,14,384]{3,0,2,1:T(8,128)} %get-tuple-element.1, ...), kind=kLoop, calls=%fused_computation.236 | loop fusion | flops 43345152 | bytes 9661440 | tf_op jit(solution)/shard_map/reduce_sum | solution.py:189
  329.2 3.0 reduce_sum.713
  333.8 9.4 %fusion.137 = f32[1536,384]{1,0:T(8,128)} fusion(bf16[3136,1536]{1,0:T(8,128)(2,1)} %copy-done.4, bf16[3136,384]{1,0:T(8,128)(2,1)S(1)} %copy-done.5), kind=kOutput, calls=%fused_computation.347 | convolution fusion | flops 3699376128 | bytes 14401536 | tf_op jit(solution)/shard_map/dot_general | solution.py:173
  343.3 9.8 %fusion.138 = f32[1536,384]{1,0:T(8,128)} fusion(bf16[3136,1536]{1,0:T(8,128)(2,1)} %get-tuple-element.152, bf16[3136,384]{1,0:T(8,128)(2,1)} %reshape.327), kind=kOutput, calls=%fused_computation.348 | convolution fusion | flops 3699376128 | bytes 14401536 | tf_op jit(solution)/shard_map/dot_general | solution.py:164
  353.2 2.9 copy.83
  356.1 3.2 reshape.330
  359.2 74.1 %copy.74 = bf16[16,7,2,7,2,384]{3,1,0,4,2,5:T(8,128)(2,1)} copy(bf16[16,7,2,7,2,384]{5,0,4,3,2,1:T(8,128)(2,1)S(1)} %bitcast.58) | data formatting | bytes 4816896 | tf_op jit(solution)/shard_map/reshape | solution.py:96
  433.3 56.8 %reshape.325 = bf16[784,1536]{0,1:T(8,128)(2,1)S(1)} reshape(bf16[16,7,7,384,2,2]{2,1,0,5,4,3:T(8,128)(2,1)} %bitcast.46) | data formatting | bytes 4816896 | tf_op jit(solution)/shard_map/reshape | solution.py:98
  490.5 5.5 fusion.139
  497.1 86.9 %broadcast_multiply_fusion = (f32[16,14,14,384]{3,0,2,1:T(8,128)S(1)}, f32[16,14,14,384]{3,0,2,1:T(8,128)}) fusion(f32[16]{0:T(128)} %broadcast_subtract_fusion.1, f32[384]{0:T(512)S(1)} %copy-done.62, f32[384]{0:T(512)S(1)} %copy-done.60, f32[384]{0:T(512)S(1)} %copy-done.58, f32[384]{0:T(512)S(1)} %copy-done.56, f32[384]{0:T(512)S(1)} %copy-done.54, ...), kind=kLoop, calls=%fused_computation.288 | loop fusion | flops 119218176 | bytes 19342912 | tf_op jit(solution)/shard_map/mul | solution.py:280
  584.0 3.9 copy.81
  587.9 4.7 reshape.329
  592.6 5.0 dot_general.56
  597.7 4.8 add_convert_fusion.3
  602.5 2.2 convert_element_type.75
  604.9 11.5 %multiply_add_fusion = f32[16,14,14,384]{3,0,2,1:T(8,128)} fusion(f32[16,14,14,384]{3,0,2,1:T(8,128)} %get-tuple-element.149, f32[16]{0:T(128)S(1)} %copy-done.106, f32[14,14,384,16]{2,1,0,3:T(8,128)} %dot_general.56, s32[16]{0:T(128)S(1)} %copy-done.108), kind=kOutput, calls=%fused_computation.267 | convolution fusion | flops 233619712 | bytes 14450816 | tf_op jit(solution)/shard_map/dot_general | solution.py:281
  619.3 44.1 %reduce-scatter.6.cloned.1.call-done = f32[48,384]{1,0:T(8,128)} async-done(((f32[1536,384]{1,0:T(8,128)}), f32[48,384]{1,0:T(8,128)}) %reduce-scatter.6.cloned.1.call-update) | async-done | bytes 73744 | tf_op jit(solution)/shard_map/reduce_scatter | solution.py:289
  666.3 108.6 %reduce-scatter.8.cloned.1.call-done = f32[48,768]{1,0:T(8,128)} async-done(((f32[1536,768]{1,0:T(8,128)}), f32[48,768]{1,0:T(8,128)}) %reduce-scatter.8.cloned.1.call-update) | async-done | bytes 147472 | tf_op jit(solution)/shard_map/reduce_scatter | solution.py:290
  779.0 40.0 %psum.7 = f32[]{:T(128)} all-reduce(f32[]{:T(128)S(6)} %add.634), channel_id=1, replica_groups=mesh['dp'=32] {'dp'}, use_global_device_ids=true, to_apply=%region_74.75 | all-reduce | flops 1 | bytes 8 | tf_op jit(solution)/shard_map/psum | solution.py:294
  819.8 1.7 multiply_subtract_fusion
  823.0 1.8 multiply_subtract_fusion.1
  (356 shorter events, 28.3 us)
Async XLA Ops:
  7.2 129.1 %all-gather.4.cloned.1.call-start = ((), (), s32[]{:S(2)}) async-start(), calls=%async_computation.3 | async-start | bytes 1216512 | tf_op jit(solution)/shard_map/all_gather | solution.py:254
  8.8 175.4 %all-gather.6.cloned.1.call-start = ((), (), s32[]{:S(2)}) async-start(), calls=%async_computation.4 | async-start | bytes 1216512 | tf_op jit(solution)/shard_map/all_gather | solution.py:255
  10.3 200.3 %all-gather.8.cloned.1.call-start = ((), (), s32[]{:S(2)}) async-start(), calls=%async_computation.5 | async-start | bytes 2433024 | tf_op jit(solution)/shard_map/all_gather | solution.py:256
  12.0 604.5 %all-reduce.6.cloned.1.call-start = ((), (), s32[]{:S(2)}) async-start(), calls=%async_computation.9 | async-start | bytes 196608
  55.4 17.7 %copy-start.27 = (f32[384]{0:T(512)}, f32[384]{0:T(512)S(1)}, u32[]{:S(2)}) copy-start(f32[384]{0:T(512)S(1)} %get-tuple-element.195) | copy-start | bytes 4612
  55.4 17.7 %copy-start.29 = (f32[384]{0:T(512)}, f32[384]{0:T(512)S(1)}, u32[]{:S(2)}) copy-start(f32[384]{0:T(512)S(1)} %get-tuple-element.196) | copy-start | bytes 4612
  55.4 17.7 %copy-start.31 = (f32[384]{0:T(512)}, f32[384]{0:T(512)S(1)}, u32[]{:S(2)}) copy-start(f32[384]{0:T(512)S(1)} %get-tuple-element.197) | copy-start | bytes 4612
  55.4 17.7 %copy-start.33 = (f32[384]{0:T(512)}, f32[384]{0:T(512)S(1)}, u32[]{:S(2)}) copy-start(f32[384]{0:T(512)S(1)} %get-tuple-element.198) | copy-start | bytes 4612
  55.5 17.7 %copy-start.35 = (f32[384]{0:T(512)}, f32[384]{0:T(512)S(1)}, u32[]{:S(2)}) copy-start(f32[384]{0:T(512)S(1)} %get-tuple-element.199) | copy-start | bytes 4612
  55.5 17.7 %copy-start.37 = (f32[384]{0:T(512)}, f32[384]{0:T(512)S(1)}, u32[]{:S(2)}) copy-start(f32[384]{0:T(512)S(1)} %get-tuple-element.200) | copy-start | bytes 4612
  55.5 17.7 %copy-start.39 = (f32[384]{0:T(512)}, f32[384]{0:T(512)S(1)}, u32[]{:S(2)}) copy-start(f32[384]{0:T(512)S(1)} %get-tuple-element.201) | copy-start | bytes 4612
  55.5 17.7 %copy-start.41 = (f32[384]{0:T(512)}, f32[384]{0:T(512)S(1)}, u32[]{:S(2)}) copy-start(f32[384]{0:T(512)S(1)} %get-tuple-element.202) | copy-start | bytes 4612
  55.5 17.7 %copy-start.43 = (f32[384]{0:T(512)}, f32[384]{0:T(512)S(1)}, u32[]{:S(2)}) copy-start(f32[384]{0:T(512)S(1)} %get-tuple-element.203) | copy-start | bytes 4612
  55.5 17.7 %copy-start.45 = (f32[384]{0:T(512)}, f32[384]{0:T(512)S(1)}, u32[]{:S(2)}) copy-start(f32[384]{0:T(512)S(1)} %get-tuple-element.204) | copy-start | bytes 4612
  55.5 17.7 %copy-start.47 = (f32[384]{0:T(512)}, f32[384]{0:T(512)S(1)}, u32[]{:S(2)}) copy-start(f32[384]{0:T(512)S(1)} %get-tuple-element.205) | copy-start | bytes 4612
  55.5 17.7 %copy-start.49 = (f32[384]{0:T(512)}, f32[384]{0:T(512)S(1)}, u32[]{:S(2)}) copy-start(f32[384]{0:T(512)S(1)} %get-tuple-element.206) | copy-start | bytes 4612
  55.5 17.7 %copy-start.51 = (f32[384]{0:T(512)}, f32[384]{0:T(512)S(1)}, u32[]{:S(2)}) copy-start(f32[384]{0:T(512)S(1)} %get-tuple-element.207) | copy-start | bytes 4612
  55.5 17.7 %copy-start.53 = (f32[384]{0:T(512)}, f32[384]{0:T(512)S(1)}, u32[]{:S(2)}) copy-start(f32[384]{0:T(512)S(1)} %get-tuple-element.208) | copy-start | bytes 4612
  55.6 17.7 %copy-start.55 = (f32[384]{0:T(512)}, f32[384]{0:T(512)S(1)}, u32[]{:S(2)}) copy-start(f32[384]{0:T(512)S(1)} %get-tuple-element.209) | copy-start | bytes 4612
  55.6 17.7 %copy-start.57 = (f32[384]{0:T(512)}, f32[384]{0:T(512)S(1)}, u32[]{:S(2)}) copy-start(f32[384]{0:T(512)S(1)} %get-tuple-element.210) | copy-start | bytes 4612
  55.6 17.7 %copy-start.59 = (f32[384]{0:T(512)}, f32[384]{0:T(512)S(1)}, u32[]{:S(2)}) copy-start(f32[384]{0:T(512)S(1)} %get-tuple-element.211) | copy-start | bytes 4612
  55.6 17.7 %copy-start.61 = (f32[384]{0:T(512)}, f32[384]{0:T(512)S(1)}, u32[]{:S(2)}) copy-start(f32[384]{0:T(512)S(1)} %get-tuple-element.212) | copy-start | bytes 4612
  56.2 17.1 %copy-start.71 = (f32[384]{0:T(512)}, f32[384]{0:T(512)S(1)}, u32[]{:S(2)}) copy-start(f32[384]{0:T(512)S(1)} %get-tuple-element.180) | copy-start | bytes 4612
  56.2 17.1 %copy-start.73 = (f32[384]{0:T(512)}, f32[384]{0:T(512)S(1)}, u32[]{:S(2)}) copy-start(f32[384]{0:T(512)S(1)} %get-tuple-element.181) | copy-start | bytes 4612
  56.2 17.1 %copy-start.75 = (f32[384]{0:T(512)}, f32[384]{0:T(512)S(1)}, u32[]{:S(2)}) copy-start(f32[384]{0:T(512)S(1)} %get-tuple-element.182) | copy-start | bytes 4612
  56.2 17.1 %copy-start.77 = (f32[384]{0:T(512)}, f32[384]{0:T(512)S(1)}, u32[]{:S(2)}) copy-start(f32[384]{0:T(512)S(1)} %get-tuple-element.183) | copy-start | bytes 4612
  56.2 17.1 %copy-start.79 = (f32[384]{0:T(512)}, f32[384]{0:T(512)S(1)}, u32[]{:S(2)}) copy-start(f32[384]{0:T(512)S(1)} %get-tuple-element.184) | copy-start | bytes 4612
  56.3 17.1 %copy-start.81 = (f32[384]{0:T(512)}, f32[384]{0:T(512)S(1)}, u32[]{:S(2)}) copy-start(f32[384]{0:T(512)S(1)} %get-tuple-element.185) | copy-start | bytes 4612
  57.0 72.8 %copy-start.25 = (f32[384]{0:T(512)}, f32[384]{0:T(512)S(1)}, u32[]{:S(2)}) copy-start(f32[384]{0:T(512)S(1)} %get-tuple-element.161) | copy-start | bytes 4612
  73.1 55.5 %copy-start = (f32[16,14,14,384]{3,0,2,1:T(8,128)}, f32[16,14,14,384]{3,0,2,1:T(8,128)S(1)}, u32[]{:S(2)}) copy-start(f32[16,14,14,384]{3,0,2,1:T(8,128)S(1)} %multiply_add_fusion.3) | copy-start | bytes 14450692
  136.2 48.0 %copy-start.109 = (f32[384]{0:T(512)S(1)}, f32[384]{0:T(512)}, u32[]{:S(2)}) copy-start(f32[384]{0:T(512)} %get-tuple-element.160) | copy-start | bytes 4612
  240.5 20.9 %copy-start.26 = (f32[384]{0:T(512)S(1)}, f32[384]{0:T(512)}, u32[]{:S(2)}) copy-start(f32[384]{0:T(512)} %copy-done.25) | copy-start | bytes 4612
  240.5 20.9 %copy-start.110 = (bf16[1536,384]{1,0:T(8,128)(2,1)S(1)}, bf16[1536,384]{1,0:T(8,128)(2,1)}, u32[]{:S(2)}) copy-start(bf16[1536,384]{1,0:T(8,128)(2,1)} %all-gather.4.cloned.1.call-done) | copy-start | bytes 3538948
  333.7 284.1 %reduce-scatter.4.cloned.1.call-start = ((), (), s32[]{:S(2)}) async-start(), calls=%async_computation.6 | async-start | bytes 2433024 | tf_op jit(solution)/shard_map/reduce_scatter | solution.py:288
  343.2 320.2 %reduce-scatter.6.cloned.1.call-start = ((), (), s32[]{:S(2)}) async-start(), calls=%async_computation.7 | async-start | bytes 2433024 | tf_op jit(solution)/shard_map/reduce_scatter | solution.py:289
  353.1 421.8 %reduce-scatter.8.cloned.1.call-start = ((), (), s32[]{:S(2)}) async-start(), calls=%async_computation.8 | async-start | bytes 4866048 | tf_op jit(solution)/shard_map/reduce_scatter | solution.py:290
  604.8 215.0 %copy-start.13 = (f32[48,768]{1,0:T(8,128)S(1)}, f32[48,768]{1,0:T(8,128)}, u32[]{:S(2)}) copy-start(f32[48,768]{1,0:T(8,128)} %param.24) | copy-start | bytes 442372
  604.8 215.0 %copy-start.17 = (f32[48,768]{1,0:T(8,128)S(1)}, f32[48,768]{1,0:T(8,128)}, u32[]{:S(2)}) copy-start(f32[48,768]{1,0:T(8,128)} %param.31) | copy-start | bytes 442372
  604.8 215.0 %copy-start.18 = (f32[48,768]{1,0:T(8,128)S(1)}, f32[48,768]{1,0:T(8,128)}, u32[]{:S(2)}) copy-start(f32[48,768]{1,0:T(8,128)} %param.30) | copy-start | bytes 442372
  604.8 216.7 %copy-start.101 = (f32[744]{0:T(1024)S(1)}, f32[744]{0:T(1024)}, u32[]{:S(2)}) copy-start(f32[744]{0:T(1024)} %param.25) | copy-start | bytes 8932
  604.8 216.7 %copy-start.103 = (f32[744]{0:T(1024)S(1)}, f32[744]{0:T(1024)}, u32[]{:S(2)}) copy-start(f32[744]{0:T(1024)} %param.33) | copy-start | bytes 8932
  604.8 216.7 %copy-start.104 = (f32[744]{0:T(1024)S(1)}, f32[744]{0:T(1024)}, u32[]{:S(2)}) copy-start(f32[744]{0:T(1024)} %param.32) | copy-start | bytes 8932
  604.8 218.1 %copy-start.14 = (f32[48,384]{1,0:T(8,128)S(1)}, f32[48,384]{1,0:T(8,128)}, u32[]{:S(2)}) copy-start(f32[48,384]{1,0:T(8,128)} %param.22) | copy-start | bytes 221188
  604.9 218.1 %copy-start.15 = (f32[48,384]{1,0:T(8,128)S(1)}, f32[48,384]{1,0:T(8,128)}, u32[]{:S(2)}) copy-start(f32[48,384]{1,0:T(8,128)} %param.23) | copy-start | bytes 221188
  604.9 218.1 %copy-start.21 = (f32[48,384]{1,0:T(8,128)S(1)}, f32[48,384]{1,0:T(8,128)}, u32[]{:S(2)}) copy-start(f32[48,384]{1,0:T(8,128)} %param.29) | copy-start | bytes 221188
  604.9 218.1 %copy-start.22 = (f32[48,384]{1,0:T(8,128)S(1)}, f32[48,384]{1,0:T(8,128)}, u32[]{:S(2)}) copy-start(f32[48,384]{1,0:T(8,128)} %param.28) | copy-start | bytes 221188
  604.9 218.1 %copy-start.23 = (f32[48,384]{1,0:T(8,128)S(1)}, f32[48,384]{1,0:T(8,128)}, u32[]{:S(2)}) copy-start(f32[48,384]{1,0:T(8,128)} %param.27) | copy-start | bytes 221188
  604.9 218.0 %copy-start.24 = (f32[48,384]{1,0:T(8,128)S(1)}, f32[48,384]{1,0:T(8,128)}, u32[]{:S(2)}) copy-start(f32[48,384]{1,0:T(8,128)} %param.26) | copy-start | bytes 221188
  (77 other events, 582.6 us)
Sparse Core Ops, SparseCore 0:
  11.5 56.7 all-gather.3
  71.8 52.9 all-gather.5
  128.3 56.1 all-gather.7
  333.9 120.4 all-reduce.5
  459.5 99.8 reduce-scatter.3
  565.3 98.0 reduce-scatter.5
  668.9 105.9 reduce-scatter.7
where the time goes:
time: 845 us; the launch traced here: 833 us
  other arithmetic  240 us (28%)
  local copies, waits for them, and re-layouts  200 us (24%)
  waiting for transfers between devices  153 us (18%)
  matrix products  136 us (16%)
  blocking collectives  82.4 us (10%)
  between operations  21.1 us (2%)
    reduce_scatter x1, waiting for transfers between devices, local(): lax.psum_scatter(gradients[2], 'dp', scatter_dimension=0, tiled=True)  109 us
    mul x1, other arithmetic, local(): spread = ((1.0 - mix_col) * back_mixed).reshape(images_dev, -1)  86.9 us
    reshape x1, local copies, waits for them, and re-layouts, forward(): normed_two.reshape(images_dev, half_len, 2, half_len, 2, D)  74.1 us
    reduce_sum x2, other arithmetic, norm_parts(): average = jnp.mean(values, axis=-1, keepdims=True)  62.1 us
    reshape x1, local copies, waits for them, and re-layouts, forward(): patches = normed_two.reshape(images_dev, half_len, 2, half_len, 2, D).tra...  56.8 us
    dot_general x1, matrix products, forward(): lax.dot_general(normed_one, weight_in, COL_CONTRACT, preferred_element_ty...  47.9 us
    reduce_sum x3, other arithmetic, backward(): kernel_rows.append(jnp.sum(window * back_conv, axis=(0, 1, 2)))  47.6 us
    reduce_scatter x1, waiting for transfers between devices, local(): lax.psum_scatter(gradients[1], 'dp', scatter_dimension=0, tiled=True)  44.1 us
  transfers between devices with their start and end apart: 7, of which 2 were waited for; matrix products, arithmetic and copies ran while one was open for 53% of the time, Pallas kernels for 0%

commit v1 on v0

v1 whole, which is shorter than its diff:
```python
import functools
import jax
import jax.numpy as jnp
from jax import lax
from jax.experimental import pallas as pl
from jax.experimental.pallas import tpu as pltpu
from jax.sharding import PartitionSpec as P

STEP = 10
DROP_RATE = 0.2
RATE_MATRIX = 0.05
RATE_VECTOR = 0.3
LAYER_DECAY = 0.8
BETA_ONE = 0.9
BETA_TWO = 0.999
ADAM_EPS = 1e-08
WEIGHT_DECAY = 0.05
CLIP_NORM = 1.0
D = 384
FF = 1536
LN_EPS = 1e-06
F32 = jnp.float32
BF16 = jnp.bfloat16
VMEM = pl.BlockSpec(memory_space=pltpu.VMEM)
ROWS = (((0,), (0,)), ((), ()))
COLS = (((1,), (1,)), ((), ()))


def limit(mib):
    return pltpu.CompilerParams(vmem_limit_bytes=mib << 20)


def shaped(shape, dtype):
    return jax.ShapeDtypeStruct(shape, dtype)


def conv_rows(src, taps, h, t, lanes, side, base, flip):
    def one(ky, acc):
        acc = list(acc)
        x = [src[h + ky - 3, w, t, lanes] for w in range(side)]
        for kx in range(7):
            tap = taps[48 - (ky * 7 + kx) if flip else ky * 7 + kx, :, lanes]
            for w in range(side):
                if 0 <= w + kx - 3 < side:
                    acc[w] = acc[w] + x[w + kx - 3] * tap
        return tuple(acc)

    first = jnp.maximum(3 - h, 0)
    last = jnp.minimum(7, side + 3 - h)
    return lax.fori_loop(first, last, one, tuple(base))


def conv_kernel(sel_ref, mix_ref, img_ref, dk_ref, vec_ref, mixed_ref, unit_ref, inv_ref, norm_ref, taps):
    side, _, imgs, _ = img_ref.shape
    for t in range(49):
        taps[t] = jnp.broadcast_to(dk_ref[t : t + 1, :], (8, D))
    mix = mix_ref[...][None]
    rest = 1.0 - mix

    def mixing(h, _):
        x = img_ref[h].reshape(side * imgs, D)
        other = jnp.dot(sel_ref[...], x, preferred_element_type=F32).reshape(side, imgs, D)
        mixed_ref[h] = mix * x.reshape(side, imgs, D).astype(F32) + rest * other
        return 0

    lax.fori_loop(0, side, mixing, 0)

    def conv(h, _):
        for t in range(imgs // 8):
            at = pl.ds(t * 8, 8)
            for g in range(D // 128):
                lanes = pl.ds(g * 128, 128)
                base = jnp.broadcast_to(vec_ref[0:1, lanes], (8, 128))
                acc = conv_rows(mixed_ref, taps, h, at, lanes, side, [base] * side, False)
                for w in range(side):
                    unit_ref[h, w, at, lanes] = acc[w]
        return 0

    lax.fori_loop(0, side, conv, 0)
    gain = vec_ref[1:2, :][None]
    bias = vec_ref[2:3, :][None]

    def norm(h, _):
        v = unit_ref[h]
        c = v - jnp.mean(v, axis=-1, keepdims=True)
        inv = lax.rsqrt(jnp.mean(c * c, axis=-1, keepdims=True) + LN_EPS)
        unit = c * inv
        unit_ref[h] = unit
        inv_ref[h] = inv
        norm_ref[h] = (unit * gain + bias).astype(BF16)
        return 0

    lax.fori_loop(0, side, norm, 0)


def conv_forward(sel, mix, img, dk, vec):
    side, _, imgs, _ = img.shape
    full = (side, side, imgs, D)
    return pl.pallas_call(
        conv_kernel,
        out_shape=(shaped(full, F32), shaped(full, F32), shaped(full[:3] + (1,), F32), shaped(full, BF16)),
        in_specs=[VMEM] * 5,
        out_specs=(VMEM,) * 4,
        scratch_shapes=[pltpu.VMEM((49, 8, D), F32)],
        compiler_params=limit(24),
    )(sel, mix, img, dk, vec)


def hidden_kernel(block, chunk, norm_ref, win_ref, wout_ref, hb_ref, vec_ref, kl_ref, mixed_ref, act_ref, dg_ref, branch_ref, unit_ref, inv_ref, out_ref):
    rows = norm_ref.shape[0]
    imgs = kl_ref.shape[0]
    gain = vec_ref[5:6, :][None]
    bias = vec_ref[6:7, :][None]

    def body(i, _):
        at = pl.ds(pl.multiple_of(i * block, block), block)
        x = norm_ref[at, :]
        branch = jnp.broadcast_to(vec_ref[3:4, :], (block, D))
        for j in range(FF // chunk):
            cols = pl.ds(j * chunk, chunk)
            pre = lax.dot_general(x, win_ref[cols, :], COLS, preferred_element_type=F32) + hb_ref[:, cols]
            phi = 0.5 + 0.5 * lax.erf(pre * 0.7071067811865476)
            bell = jnp.exp2(pre * pre * -0.7213475204444817) * 0.3989422804014327
            act = (pre * phi).astype(BF16)
            act_ref[at, cols] = act
            dg_ref[at, cols] = (phi + pre * bell).astype(BF16)
            branch = branch + jnp.dot(act, wout_ref[cols, :], preferred_element_type=F32)
        branch_ref[at, :] = branch
        shape = (block // imgs, imgs, D)
        v = mixed_ref[at, :].reshape(shape) + kl_ref[...][None] * branch.reshape(shape)
        c = v - jnp.mean(v, axis=-1, keepdims=True)
        inv = lax.rsqrt(jnp.mean(c * c, axis=-1, keepdims=True) + LN_EPS)
        unit = c * inv
        unit_ref[at, :] = unit.reshape(block, D)
        inv_ref[at, :] = inv.reshape(block, 1)
        out_ref[at, :] = (unit * gain + bias).astype(BF16).reshape(block, D)
        return 0

    lax.fori_loop(0, rows // block, body, 0)


def hidden_forward(norm, win, wout, hb, vec, kl, mixed, block=224, chunk=512):
    rows = norm.shape[0]
    return pl.pallas_call(
        functools.partial(hidden_kernel, block, chunk),
        out_shape=(
            shaped((rows, FF), BF16),
            shaped((rows, FF), BF16),
            shaped((rows, D), F32),
            shaped((rows, D), F32),
            shaped((rows, 1), F32),
            shaped((rows, D), BF16),
        ),
        in_specs=[VMEM] * 7,
        out_specs=(VMEM,) * 6,
        compiler_params=limit(24),
    )(norm, win, wout, hb, vec, kl, mixed)


def down_kernel(norm_ref, dy_ref, wd_ref, unit_ref, inv_ref, branch_ref, vec_ref, keep_ref, db_ref, out_ref, gd_ref, res_ref, bb_ref, sums_ref, gdb_ref, acc):
    half, _, _, _, imgs, _ = norm_ref.shape
    rows = half * half * imgs
    dy = dy_ref[...].reshape(rows, 2 * D)
    acc[...] = jnp.broadcast_to(db_ref[...], acc.shape)
    sums_ref[...] = jnp.zeros(sums_ref.shape, F32)
    shape = (half * half, imgs, D)
    gain = vec_ref[5:6, :][None]
    keep = keep_ref[...][None]
    scale = keep * vec_ref[4:5, :][None]

    def part(k, _):
        a = k // 2
        b = k % 2
        x = norm_ref[:, a, :, b].reshape(rows, D)
        acc[...] += jnp.dot(x, wd_ref[k], preferred_element_type=F32)
        gd_ref[k] = lax.dot_general(x, dy, ROWS, preferred_element_type=F32)
        back = lax.dot_general(dy, wd_ref[k], COLS, preferred_element_type=F32).reshape(shape)
        unit = unit_ref[:, a, :, b].reshape(shape)
        sums_ref[0] += jnp.sum(back * unit, axis=0)
        sums_ref[1] += jnp.sum(back, axis=0)
        scaled = back * gain
        m1 = jnp.mean(scaled, axis=-1, keepdims=True)
        m2 = jnp.mean(scaled * unit, axis=-1, keepdims=True)
        inv = inv_ref[:, a, :, b].reshape(half * half, imgs, 1)
        res = inv * (scaled - m1 - unit * m2)
        res_ref[:, a, :, b] = res.reshape(half, half, imgs, D)
        sums_ref[2] += jnp.sum(res * keep * branch_ref[:, a, :, b].reshape(shape), axis=0)
        bb = (res * scale).astype(BF16)
        bb_ref[:, a, :, b] = bb.reshape(half, half, imgs, D)
        sums_ref[3] += jnp.sum(bb.astype(F32), axis=0)
        return 0

    lax.fori_loop(0, 4, part, 0)
    out_ref[...] = acc[...].astype(BF16).reshape(out_ref.shape)
    gdb_ref[...] = jnp.sum(dy.astype(F32).reshape(half * half, imgs, 2 * D), axis=0)


def down_both(norm, dy, wd, unit, inv, branch, vec, keep, db):
    half, _, _, _, imgs, _ = norm.shape
    return pl.pallas_call(
        down_kernel,
        out_shape=(
            shaped((half, half, imgs, 2 * D), BF16),
            shaped((4, D, 2 * D), F32),
            shaped(norm.shape, F32),
            shaped(norm.shape, BF16),
            shaped((4, imgs, D), F32),
            shaped((imgs, 2 * D), F32),
        ),
        in_specs=[VMEM] * 9,
        out_specs=(VMEM,) * 6,
        scratch_shapes=[pltpu.VMEM((half * half * imgs, 2 * D), F32)],
        compiler_params=limit(28),
    )(norm, dy, wd, unit, inv, branch, vec, keep, db)


def grad_out_kernel(act_ref, bb_ref, g_ref):
    def body(j, _):
        cols = pl.ds(pl.multiple_of(j * 256, 256), 256)
        g_ref[cols, :] = lax.dot_general(act_ref[:, cols], bb_ref[...], ROWS, preferred_element_type=F32)
        return 0

    lax.fori_loop(0, FF // 256, body, 0)


def grad_out_of(act, bb):
    return pl.pallas_call(
        grad_out_kernel,
        out_shape=shaped((FF, D), F32),
        in_specs=[VMEM] * 2,
        out_specs=VMEM,
        compiler_params=limit(24),
    )(act, bb)


def hidden_back_kernel(block, bb_ref, wout_ref, win_ref, dg_ref, norm_ref, unit_ref, inv_ref, vec_ref, gi_ref, conv_ref, hb_ref, sums_ref, pre):
    rows = bb_ref.shape[0]
    imgs = sums_ref.shape[1]
    shape = (block // imgs, imgs, D)
    gain = vec_ref[1:2, :][None]
    gi_ref[...] = jnp.zeros(gi_ref.shape, F32)
    hb_ref[...] = jnp.zeros(hb_ref.shape, F32)
    sums_ref[...] = jnp.zeros(sums_ref.shape, F32)
    chunk = 512

    def body(i, _):
        at = pl.ds(pl.multiple_of(i * block, block), block)
        b = bb_ref[at, :]
        x = norm_ref[at, :]
        back = jnp.zeros((block, D), F32)
        for j in range(FF // chunk):
            cols = pl.ds(j * chunk, chunk)
            act = lax.dot_general(b, wout_ref[cols, :], COLS, preferred_element_type=F32)
            p = (act * dg_ref[at, cols].astype(F32)).astype(BF16)
            hb_ref[:, cols] += jnp.sum(p.astype(F32).reshape(block // imgs, imgs, chunk), axis=0)
            back = back + jnp.dot(p, win_ref[cols, :], preferred_element_type=F32)
            gi_ref[cols, :] += lax.dot_general(p, x, ROWS, preferred_element_type=F32)
        back = back.reshape(shape)
        unit = unit_ref[at, :].reshape(shape)
        sums_ref[0] += jnp.sum(back * unit, axis=0)
        sums_ref[1] += jnp.sum(back, axis=0)
        scaled = back * gain
        m1 = jnp.mean(scaled, axis=-1, keepdims=True)
        m2 = jnp.mean(scaled * unit, axis=-1, keepdims=True)
        out = inv_ref[at, :].reshape(shape[:2] + (1,)) * (scaled - m1 - unit * m2)
        sums_ref[2] += jnp.sum(out, axis=0)
        conv_ref[at, :] = out.reshape(block, D)
        return 0

    lax.fori_loop(0, rows // block, body, 0)


def hidden_back(bb, wout, win, dg, norm, unit, inv, vec, imgs, block=784):
    rows = bb.shape[0]
    return pl.pallas_call(
        functools.partial(hidden_back_kernel, block),
        out_shape=(
            shaped((FF, D), F32),
            shaped((rows, D), F32),
            shaped((imgs, FF), F32),
            shaped((3, imgs, D), F32),
        ),
        in_specs=[VMEM] * 8,
        out_specs=(VMEM,) * 4,
        scratch_shapes=[pltpu.VMEM((8, 128), F32)],
        compiler_params=limit(32),
    )(bb, wout, win, dg, norm, unit, inv, vec)


def taps_kernel(mixed_ref, conv_ref, g_ref):
    side, _, imgs, _ = mixed_ref.shape

    def per_ky(ky, _):
        first = jnp.maximum(3 - ky, 0)
        last = jnp.minimum(side, side + 3 - ky)
        for g in range(D // 128):
            lanes = pl.ds(g * 128, 128)

            def row(h, acc):
                acc = list(acc)
                for t in range(imgs // 8):
                    at = pl.ds(t * 8, 8)
                    x = [mixed_ref[h + ky - 3, w, at, lanes] for w in range(side)]
                    for w in range(side):
                        d = conv_ref[h, w, at, lanes]
                        for kx in range(7):
                            if 0 <= w + kx - 3 < side:
                                acc[kx] = acc[kx] + x[w + kx - 3] * d
                return tuple(acc)

            acc = lax.fori_loop(first, last, row, (jnp.zeros((8, 128), F32),) * 7)
            for kx in range(7):
                g_ref[ky * 7 + kx, :, lanes] = jnp.sum(acc[kx], axis=0, keepdims=True)
        return 0

    lax.fori_loop(0, 7, per_ky, 0)


def taps_grad(mixed, conv):
    return pl.pallas_call(
        taps_kernel,
        out_shape=shaped((49, 1, D), F32),
        in_specs=[VMEM] * 2,
        out_specs=VMEM,
        compiler_params=limit(24),
    )(mixed, conv)


def images_kernel(conv_ref, res_ref, dk_ref, mix_ref, sel_ref, g_ref, taps):
    side, _, imgs, _ = conv_ref.shape
    for t in range(49):
        taps[t] = jnp.broadcast_to(dk_ref[t : t + 1, :], (8, D))
    mix = mix_ref[...][None]
    rest = 1.0 - mix

    def row(h, _):
        for t in range(imgs // 8):
            at = pl.ds(t * 8, 8)
            for g in range(D // 128):
                lanes = pl.ds(g * 128, 128)
                base = [res_ref[h, w, at, lanes] for w in range(side)]
                acc = conv_rows(conv_ref, taps, h, at, lanes, side, base, True)
                for w in range(side):
                    g_ref[h, w, at, lanes] = acc[w]
        return 0

    lax.fori_loop(0, side, row, 0)

    def unmix(h, _):
        v = g_ref[h]
        part = (rest * v).reshape(side * imgs, D)
        high = part.astype(BF16)
        low = (part - high.astype(F32)).astype(BF16)
        back = jnp.dot(sel_ref[...], high, preferred_element_type=F32) + jnp.dot(sel_ref[...], low, preferred_element_type=F32)
        g_ref[h] = mix * v + back.reshape(side, imgs, D)
        return 0

    lax.fori_loop(0, side, unmix, 0)


def images_back(conv, res, dk, mix, selt):
    return pl.pallas_call(
        images_kernel,
        out_shape=shaped(conv.shape, F32),
        in_specs=[VMEM] * 5,
        out_specs=VMEM,
        scratch_shapes=[pltpu.VMEM((49, 8, D), F32)],
        compiler_params=limit(24),
    )(conv, res, dk, mix, selt)


def swap(x, bit, n):
    return lax.ppermute(x, "dp", [(i, i ^ bit) for i in range(n)])


def bits_of(n):
    return [1 << k for k in range(n.bit_length() - 1)]


def is_set(bit):
    return (lax.axis_index("dp") & bit) != 0


def gather_tree(shard, n, order):
    have = shard
    met = []
    for bit in order:
        other = swap(have, bit, n)
        axis = sum(1 for b in met if b > bit)
        mine = is_set(bit)
        low = jnp.where(mine, other, have)
        high = jnp.where(mine, have, other)
        have = jnp.stack([low, high], axis=axis)
        met.append(bit)
    return have.reshape((n,) + shard.shape)


def scatter_tree(total, n, order):
    shape = total.shape[1:]
    left = sorted(order, reverse=True)
    have = total.reshape((2,) * len(left) + shape)
    for bit in order:
        axis = left.index(bit)
        mine = is_set(bit).astype(jnp.int32)
        keep = lax.dynamic_index_in_dim(have, mine, axis, keepdims=False)
        send = lax.dynamic_index_in_dim(have, 1 - mine, axis, keepdims=False)
        have = keep.astype(F32) + swap(send.astype(BF16), bit, n).astype(F32)
        left.remove(bit)
    return have


def adamw_step(weight, first_mom, second, gradient, step_rate, decay_rate):
    first_mom = BETA_ONE * first_mom + (1.0 - BETA_ONE) * gradient
    second = BETA_TWO * second + (1.0 - BETA_TWO) * gradient * gradient
    first_hat = first_mom / (1.0 - BETA_ONE**STEP)
    second_hat = second / (1.0 - BETA_TWO**STEP)
    weight = weight - step_rate * (first_hat / (jnp.sqrt(second_hat) + ADAM_EPS) + decay_rate * weight)
    return (first_mom, second, weight)


def local(n, images, mix_weight, partner, keep_mask, cotangent, weight_in, weight_out, weight_down, small_params,
          first_in, second_in, first_out, second_out, first_down, second_down, first_small, second_small):
    imgs, side = images.shape[:2]
    half = side // 2
    pixels = side * side * imgs
    bits = bits_of(n)
    up = bits[1:] + bits[:1]
    small = gather_tree(small_params.astype(BF16), n, up).reshape(-1, D).astype(F32)
    pair = jnp.concatenate([weight_in, weight_out], axis=1).astype(BF16)
    pair = gather_tree(pair, n, up).reshape(FF, 2 * D)
    win = pair[:, :D]
    wout = pair[:, D:]
    wd = lax.all_gather(weight_down.astype(BF16), "dp", axis=0, tiled=True).reshape(D, 4, 2 * D).transpose(1, 0, 2)

    dk = small[:49]
    vec = jnp.concatenate([small[49:52], small[56:60], small[56:57]], axis=0)
    hb = small[52:56].reshape(1, FF)
    db = small[60:62].reshape(1, 2 * D)
    place = partner - lax.axis_index("dp") * imgs
    spot = jnp.arange(side * imgs, dtype=jnp.int32)
    target = jnp.tile(place, side) + (spot // imgs) * imgs
    sel = target[:, None] == spot[None, :]
    selt = (target[None, :] == spot[:, None]).astype(BF16)
    sel = sel.astype(BF16)
    mix = jnp.broadcast_to(mix_weight[:, None], (imgs, D))
    keep = jnp.broadcast_to((keep_mask.astype(F32) / (1.0 - DROP_RATE))[:, None], (imgs, D))

    img = images.transpose(1, 2, 0, 3)
    dy = cotangent.transpose(1, 2, 0, 3)
    flat = lambda a: a.reshape(pixels, a.shape[-1])
    paired = lambda a: a.reshape(half, 2, half, 2, imgs, a.shape[-1])
    square = lambda a: a.reshape(side, side, imgs, a.shape[-1])
    mixed, unit1, inv1, norm1 = conv_forward(sel, mix, img, dk, vec)
    act, dg, branch, unit2, inv2, norm2 = hidden_forward(flat(norm1), win, wout, hb, vec, keep * vec[4:5], flat(mixed))
    out, gd, res, bb, sums2, gdb = down_both(
        paired(norm2), dy, wd, paired(unit2), paired(inv2), paired(branch), vec, keep, db
    )
    gd = gd.astype(BF16).transpose(1, 0, 2).reshape(n, FF // n, 2 * D)
    gd = scatter_tree(gd, n, [1, 4, 2] + bits[3:])
    go = grad_out_of(act, flat(bb)).reshape(n, FF // n, D)
    go = scatter_tree(go, n, [1, 2, 4] + bits[3:])
    gi, back_conv, ghb, sums1 = hidden_back(flat(bb), wout, win, dg, flat(norm1), flat(unit1), flat(inv1), vec, imgs)
    gi = scatter_tree(gi.reshape(n, FF // n, D), n, [1, 8, 2, 4] + bits[4:])
    back_conv = square(back_conv)
    gk = taps_grad(mixed, back_conv)
    one = jnp.sum(sums1, axis=1)
    two = jnp.sum(sums2, axis=1)
    gs = jnp.concatenate(
        [
            gk.reshape(49, D),
            one[2:3],
            one[0:2],
            jnp.sum(ghb, axis=0).reshape(4, D),
            two[3:4],
            two[2:3],
            two[0:2],
            jnp.sum(gdb, axis=0).reshape(2, D),
        ],
        axis=0,
    )
    gs = scatter_tree(gs.reshape(n, -1), n, up[-1:] + up[:-1])
    images_grad = images_back(back_conv, square(res), dk, mix, selt)

    squares = sum(jnp.sum(g * g) for g in (gi, go, gd, gs)).reshape(1, 1)
    for bit in bits:
        squares = squares + swap(squares, bit, n)
    grad_norm = jnp.sqrt(squares[0, 0])
    factor = CLIP_NORM / jnp.maximum(grad_norm, CLIP_NORM)
    shard_len = gs.shape[0]
    position = lax.axis_index("dp") * shard_len + jnp.arange(shard_len, dtype=jnp.int32)
    small_rate = jnp.where(position < 54 * D + FF, LAYER_DECAY * RATE_VECTOR, RATE_VECTOR)
    small_decay = jnp.where(position < 49 * D, WEIGHT_DECAY, 0.0)
    new_in = adamw_step(weight_in, first_in, second_in, gi * factor, LAYER_DECAY * RATE_MATRIX, WEIGHT_DECAY)
    new_out = adamw_step(weight_out, first_out, second_out, go * factor, LAYER_DECAY * RATE_MATRIX, WEIGHT_DECAY)
    new_down = adamw_step(weight_down, first_down, second_down, gd * factor, RATE_MATRIX, WEIGHT_DECAY)
    new_small = adamw_step(small_params, first_small, second_small, gs * factor, small_rate, small_decay)
    return (
        out.transpose(2, 0, 1, 3),
        images_grad.transpose(2, 0, 1, 3),
        grad_norm,
        *new_in,
        *new_out,
        *new_down,
        *new_small,
    )


def solution(mesh):
    four = P("dp", None, None, None)
    two = P("dp", None)
    one = P("dp")
    return jax.shard_map(
        functools.partial(local, mesh.shape["dp"]),
        mesh=mesh,
        in_specs=(four, one, one, one, four, two, two, two, one) + (two,) * 6 + (one,) * 2,
        out_specs=(four, four, P()) + (two,) * 9 + (one,) * 3,
        check_vma=False,
    )
```

time: 845 us -> 350 us (0.41); the launches traced: 833 us -> 349 us
  other arithmetic: 240 us -> 18.4 us
  local copies, waits for them, and re-layouts: 200 us -> 55.4 us
  matrix products: 136 us -> 0 us
  Pallas kernels: 0 us -> 131 us
  blocking collectives: 82.4 us -> 0 us
  waiting for transfers between devices: 153 us -> 82.9 us
  starting transfers between devices: 0.29 us -> 40.6 us
    reduce_scatter x3 -> x0, waiting for transfers between devices: 153 us -> none  [the longest x1 109 us: local(): lax.psum_scatter(gradients[2], 'dp', scatter_dimension=0, tiled=True)]
    reshape x10 -> x4, local copies, waits for them, and re-layouts: 159 us -> 7.3 us  [the longest x2 7.28 us: local(): lax.all_gather(weight_down.astype(BF16), 'dp', axis=0, tiled=True)]
    dot_general x11 -> x0, matrix products: 136 us -> none  [the longest x1 47.9 us: forward(): lax.dot_general(normed_one, weight_in, COL_CONTRACT, preferred_element_ty...]
    reduce_sum x17 -> x8, other arithmetic: 138 us -> 2.58 us  [the longest x4 2.48 us: local(): squares = sum((jnp.sum(g * g) for g in (gi, go, gd, gs))).reshape(1, 1)]
    pallas_call x0 -> x7, Pallas kernels: none -> 131 us  [the longest x1 30.2 us: hidden_forward(): pl.pallas_call(functools.partial(hidden_kernel, block, chunk), out_shape=...]
    mul x2 -> x1, other arithmetic: 88.2 us -> 0.07 us  [local(): keep * vec[4:5]]
    ppermute x0 -> x35, waiting for transfers between devices: none -> 82.9 us  [swap(): return lax.ppermute(x, 'dp', [(i, i ^ bit) for i in range(n)])]
    unnamed x1 -> x0, blocking collectives: 42.4 us -> none
  transfers between devices with their start and end apart: 7 -> 36, of which waited for: 2 -> 22; matrix products, arithmetic and copies ran while one was open for 53% -> 7% of each run, Pallas kernels for 0% -> 23%
where the time goes in v1:
time: 350 us; the launch traced here: 349 us
  Pallas kernels  131 us (37%)
  waiting for transfers between devices  82.9 us (24%)
  local copies, waits for them, and re-layouts  55.4 us (16%)
  starting transfers between devices  40.6 us (12%)
  between operations  21.7 us (6%)
  other arithmetic  18.4 us (5%)
    ppermute x35, waiting for transfers between devices, swap(): return lax.ppermute(x, 'dp', [(i, i ^ bit) for i in range(n)])  82.9 us
    ppermute x35, starting transfers between devices, swap(): return lax.ppermute(x, 'dp', [(i, i ^ bit) for i in range(n)])  40.5 us
    unnamed x101, local copies, waits for them, and re-layouts  37.6 us
    pallas_call x1, Pallas kernels, hidden_forward(): pl.pallas_call(functools.partial(hidden_kernel, block, chunk), out_shape=...  30.2 us
    pallas_call x1, Pallas kernels, images_back(): pl.pallas_call(images_kernel, out_shape=shaped(conv.shape, F32), in_specs...  22.3 us
    pallas_call x1, Pallas kernels, hidden_back(): pl.pallas_call(functools.partial(hidden_back_kernel, block), out_shape=(s...  21.9 us
    pallas_call x1, Pallas kernels, conv_forward(): pl.pallas_call(conv_kernel, out_shape=(shaped(full, F32), shaped(full, F3...  21.5 us
    pallas_call x1, Pallas kernels, down_both(): pl.pallas_call(down_kernel, out_shape=(shaped((half, half, imgs, 2 * D),...  14.8 us
  transfers between devices with their start and end apart: 36, of which 22 were waited for; matrix products, arithmetic and copies ran while one was open for 7% of the time, Pallas kernels for 23%

profile of v1, /device:TPU:0, one launch (start us, length us, event | category | flops | bytes accessed | tf_op | source)
XLA Modules:
  0.0 349.4 jit_solution(16766827429352919069)
XLA Ops:
  9.0 3.0 collective-permute-start.5
  20.7 1.6 collective-permute-start.2
  25.8 7.7 %collective-permute-done.7 = bf16[2,2,48,768]{3,2,1,0:T(8,128)(2,1)S(1)} collective-permute-done((bf16[2,2,48,768]{3,2,1,0:T(8,128)(2,1)S(1)}, bf16[2,2,48,768]{3,2,1,0:T(8,128)(2,1)S(1)}, u32[]{:S(2)}, u32[]{:S(2)}) %collective-permute-start.7) | collective-permute-done | bytes 294944 | tf_op jit(solution)/shard_map/ppermute | solution.py:373
  36.7 22.3 %collective-permute-done.3 = bf16[2,2,2,744]{3,2,1,0:T(2,128)(2,1)S(1)} collective-permute-done((bf16[2,2,2,744]{3,2,1,0:T(2,128)(2,1)S(1)}, bf16[2,2,2,744]{3,2,1,0:T(2,128)(2,1)S(1)}, u32[]{:S(2)}, u32[]{:S(2)}) %collective-permute-start.3) | collective-permute-done | bytes 11936 | tf_op jit(solution)/shard_map/ppermute | solution.py:373
  62.3 21.5 %shard_map.280 = (f32[14,14,16,384]{3,2,1,0:T(8,128)S(1)}, f32[14,14,16,384]{3,2,1,0:T(8,128)S(1)}, f32[14,14,16,1]{3,2,1,0:T(8,128)S(1)}, bf16[14,14,16,384]{3,2,1,0:T(8,128)(2,1)S(1)}) custom-call(bf16[224,224]{1,0:T(8,128)(2,1)S(1)} %get-tuple-element.96.sel_ref, f32[16,384]{1,0:T(8,128)S(1)} %broadcast_in_dim.30.mix_ref, ...), custom_call_target="tpu_custom_call" | custom-call | tf_op jit(solution)/shard_map/pallas_call | solution.py:99
  83.8 2.1 copy-done.14
  87.2 2.4 select_bitcast_fusion.1
  90.3 30.2 %shard_map.281 = (bf16[3136,1536]{1,0:T(8,128)(2,1)}, bf16[3136,1536]{1,0:T(8,128)(2,1)}, f32[3136,384]{1,0:T(8,128)S(1)}, f32[3136,384]{1,0:T(8,128)S(1)}, f32[...) custom-call(bf16[3136,384]{1,0:T(8,128)(2,1)S(1)} %bitcast.184, bf16[1536,384]{1,0:T(8,128)(2,1)S(1)} %get-tuple-element.68.win_ref, ...), custom_call_target="tpu_custom_call" | custom-call | tf_op jit(solution)/shard_map/pallas_call | solution.py:144
  120.5 2.1 copy-done.11
  122.7 2.2 copy-done.12
  127.5 5.2 %reshape.155 = bf16[384,4,768]{2,1,0:T(4,128)(2,1)} reshape(bf16[1536,768]{1,0:T(8,128)(2,1)} %all-gather.2.cloned.1.call-done) | data formatting | bytes 4718592 | tf_op jit(solution)/shard_map/reshape | solution.py:433
  132.6 2.1 copy.80
  135.5 2.4 copy-done.13
  139.1 14.8 %shard_map.282 = (bf16[7,7,16,768]{3,2,1,0:T(8,128)(2,1)}, f32[4,384,768]{2,1,0:T(8,128)S(1)}, f32[7,2,7,2,16,384]{5,4,3,2,1,0:T(8,128)S(1)}, bf16[7,2,7,2,16,38...) custom-call(bf16[7,2,7,2,16,384]{5,4,3,2,1,0:T(8,128)(2,1)S(1)} %bitcast.194, ...), custom_call_target="tpu_custom_call" | custom-call | tf_op jit(solution)/shard_map/pallas_call | solution.py:200
  153.9 2.2 copy-done.9
  156.1 2.1 copy-done.16
  158.2 3.2 copy-done.15
  161.5 21.9 %shard_map.283 = (f32[1536,384]{1,0:T(8,128)S(1)}, f32[3136,384]{1,0:T(8,128)S(1)}, f32[16,1536]{1,0:T(8,128)S(1)}, f32[3,16,384]{2,1,0:T(8,128)S(1)}) custom-call(bf16[3136,384]{1,0:T(8,128)(2,1)S(1)} %bitcast.182, bf16[1536,384]{1,0:T(8,128)(2,1)S(1)} %get-tuple-element.67.wout_ref, bf16[1536,384]{1,0:T(8,128)(2,1)S(1)} %get-tuple-element.68.win_ref, ...), custom_call_target="tpu_custom_call" | custom-call | tf_op jit(solution)/shard_map/pallas_call | solution.py:275
  183.4 2.2 copy-done
  187.2 2.4 copy-done.1
  189.5 2.4 copy-done.3
  191.9 13.3 %shard_map.286 = f32[49,1,384]{2,1,0:T(1,128)S(1)} custom-call(f32[14,14,16,384]{3,2,1,0:T(8,128)S(1)} %copy-done.3, f32[14,14,16,384]{3,2,1,0:T(8,128)S(1)} %bitcast.177), custom_call_target="tpu_custom_call" | custom-call | tf_op jit(solution)/shard_map/pallas_call | solution.py:320
  206.1 2.6 convert_bitcast_fusion
  208.7 3.2 copy.45
  211.9 5.2 %reshape_reshape.19 = bf16[2,2,2,2,2,48,768]{6,5,4,3,2,1,0:T(8,128)(2,1)} reshape(bf16[384,4,768]{2,1,0:T(4,128)(2,1)} %copy.45) | data formatting | bytes 4718592 | tf_op jit(solution)/shard_map/reshape;reshape | solution.py:401
  217.1 3.9 %copy-done.4 = bf16[3136,1536]{1,0:T(8,128)(2,1)S(1)} copy-done((bf16[3136,1536]{1,0:T(8,128)(2,1)S(1)}, bf16[3136,1536]{1,0:T(8,128)(2,1)}, u32[]{:S(2)}) %copy-start.4) | copy-done | bytes 9633816
  221.0 6.5 %shard_map.285 = f32[1536,384]{1,0:T(8,128)S(1)} custom-call(bf16[3136,1536]{1,0:T(8,128)(2,1)S(1)} %copy-done.4, bf16[3136,384]{1,0:T(8,128)(2,1)S(1)} %bitcast.183), custom_call_target="tpu_custom_call" | custom-call | tf_op jit(solution)/shard_map/pallas_call | solution.py:227
  229.8 2.3 collective-permute-done.26
  232.4 3.5 collective-permute-done.27
  236.6 3.0 collective-permute-done.28
  239.6 2.1 collective-permute-start.29
  241.9 2.4 copy-done.10
  244.3 22.3 %shard_map.284 = f32[14,14,16,384]{3,2,1,0:T(8,128)} custom-call(f32[14,14,16,384]{3,2,1,0:T(8,128)S(1)} %bitcast.180, f32[14,14,16,384]{3,2,1,0:T(8,128)S(1)} %bitcast.189, f32[49,384]{1,0:T(8,128)S(1)} %slice.57.dk_ref, f32[16,384]{1,0:T(8,128)S(1)} %broadcast_in_dim.30.mix_ref, bf16[224,224]{1,0:T(8,128)(2,1)S(1)} %get-tuple-element.95.sel_ref), custom_call_target="tpu_custom_call" | custom-call | tf_op jit(solution)/shard_map/pallas_call | solution.py:362
  268.9 2.1 collective-permute-start.11
  271.0 5.8 %collective-permute-done.16 = bf16[2,2,2,48,384]{4,3,0,1,2:T(8,128)(2,1)S(1)} collective-permute-done((bf16[2,2,2,48,384]{4,3,0,1,2:T(8,128)(2,1)S(1)}, bf16[2,2,2,48,384]{4,3,0,1,2:T(8,128)(2,1)S(1)}, u32[]{:S(2)}, u32[]{:S(2)}) %collective-permute-start.16) | collective-permute-done | bytes 294944 | tf_op jit(solution)/shard_map/ppermute | solution.py:373
  279.3 3.2 collective-permute-done.17
  283.5 2.1 collective-permute-start.18
  287.9 9.9 %collective-permute-done.21 = bf16[2,2,2,48,768]{4,3,2,1,0:T(8,128)(2,1)S(1)} collective-permute-done((bf16[2,2,2,48,768]{4,3,2,1,0:T(8,128)(2,1)S(1)}, bf16[2,2,2,48,768]{4,3,2,1,0:T(8,128)(2,1)S(1)}, u32[]{:S(2)}, u32[]{:S(2)}) %collective-permute-start.21) | collective-permute-done | bytes 589856 | tf_op jit(solution)/shard_map/ppermute | solution.py:373
  300.3 4.4 %collective-permute-done.22 = bf16[2,2,48,768]{3,2,1,0:T(8,128)(2,1)S(1)} collective-permute-done((bf16[2,2,48,768]{3,2,1,0:T(8,128)(2,1)S(1)}, bf16[2,2,48,768]{3,2,1,0:T(8,128)(2,1)S(1)}, u32[]{:S(2)}, u32[]{:S(2)}) %collective-permute-start.22) | collective-permute-done | bytes 294944 | tf_op jit(solution)/shard_map/ppermute | solution.py:373
  305.0 2.1 collective-permute-start.23
  307.7 3.3 collective-permute-done.23
  314.0 3.1 collective-permute-done.24
  321.0 2.6 collective-permute-start.31
  325.2 2.0 collective-permute-start.32
  327.3 1.7 collective-permute-done.32
  329.5 1.9 collective-permute-start.33
  331.4 1.8 collective-permute-done.33
  335.2 3.2 collective-permute-done.34
  (243 shorter events, 52.4 us)
Async XLA Ops:
  7.2 120.3 %all-gather.2.cloned.1.call-start = ((), (), s32[]{:S(2)}) async-start(), calls=%async_computation | async-start | bytes 2433024 | tf_op jit(solution)/shard_map/all_gather | solution.py:433
  9.0 9.6 %collective-permute-start.5 = (bf16[48,768]{1,0:T(8,128)(2,1)S(1)}, bf16[48,768]{1,0:T(8,128)(2,1)S(1)}, u32[]{:S(2)}, u32[]{:S(2)}) collective-permute-start(bf16[48,768]{1,0:T(8,128)(2,1)S(1)} %pad_maximum_fusion.5), channel_id=1, source_target_pairs={{0,2},{1,3},{2,0},{3,1},{4,6},{5,7},{6,4},{7,5},{8,10},{9,11},{10,... | collective-permute-start | bytes 221192 | tf_op jit(solution)/shard_map/ppermute | solution.py:373
  12.7 3.6 %collective-permute-start = (bf16[744]{0:T(1024)(128)(2,1)S(1)}, bf16[744]{0:T(1024)(128)(2,1)S(1)}, u32[]{:S(2)}, u32[]{:S(2)}) collective-permute-start(bf16[744]{0:T(1024)(128)(2,1)S(1)} %convert_element_type.236), channel_id=1, source_target_pairs={{0,2},{1,3},{2,0},{3,1},{4,6},{5,7},{6,4},{7,5},{8,10},{9,11},{10,... | collective-permute-start | bytes 4472 | tf_op jit(solution)/shard_map/ppermute | solution.py:373
  17.0 3.7 %collective-permute-start.1 = (bf16[2,744]{1,0:T(2,128)(2,1)S(1)}, bf16[2,744]{1,0:T(2,128)(2,1)S(1)}, u32[]{:S(2)}, u32[]{:S(2)}) collective-permute-start(bf16[2,744]{1,0:T(2,128)(2,1)S(1)} %pad_maximum_fusion.10), channel_id=1, source_target_pairs={{0,4},{1,5},{2,6},{3,7},{4,0},{5,1},{6,2},{7,3},{8,12},{9,13},{10,... | collective-permute-start | bytes 8936 | tf_op jit(solution)/shard_map/ppermute | solution.py:373
  18.7 5.2 %collective-permute-start.6 = (bf16[2,48,768]{2,1,0:T(8,128)(2,1)S(1)}, bf16[2,48,768]{2,1,0:T(8,128)(2,1)S(1)}, u32[]{:S(2)}, u32[]{:S(2)}) collective-permute-start(bf16[2,48,768]{2,1,0:T(8,128)(2,1)S(1)} %pad_maximum_fusion.4), channel_id=1, source_target_pairs={{0,4},{1,5},{2,6},{3,7},{4,0},{5,1},{6,2},{7,3},{8,12},{9,13},{10,... | collective-permute-start | bytes 442376 | tf_op jit(solution)/shard_map/ppermute | solution.py:373
  20.7 5.0 %collective-permute-start.2 = (bf16[2,2,744]{2,1,0:T(2,128)(2,1)S(1)}, bf16[2,2,744]{2,1,0:T(2,128)(2,1)S(1)}, u32[]{:S(2)}, u32[]{:S(2)}) collective-permute-start(bf16[2,2,744]{2,1,0:T(2,128)(2,1)S(1)} %pad_maximum_fusion.9), channel_id=1, source_target_pairs={{0,8},{1,9},{2,10},{3,11},{4,12},{5,13},{6,14},{7,15},{8,0},{9,1},... | collective-permute-start | bytes 17864 | tf_op jit(solution)/shard_map/ppermute | solution.py:373
  24.0 9.5 %collective-permute-start.7 = (bf16[2,2,48,768]{3,2,1,0:T(8,128)(2,1)S(1)}, bf16[2,2,48,768]{3,2,1,0:T(8,128)(2,1)S(1)}, u32[]{:S(2)}, u32[]{:S(2)}) collective-permute-start(bf16[2,2,48,768]{3,2,1,0:T(8,128)(2,1)S(1)} %pad_maximum_fusion.3), channel_id=1, source_target_pairs={{0,8},{1,9},{2,10},{3,11},{4,12},{5,13},{6,14},{7,15},{8,0},{9,1},... | collective-permute-start | bytes 884744 | tf_op jit(solution)/shard_map/ppermute | solution.py:373
  33.6 25.5 %collective-permute-start.8 = (bf16[2,2,2,48,768]{4,3,2,1,0:T(8,128)(2,1)S(1)}, bf16[2,2,2,48,768]{4,3,2,1,0:T(8,128)(2,1)S(1)}, u32[]{:S(2)}, u32[]{:S(2)}) collective-permute-start(bf16[2,2,2,48,768]{4,3,2,1,0:T(8,128)(2,1)S(1)} %pad_maximum_fusion.2), channel_id=1, source_target_pairs={{0,16},{1,17},{2,18},{3,19},{4,20},{5,21},{6,22},{7,23},{8,24},{9,... | collective-permute-start | bytes 1769480 | tf_op jit(solution)/shard_map/ppermute | solution.py:373
  35.1 23.8 %collective-permute-start.3 = (bf16[2,2,2,744]{3,2,1,0:T(2,128)(2,1)S(1)}, bf16[2,2,2,744]{3,2,1,0:T(2,128)(2,1)S(1)}, u32[]{:S(2)}, u32[]{:S(2)}) collective-permute-start(bf16[2,2,2,744]{3,2,1,0:T(2,128)(2,1)S(1)} %pad_maximum_fusion.7), channel_id=1, source_target_pairs={{0,16},{1,17},{2,18},{3,19},{4,20},{5,21},{6,22},{7,23},{8,24},{9,... | collective-permute-start | bytes 35720 | tf_op jit(solution)/shard_map/ppermute | solution.py:373
  59.1 2.6 collective-permute-start.4
  61.2 26.0 %collective-permute-start.9 = (bf16[2,2,2,2,48,768]{5,4,3,2,1,0:T(8,128)(2,1)}, bf16[2,2,2,2,48,768]{5,4,3,2,1,0:T(8,128)(2,1)}, u32[]{:S(2)}, u32[]{:S(2)}) collective-permute-start(bf16[2,2,2,2,48,768]{5,4,3,2,1,0:T(8,128)(2,1)} %pad_maximum_fusion.1), channel_id=1, source_target_pairs={{0,1},{1,0},{2,3},{3,2},{4,5},{5,4},{6,7},{7,6},{8,9},{9,8},{10,11... | collective-permute-start | bytes 3538952 | tf_op jit(solution)/shard_map/ppermute | solution.py:373
  205.6 22.6 %collective-permute-start.25 = (bf16[2,2,2,2,744]{4,3,2,1,0:T(2,128)(2,1)S(1)}, bf16[2,2,2,2,744]{4,3,2,1,0:T(2,128)(2,1)S(1)}, u32[]{:S(2)}, u32[]{:S(2)}) collective-permute-start(bf16[2,2,2,2,744]{4,3,2,1,0:T(2,128)(2,1)S(1)} %bitcast.205), channel_id=1, source_target_pairs={{0,1},{1,0},{2,3},{3,2},{4,5},{5,4},{6,7},{7,6},{8,9},{9,8},{10,11... | collective-permute-start | bytes 71432 | tf_op jit(solution)/shard_map/ppermute | solution.py:373
  227.6 39.7 %collective-permute-start.15 = (bf16[2,2,2,2,48,384]{5,4,0,1,2,3:T(8,128)(2,1)S(1)}, bf16[2,2,2,2,48,384]{5,4,0,1,2,3:T(8,128)(2,1)S(1)}, u32[]{:S(2)}, u32[]{:S(2)}) collective-permute-start(bf16[2,2,2,2,48,384]{5,4,0,1,2,3:T(8,128)(2,1)S(1)} %fusion.2), channel_id=1, source_target_pairs={{0,1},{1,0},{2,3},{3,2},{4,5},{5,4},{6,7},{7,6},{8,9},{9,8},{10,11... | collective-permute-start | bytes 1769480 | tf_op jit(solution)/shard_map/ppermute | solution.py:373
  227.8 40.9 %collective-permute-start.10 = (bf16[2,2,2,2,48,384]{5,4,0,2,3,1:T(8,128)(2,1)S(1)}, bf16[2,2,2,2,48,384]{5,4,0,2,3,1:T(8,128)(2,1)S(1)}, u32[]{:S(2)}, u32[]{:S(2)}) collective-permute-start(bf16[2,2,2,2,48,384]{5,4,0,2,3,1:T(8,128)(2,1)S(1)} %fusion.1), channel_id=1, source_target_pairs={{0,1},{1,0},{2,3},{3,2},{4,5},{5,4},{6,7},{7,6},{8,9},{9,8},{10,11... | collective-permute-start | bytes 1769480 | tf_op jit(solution)/shard_map/ppermute | solution.py:373
  228.4 3.8 %collective-permute-start.26 = (bf16[2,2,2,744]{3,2,1,0:T(2,128)(2,1)S(1)}, bf16[2,2,2,744]{3,2,1,0:T(2,128)(2,1)S(1)}, u32[]{:S(2)}, u32[]{:S(2)}) collective-permute-start(bf16[2,2,2,744]{3,2,1,0:T(2,128)(2,1)S(1)} %bitcast.206), channel_id=1, source_target_pairs={{0,2},{1,3},{2,0},{3,1},{4,6},{5,7},{6,4},{7,5},{8,10},{9,11},{10,... | collective-permute-start | bytes 35720 | tf_op jit(solution)/shard_map/ppermute | solution.py:373
  232.2 3.7 %collective-permute-start.27 = (bf16[2,2,744]{2,1,0:T(2,128)(2,1)S(1)}, bf16[2,2,744]{2,1,0:T(2,128)(2,1)S(1)}, u32[]{:S(2)}, u32[]{:S(2)}) collective-permute-start(bf16[2,2,744]{2,1,0:T(2,128)(2,1)S(1)} %bitcast.207), channel_id=1, source_target_pairs={{0,4},{1,5},{2,6},{3,7},{4,0},{5,1},{6,2},{7,3},{8,12},{9,13},{10,... | collective-permute-start | bytes 17864 | tf_op jit(solution)/shard_map/ppermute | solution.py:373
  235.9 3.7 %collective-permute-start.28 = (bf16[2,744]{1,0:T(2,128)(2,1)S(1)}, bf16[2,744]{1,0:T(2,128)(2,1)S(1)}, u32[]{:S(2)}, u32[]{:S(2)}) collective-permute-start(bf16[2,744]{1,0:T(2,128)(2,1)S(1)} %bitcast.208), channel_id=1, source_target_pairs={{0,8},{1,9},{2,10},{3,11},{4,12},{5,13},{6,14},{7,15},{8,0},{9,1},... | collective-permute-start | bytes 8936 | tf_op jit(solution)/shard_map/ppermute | solution.py:373
  239.6 27.0 %collective-permute-start.29 = (bf16[744]{0:T(1024)(128)(2,1)S(1)}, bf16[744]{0:T(1024)(128)(2,1)S(1)}, u32[]{:S(2)}, u32[]{:S(2)}) collective-permute-start(bf16[744]{0:T(1024)(128)(2,1)S(1)} %fusion.34), channel_id=1, source_target_pairs={{0,16},{1,17},{2,18},{3,19},{4,20},{5,21},{6,22},{7,23},{8,24},{9,... | collective-permute-start | bytes 4472 | tf_op jit(solution)/shard_map/ppermute | solution.py:373
  241.8 40.7 %collective-permute-start.20 = (bf16[2,2,2,2,48,768]{5,4,3,2,1,0:T(8,128)(2,1)S(1)}, bf16[2,2,2,2,48,768]{5,4,3,2,1,0:T(8,128)(2,1)S(1)}, u32[]{:S(2)}, u32[]{:S(2)}) collective-permute-start(bf16[2,2,2,2,48,768]{5,4,3,2,1,0:T(8,128)(2,1)S(1)} %dynamic-slice_bitcast_fusion), channel_id=1, source_target_pairs={{0,1},{1,0},{2,3},{3,2},{4,5},{5,4},{6,7},{7,6},{8,9},{9,8},{10,11... | collective-permute-start | bytes 3538952 | tf_op jit(solution)/shard_map/ppermute | solution.py:373
  267.4 9.5 %collective-permute-start.16 = (bf16[2,2,2,48,384]{4,3,0,1,2:T(8,128)(2,1)S(1)}, bf16[2,2,2,48,384]{4,3,0,1,2:T(8,128)(2,1)S(1)}, u32[]{:S(2)}, u32[]{:S(2)}) collective-permute-start(bf16[2,2,2,48,384]{4,3,0,1,2:T(8,128)(2,1)S(1)} %fusion.4), channel_id=1, source_target_pairs={{0,2},{1,3},{2,0},{3,1},{4,6},{5,7},{6,4},{7,5},{8,10},{9,11},{10,... | collective-permute-start | bytes 884744 | tf_op jit(solution)/shard_map/ppermute | solution.py:373
  268.9 9.5 %collective-permute-start.11 = (bf16[2,2,2,48,384]{4,3,0,1,2:T(8,128)(2,1)S(1)}, bf16[2,2,2,48,384]{4,3,0,1,2:T(8,128)(2,1)S(1)}, u32[]{:S(2)}, u32[]{:S(2)}) collective-permute-start(bf16[2,2,2,48,384]{4,3,0,1,2:T(8,128)(2,1)S(1)} %fusion.3), channel_id=1, source_target_pairs={{0,8},{1,9},{2,10},{3,11},{4,12},{5,13},{6,14},{7,15},{8,0},{9,1},... | collective-permute-start | bytes 884744 | tf_op jit(solution)/shard_map/ppermute | solution.py:373
  277.0 5.5 %collective-permute-start.17 = (bf16[2,2,48,384]{3,2,0,1:T(8,128)(2,1)S(1)}, bf16[2,2,48,384]{3,2,0,1:T(8,128)(2,1)S(1)}, u32[]{:S(2)}, u32[]{:S(2)}) collective-permute-start(bf16[2,2,48,384]{3,2,0,1:T(8,128)(2,1)S(1)} %fusion.10), channel_id=1, source_target_pairs={{0,4},{1,5},{2,6},{3,7},{4,0},{5,1},{6,2},{7,3},{8,12},{9,13},{10,... | collective-permute-start | bytes 442376 | tf_op jit(solution)/shard_map/ppermute | solution.py:373
  278.5 7.1 %collective-permute-start.12 = (bf16[2,2,48,384]{3,2,0,1:T(8,128)(2,1)S(1)}, bf16[2,2,48,384]{3,2,0,1:T(8,128)(2,1)S(1)}, u32[]{:S(2)}, u32[]{:S(2)}) collective-permute-start(bf16[2,2,48,384]{3,2,0,1:T(8,128)(2,1)S(1)} %fusion.9), channel_id=1, source_target_pairs={{0,2},{1,3},{2,0},{3,1},{4,6},{5,7},{6,4},{7,5},{8,10},{9,11},{10,... | collective-permute-start | bytes 442376 | tf_op jit(solution)/shard_map/ppermute | solution.py:373
  282.9 14.9 %collective-permute-start.21 = (bf16[2,2,2,48,768]{4,3,2,1,0:T(8,128)(2,1)S(1)}, bf16[2,2,2,48,768]{4,3,2,1,0:T(8,128)(2,1)S(1)}, u32[]{:S(2)}, u32[]{:S(2)}) collective-permute-start(bf16[2,2,2,48,768]{4,3,2,1,0:T(8,128)(2,1)S(1)} %fusion), channel_id=1, source_target_pairs={{0,4},{1,5},{2,6},{3,7},{4,0},{5,1},{6,2},{7,3},{8,12},{9,13},{10,... | collective-permute-start | bytes 1769480 | tf_op jit(solution)/shard_map/ppermute | solution.py:373
  283.5 4.4 %collective-permute-start.18 = (bf16[2,48,384]{2,1,0:T(8,128)(2,1)S(1)}, bf16[2,48,384]{2,1,0:T(8,128)(2,1)S(1)}, u32[]{:S(2)}, u32[]{:S(2)}) collective-permute-start(bf16[2,48,384]{2,1,0:T(8,128)(2,1)S(1)} %fusion.15), channel_id=1, source_target_pairs={{0,8},{1,9},{2,10},{3,11},{4,12},{5,13},{6,14},{7,15},{8,0},{9,1},... | collective-permute-start | bytes 221192 | tf_op jit(solution)/shard_map/ppermute | solution.py:373
  285.6 14.6 %collective-permute-start.13 = (bf16[2,48,384]{2,1,0:T(8,128)(2,1)S(1)}, bf16[2,48,384]{2,1,0:T(8,128)(2,1)S(1)}, u32[]{:S(2)}, u32[]{:S(2)}) collective-permute-start(bf16[2,48,384]{2,1,0:T(8,128)(2,1)S(1)} %fusion.14), channel_id=1, source_target_pairs={{0,4},{1,5},{2,6},{3,7},{4,0},{5,1},{6,2},{7,3},{8,12},{9,13},{10,... | collective-permute-start | bytes 221192 | tf_op jit(solution)/shard_map/ppermute | solution.py:373
  298.0 6.8 %collective-permute-start.22 = (bf16[2,2,48,768]{3,2,1,0:T(8,128)(2,1)S(1)}, bf16[2,2,48,768]{3,2,1,0:T(8,128)(2,1)S(1)}, u32[]{:S(2)}, u32[]{:S(2)}) collective-permute-start(bf16[2,2,48,768]{3,2,1,0:T(8,128)(2,1)S(1)} %fusion.5), channel_id=1, source_target_pairs={{0,2},{1,3},{2,0},{3,1},{4,6},{5,7},{6,4},{7,5},{8,10},{9,11},{10,... | collective-permute-start | bytes 884744 | tf_op jit(solution)/shard_map/ppermute | solution.py:373
  299.3 7.7 %collective-permute-start.19 = (bf16[48,384]{1,0:T(8,128)(2,1)S(1)}, bf16[48,384]{1,0:T(8,128)(2,1)S(1)}, u32[]{:S(2)}, u32[]{:S(2)}) collective-permute-start(bf16[48,384]{1,0:T(8,128)(2,1)S(1)} %fusion.18), channel_id=1, source_target_pairs={{0,16},{1,17},{2,18},{3,19},{4,20},{5,21},{6,22},{7,23},{8,24},{9,... | collective-permute-start | bytes 110600 | tf_op jit(solution)/shard_map/ppermute | solution.py:373
  300.3 38.8 %copy-start.30 = (f32[48,768]{1,0:T(8,128)S(1)}, f32[48,768]{1,0:T(8,128)}, u32[]{:S(2)}) copy-start(f32[48,768]{1,0:T(8,128)} %param.24) | copy-start | bytes 442372
  300.3 38.8 %copy-start.33 = (f32[48,768]{1,0:T(8,128)S(1)}, f32[48,768]{1,0:T(8,128)}, u32[]{:S(2)}) copy-start(f32[48,768]{1,0:T(8,128)} %param.31) | copy-start | bytes 442372
  300.3 38.8 %copy-start.34 = (f32[48,768]{1,0:T(8,128)S(1)}, f32[48,768]{1,0:T(8,128)}, u32[]{:S(2)}) copy-start(f32[48,768]{1,0:T(8,128)} %param.30) | copy-start | bytes 442372
  304.8 35.1 %copy-start.39 = (f32[744]{0:T(1024)S(1)}, f32[744]{0:T(1024)}, u32[]{:S(2)}) copy-start(f32[744]{0:T(1024)} %param.25) | copy-start | bytes 8932
  304.8 35.1 %copy-start.40 = (f32[744]{0:T(1024)S(1)}, f32[744]{0:T(1024)}, u32[]{:S(2)}) copy-start(f32[744]{0:T(1024)} %param.33) | copy-start | bytes 8932
  304.9 35.1 %copy-start.41 = (f32[744]{0:T(1024)S(1)}, f32[744]{0:T(1024)}, u32[]{:S(2)}) copy-start(f32[744]{0:T(1024)} %param.32) | copy-start | bytes 8932
  304.9 35.7 %copy-start.31 = (f32[48,384]{1,0:T(8,128)S(1)}, f32[48,384]{1,0:T(8,128)}, u32[]{:S(2)}) copy-start(f32[48,384]{1,0:T(8,128)} %param.23) | copy-start | bytes 221188
  304.9 35.7 %copy-start.32 = (f32[48,384]{1,0:T(8,128)S(1)}, f32[48,384]{1,0:T(8,128)}, u32[]{:S(2)}) copy-start(f32[48,384]{1,0:T(8,128)} %param.22) | copy-start | bytes 221188
  304.9 35.7 %copy-start.35 = (f32[48,384]{1,0:T(8,128)S(1)}, f32[48,384]{1,0:T(8,128)}, u32[]{:S(2)}) copy-start(f32[48,384]{1,0:T(8,128)} %param.29) | copy-start | bytes 221188
  304.9 35.7 %copy-start.36 = (f32[48,384]{1,0:T(8,128)S(1)}, f32[48,384]{1,0:T(8,128)}, u32[]{:S(2)}) copy-start(f32[48,384]{1,0:T(8,128)} %param.28) | copy-start | bytes 221188
  304.9 35.7 %copy-start.37 = (f32[48,384]{1,0:T(8,128)S(1)}, f32[48,384]{1,0:T(8,128)}, u32[]{:S(2)}) copy-start(f32[48,384]{1,0:T(8,128)} %param.27) | copy-start | bytes 221188
  304.9 35.7 %copy-start.38 = (f32[48,384]{1,0:T(8,128)S(1)}, f32[48,384]{1,0:T(8,128)}, u32[]{:S(2)}) copy-start(f32[48,384]{1,0:T(8,128)} %param.26) | copy-start | bytes 221188
  305.0 6.0 %collective-permute-start.23 = (bf16[2,48,768]{2,1,0:T(8,128)(2,1)S(1)}, bf16[2,48,768]{2,1,0:T(8,128)(2,1)S(1)}, u32[]{:S(2)}, u32[]{:S(2)}) collective-permute-start(bf16[2,48,768]{2,1,0:T(8,128)(2,1)S(1)} %fusion.11), channel_id=1, source_target_pairs={{0,8},{1,9},{2,10},{3,11},{4,12},{5,13},{6,14},{7,15},{8,0},{9,1},... | collective-permute-start | bytes 442376 | tf_op jit(solution)/shard_map/ppermute | solution.py:373
  307.1 5.1 %collective-permute-start.14 = (bf16[48,384]{1,0:T(8,128)(2,1)S(1)}, bf16[48,384]{1,0:T(8,128)(2,1)S(1)}, u32[]{:S(2)}, u32[]{:S(2)}) collective-permute-start(bf16[48,384]{1,0:T(8,128)(2,1)S(1)} %fusion.17), channel_id=1, source_target_pairs={{0,16},{1,17},{2,18},{3,19},{4,20},{5,21},{6,22},{7,23},{8,24},{9,... | collective-permute-start | bytes 110600 | tf_op jit(solution)/shard_map/ppermute | solution.py:373
  311.0 6.1 %collective-permute-start.24 = (bf16[48,768]{1,0:T(8,128)(2,1)S(1)}, bf16[48,768]{1,0:T(8,128)(2,1)S(1)}, u32[]{:S(2)}, u32[]{:S(2)}) collective-permute-start(bf16[48,768]{1,0:T(8,128)(2,1)S(1)} %fusion.16), channel_id=1, source_target_pairs={{0,16},{1,17},{2,18},{3,19},{4,20},{5,21},{6,22},{7,23},{8,24},{9,... | collective-permute-start | bytes 221192 | tf_op jit(solution)/shard_map/ppermute | solution.py:373
  319.1 1.3 collective-permute-start.30
  321.0 3.7 %collective-permute-start.31 = (f32[1,1]{1,0:T(1,128)}, f32[1,1]{1,0:T(1,128)}, u32[]{:S(2)}, u32[]{:S(2)}) collective-permute-start(f32[1,1]{1,0:T(1,128)} %add.279), channel_id=1, source_target_pairs={{0,2},{1,3},{2,0},{3,1},{4,6},{5,7},{6,4},{7,5},{8,10},{9,11},{10,... | collective-permute-start | bytes 20 | tf_op jit(solution)/shard_map/ppermute | solution.py:373
  325.2 3.7 %collective-permute-start.32 = (f32[1,1]{1,0:T(1,128)}, f32[1,1]{1,0:T(1,128)}, u32[]{:S(2)}, u32[]{:S(2)}) collective-permute-start(f32[1,1]{1,0:T(1,128)} %add.280), channel_id=1, source_target_pairs={{0,4},{1,5},{2,6},{3,7},{4,0},{5,1},{6,2},{7,3},{8,12},{9,13},{10,... | collective-permute-start | bytes 20 | tf_op jit(solution)/shard_map/ppermute | solution.py:373
  329.5 3.7 %collective-permute-start.33 = (f32[1,1]{1,0:T(1,128)}, f32[1,1]{1,0:T(1,128)}, u32[]{:S(2)}, u32[]{:S(2)}) collective-permute-start(f32[1,1]{1,0:T(1,128)} %add.281), channel_id=1, source_target_pairs={{0,8},{1,9},{2,10},{3,11},{4,12},{5,13},{6,14},{7,15},{8,0},{9,1},... | collective-permute-start | bytes 20 | tf_op jit(solution)/shard_map/ppermute | solution.py:373
  333.8 4.6 %collective-permute-start.34 = (f32[1,1]{1,0:T(1,128)}, f32[1,1]{1,0:T(1,128)}, u32[]{:S(2)}, u32[]{:S(2)}) collective-permute-start(f32[1,1]{1,0:T(1,128)} %add.282), channel_id=1, source_target_pairs={{0,16},{1,17},{2,18},{3,19},{4,20},{5,21},{6,22},{7,23},{8,24},{9,... | collective-permute-start | bytes 20 | tf_op jit(solution)/shard_map/ppermute | solution.py:373
  (34 other events, 226.1 us)
Sparse Core Ops, SparseCore 0:
  14.4 72.3 all-gather.1

commit v2 on v1

v2 whole, which is shorter than its diff:
```python
import functools
import jax
import jax.numpy as jnp
import numpy as np
from jax import lax
from jax.experimental import pallas as pl
from jax.experimental.pallas import tpu as pltpu
from jax.sharding import PartitionSpec as P

STEP = 10
DROP_RATE = 0.2
RATE_MATRIX = 0.05
RATE_VECTOR = 0.3
LAYER_DECAY = 0.8
BETA_ONE = 0.9
BETA_TWO = 0.999
ADAM_EPS = 1e-08
WEIGHT_DECAY = 0.05
CLIP_NORM = 1.0
D = 384
FF = 1536
LN_EPS = 1e-06
F32 = jnp.float32
BF16 = jnp.bfloat16
VMEM = pl.BlockSpec(memory_space=pltpu.VMEM)
SMEM = pl.BlockSpec(memory_space=pltpu.SMEM)
HBM = pl.BlockSpec(memory_space=pltpu.HBM)
ROWS = (((0,), (0,)), ((), ()))
COLS = (((1,), (1,)), ((), ()))
DEPTH_BIAS, GAIN_ONE, BIAS_ONE, HIDDEN_BIAS, OUT_BIAS, LAYER_SCALE, GAIN_TWO, BIAS_TWO, DOWN_BIAS = 49, 50, 51, 52, 56, 57, 58, 59, 60


def near(shape, dtype):
    return jax.ShapeDtypeStruct(shape, dtype)


def far(shape, dtype):
    return pltpu.HBM(shape, dtype)


def held(x):
    return pltpu.with_memory_space_constraint(x, pltpu.HBM)


def dma(src, dst, sem):
    return pltpu.make_async_copy(src, dst, sem)


def start(copies):
    for copy in copies:
        copy.start()


def wait(copies):
    for copy in copies:
        copy.wait()


def kernel_call(body, out, specs, scratch, args, after, us, mib, aliases=None):
    specs = specs + [HBM] * len(after)
    args = tuple(args) + tuple(after)
    args = [held(x) if spec is HBM else x for spec, x in zip(specs, args)]
    return pl.pallas_call(
        body,
        out_shape=tuple(out),
        in_specs=specs,
        out_specs=tuple(HBM if isinstance(x, type(far((8, 128), F32))) else VMEM for x in out),
        scratch_shapes=scratch,
        input_output_aliases=aliases or {},
        cost_estimate=pl.CostEstimate(flops=int(us * 1e9), bytes_accessed=0, transcendentals=0),
        compiler_params=pltpu.CompilerParams(vmem_limit_bytes=mib << 20),
    )(*args)


def norm_of(v):
    c = v - jnp.mean(v, axis=-1, keepdims=True)
    inv = lax.rsqrt(jnp.mean(c * c, axis=-1, keepdims=True) + LN_EPS)
    return c * inv, inv


def norm_back(back, unit, inv, gain):
    scaled = back * gain
    m1 = jnp.mean(scaled, axis=-1, keepdims=True)
    m2 = jnp.mean(scaled * unit, axis=-1, keepdims=True)
    return inv * (scaled - m1 - unit * m2)


def conv_rows(src, taps, h, t, lanes, side, base, flip):
    def one(ky, acc):
        acc = list(acc)
        x = [src[h + ky - 3, w, t, lanes] for w in range(side)]
        for kx in range(7):
            tap = taps[48 - (ky * 7 + kx) if flip else ky * 7 + kx, :, lanes]
            for w in range(side):
                if 0 <= w + kx - 3 < side:
                    acc[w] = acc[w] + x[w + kx - 3] * tap
        return tuple(acc)

    first = jnp.maximum(3 - h, 0)
    last = jnp.minimum(7, side + 3 - h)
    return lax.fori_loop(first, last, one, tuple(base))


def conv_kernel(begin, end, fresh, *refs):
    if fresh:
        small_hbm, img_hbm, sel_ref, mix_ref = refs[:4]
        mixed_hbm, unit_hbm, inv_hbm, norm_hbm, small_ref, mixed_ref, taps, conv_ref, unit_ref, inv_ref, norm_ref, sem, img_ref = refs[-13:]
    else:
        small_hbm, mixed_hbm = refs[:2]
        unit_hbm, inv_hbm, norm_hbm, small_ref, mixed_ref, taps, conv_ref, unit_ref, inv_ref, norm_ref, sem = refs[-11:]
    side, _, imgs, _ = mixed_ref.shape
    low = max(begin - 3, 0)
    high = side if fresh else min(end + 3, side)
    rows = end - begin
    load = dma(small_hbm, small_ref, sem.at[4, 0])
    load.start()

    def enter(h):
        if fresh:
            return dma(img_hbm.at[h], img_ref.at[h], sem.at[3, h])
        return dma(mixed_hbm.at[h], mixed_ref.at[h], sem.at[3, h])

    def store(h):
        return dma(mixed_ref.at[h], mixed_hbm.at[h], sem.at[5, h])

    for h in range(low, high):
        enter(h).start()
    load.wait()
    for t in range(49):
        taps[t] = jnp.broadcast_to(small_ref[t : t + 1, :], (8, D))
    if fresh:
        mix = mix_ref[...][None]
        rest = 1.0 - mix

        def blend(h, _):
            enter(h).wait()
            x = img_ref[h].reshape(side * imgs, D)
            other = jnp.dot(sel_ref[...], x, preferred_element_type=F32).reshape(side, imgs, D)
            mixed_ref[h] = mix * x.reshape(side, imgs, D).astype(F32) + rest * other
            store(h).start()
            return 0

        lax.fori_loop(0, side, blend, 0)
    else:
        for h in range(low, min(begin + 3, high)):
            enter(h).wait()

    def conv(r, _):
        h = r + begin
        if not fresh:

            @pl.when(h + 3 < high)
            def _():
                enter(h + 3).wait()

        for t in range(imgs // 8):
            at = pl.ds(t * 8, 8)
            for g in range(D // 128):
                lanes = pl.ds(g * 128, 128)
                base = jnp.broadcast_to(small_ref[DEPTH_BIAS : DEPTH_BIAS + 1, lanes], (8, 128))
                acc = conv_rows(mixed_ref, taps, h, at, lanes, side, [base] * side, False)
                for w in range(side):
                    conv_ref[r, w, at, lanes] = acc[w]
        return 0

    lax.fori_loop(0, rows, conv, 0)
    gain = small_ref[GAIN_ONE : GAIN_ONE + 1, :][None]
    bias = small_ref[BIAS_ONE : BIAS_ONE + 1, :][None]

    def leave(r):
        return (
            dma(unit_ref.at[r], unit_hbm.at[r + begin], sem.at[0, r]),
            dma(inv_ref.at[r], inv_hbm.at[r + begin], sem.at[1, r]),
            dma(norm_ref.at[r], norm_hbm.at[r + begin], sem.at[2, r]),
        )

    def norm(r, _):
        unit, inv = norm_of(conv_ref[r])
        unit_ref[r] = unit.astype(BF16)
        inv_ref[r] = inv
        norm_ref[r] = (unit * gain + bias).astype(BF16)
        start(leave(r))
        return 0

    lax.fori_loop(0, rows, norm, 0)
    for r in range(rows):
        wait(leave(r))
    if fresh:
        for h in range(side):
            store(h).wait()


def conv_forward(small, inputs, begin, end, so_far=(), after=()):
    fresh = not so_far
    full = inputs[0].shape
    side = full[0]
    thin = full[:3] + (1,)
    rows = end - begin
    out = [far(full, BF16), far(thin, F32), far(full, BF16)]
    scratch = [
        pltpu.VMEM(small.shape, F32),
        pltpu.VMEM(full, F32),
        pltpu.VMEM((49, 8, D), F32),
        pltpu.VMEM((rows,) + full[1:], F32),
        pltpu.VMEM((rows,) + full[1:], BF16),
        pltpu.VMEM((rows,) + thin[1:], F32),
        pltpu.VMEM((rows,) + full[1:], BF16),
        pltpu.SemaphoreType.DMA((6, side)),
    ]
    specs = [HBM] * 2
    if fresh:
        out = [far(full, F32)] + out
        scratch.append(pltpu.VMEM(full, BF16))
        specs = [HBM] * 2 + [VMEM] * 2
    return kernel_call(
        functools.partial(conv_kernel, begin, end, fresh),
        out,
        specs + [HBM] * len(so_far),
        scratch,
        (small,) + tuple(inputs) + tuple(so_far),
        after,
        21 * rows / side + 3 * fresh,
        28,
        {2 + k: k for k in range(len(so_far))},
    )


def hidden_kernel(block, norm_hbm, mixed_hbm, near_hbm, far_hbm, small_hbm, hb_ref, keep_ref, *rest):
    act_hbm, dg_hbm, branch_hbm, unit_hbm, inv_hbm, out_hbm = rest[-20:-14]
    near_ref, far_ref, small_ref, norm_ref, mixed_ref, act_ref, dg_ref, branch_ref, unit_ref, inv_ref, out_ref, isem, osem, wsem = rest[-14:]
    rows = norm_hbm.shape[0]
    steps = rows // block
    imgs = keep_ref.shape[0]
    shape = (block // imgs, imgs, D)
    wide = near_ref.shape[0]

    def spot(i):
        return pl.ds(pl.multiple_of(i * block, block), block)

    def enter(i):
        s = i % 2
        return (
            dma(norm_hbm.at[spot(i), :], norm_ref.at[s], isem.at[0, s]),
            dma(mixed_hbm.at[spot(i), :], mixed_ref.at[s], isem.at[1, s]),
        )

    def leave(i):
        s = i % 2
        pairs = ((act_ref, act_hbm), (dg_ref, dg_hbm), (branch_ref, branch_hbm), (unit_ref, unit_hbm), (inv_ref, inv_hbm), (out_ref, out_hbm))
        return [dma(a.at[s], b.at[spot(i), :], osem.at[k, s]) for k, (a, b) in enumerate(pairs)]

    loads = (dma(small_hbm, small_ref, wsem.at[0]), dma(near_hbm, near_ref, wsem.at[1]), dma(far_hbm, far_ref, wsem.at[2]))
    start(enter(0))
    start(loads)
    wait(loads)
    scale = (keep_ref[...] * small_ref[LAYER_SCALE : LAYER_SCALE + 1, :])[None]
    gain = small_ref[GAIN_TWO : GAIN_TWO + 1, :][None]
    bias = small_ref[BIAS_TWO : BIAS_TWO + 1, :][None]

    def body(i, _):
        s = i % 2

        @pl.when(i + 1 < steps)
        def _():
            start(enter(i + 1))

        @pl.when(i >= 2)
        def _():
            wait(leave(i - 2))

        wait(enter(i))
        x = norm_ref[s]
        branch = jnp.broadcast_to(small_ref[OUT_BIAS : OUT_BIAS + 1, :], (block, D))
        for j, pair_ref in enumerate((near_ref, far_ref)):
            cols = pl.ds(j * wide, wide)
            pre = lax.dot_general(x, pair_ref[:, :D], COLS, preferred_element_type=F32) + hb_ref[:, cols]
            phi = 0.5 + 0.5 * lax.erf(pre * 0.7071067811865476)
            bell = jnp.exp2(pre * pre * -0.7213475204444817) * 0.3989422804014327
            act = (pre * phi).astype(BF16)
            act_ref[s, :, cols] = act
            dg_ref[s, :, cols] = (phi + pre * bell).astype(BF16)
            branch = branch + jnp.dot(act, pair_ref[:, D:], preferred_element_type=F32)
        branch_ref[s] = branch.astype(BF16)
        unit, inv = norm_of(mixed_ref[s].reshape(shape) + scale * branch.reshape(shape))
        unit_ref[s] = unit.astype(BF16).reshape(block, D)
        inv_ref[s] = inv.reshape(block, 1)
        out_ref[s] = (unit * gain + bias).astype(BF16).reshape(block, D)
        start(leave(i))
        return 0

    lax.fori_loop(0, steps, body, 0)
    for i in range(max(steps - 2, 0), steps):
        wait(leave(i))


def hidden_forward(norm, mixed, pair, small, hb, keep, after=(), block=448):
    rows = norm.shape[0]
    two = lambda width, dtype: pltpu.VMEM((2, block, width), dtype)
    return kernel_call(
        functools.partial(hidden_kernel, block),
        [far((rows, FF), BF16)] * 2 + [far((rows, D), BF16)] * 2 + [far((rows, 1), F32), far((rows, D), BF16)],
        [HBM] * 5 + [VMEM] * 2,
        [pltpu.VMEM(pair[0].shape, BF16)] * 2
        + [pltpu.VMEM(small.shape, F32), two(D, BF16), two(D, F32), two(FF, BF16), two(FF, BF16)]
        + [two(D, BF16), two(D, BF16), two(1, F32), two(D, BF16)]
        + [pltpu.SemaphoreType.DMA((2, 2)), pltpu.SemaphoreType.DMA((6, 2)), pltpu.SemaphoreType.DMA((3,))],
        (norm, mixed, *pair, small, hb, keep),
        after,
        17,
        32,
    )


def grad_down_kernel(origin_ref, norm_hbm, dy_hbm, *rest):
    near_ref, far_ref, gdb_ref, dy_ref, norm_ref, wide, sem = rest[-7:]
    half, _, _, _, imgs, _ = norm_hbm.shape
    rows = half * half * imgs
    enter = [dma(dy_hbm, dy_ref, sem.at[4])]
    enter += [dma(norm_hbm.at[:, k // 2, :, k % 2], norm_ref.at[k], sem.at[k]) for k in range(4)]
    start(enter)
    enter[0].wait()
    dy = dy_ref[...].reshape(rows, 2 * D)
    gdb_ref[...] = jnp.sum(dy.astype(F32).reshape(half * half, imgs, 2 * D), axis=0)
    for k in range(4):
        enter[k + 1].wait()
        x = norm_ref[k].reshape(rows, D)
        for g in range(6):
            wide[g, pl.ds(k, D, stride=4), :] = lax.dot_general(
                x, dy[:, g * 128 : (g + 1) * 128], ROWS, preferred_element_type=F32
            )
    pieces = origin_ref.shape[0]
    deep = 4 * D // pieces
    for half_ref, first in ((near_ref, 0), (far_ref, pieces // 2)):
        def move(j, _):
            begin = pl.multiple_of(origin_ref[first + j] * deep, 16)
            to = pl.multiple_of(j * deep, 16)
            for g in range(6):
                half_ref[pl.ds(to, deep), pl.ds(g * 128, 128)] = wide[g, pl.ds(begin, deep), :].astype(BF16)
            return 0

        lax.fori_loop(0, pieces // 2, move, 0)


def grad_down(origin, norm, dy, after=()):
    half = dy.shape[0]
    imgs = dy.shape[2]
    return kernel_call(
        grad_down_kernel,
        [near((2 * D, 2 * D), BF16)] * 2 + [near((imgs, 2 * D), F32)],
        [SMEM] + [HBM] * 2,
        [
            pltpu.VMEM(dy.shape, BF16),
            pltpu.VMEM((4, half, half, imgs, D), BF16),
            pltpu.VMEM((6, 4 * D, 128), F32),
            pltpu.SemaphoreType.DMA((5,)),
        ],
        (origin, norm, dy),
        after,
        8,
        24,
    )


def down_kernel(origin_ref, norm_hbm, unit_hbm, inv_hbm, branch_hbm, near_hbm, far_hbm, dy_hbm, small_hbm, keep_ref, db_ref, *rest):
    out_ref, bb_hbm, sums_ref, res_hbm = rest[-20:-16]
    near_ref, far_ref, dy_ref, small_ref, norm_ref, unit_ref, inv_ref, branch_ref, bb_ref, res_ref, acc, wide, wk, wsem, isem, osem = rest[-16:]
    half, _, _, _, imgs, _ = norm_hbm.shape
    rows = half * half * imgs
    loads = [dma(near_hbm, near_ref, wsem.at[0]), dma(far_hbm, far_ref, wsem.at[1]), dma(dy_hbm, dy_ref, wsem.at[2]), dma(small_hbm, small_ref, wsem.at[3])]
    start(loads)

    def enter(k):
        pairs = ((norm_hbm, norm_ref), (unit_hbm, unit_ref), (inv_hbm, inv_ref), (branch_hbm, branch_ref))
        return [dma(a.at[:, k // 2, :, k % 2], b.at[k], isem.at[j, k]) for j, (a, b) in enumerate(pairs)]

    def leave(k):
        pairs = ((bb_ref, bb_hbm), (res_ref, res_hbm))
        return [dma(a.at[k], b.at[:, k // 2, :, k % 2], osem.at[j, k]) for j, (a, b) in enumerate(pairs)]

    for k in range(4):
        start(enter(k))
    pieces = origin_ref.shape[0]
    deep = 4 * D // pieces
    for half_ref, load, first in ((near_ref, loads[0], 0), (far_ref, loads[1], pieces // 2)):
        load.wait()

        def move(j, _):
            begin = pl.multiple_of(origin_ref[first + j] * deep, 16)
            to = pl.multiple_of(j * deep, 16)
            for g in range(6):
                wide[g, pl.ds(begin, deep), :] = half_ref[pl.ds(to, deep), pl.ds(g * 128, 128)].astype(F32)
            return 0

        lax.fori_loop(0, pieces // 2, move, 0)
    for g in range(6):
        for k in range(4):
            wk[k, :, pl.ds(g * 128, 128)] = wide[g, pl.ds(k, D, stride=4), :].astype(BF16)
    acc[...] = jnp.broadcast_to(db_ref[...], acc.shape)
    sums_ref[...] = jnp.zeros(sums_ref.shape, F32)
    shape = (half * half, imgs, D)
    loads[2].wait()
    loads[3].wait()
    gain = small_ref[GAIN_TWO : GAIN_TWO + 1, :][None]
    keep = keep_ref[...][None]
    scale = keep * small_ref[LAYER_SCALE : LAYER_SCALE + 1, :][None]

    def part(k, _):
        wait(enter(k))
        x = norm_ref[k].reshape(rows, D)
        acc[...] += jnp.dot(x, wk[k], preferred_element_type=F32)
        back = lax.dot_general(dy_ref[...].reshape(rows, 2 * D), wk[k], COLS, preferred_element_type=F32).reshape(shape)
        unit = unit_ref[k].reshape(shape).astype(F32)
        sums_ref[0] += jnp.sum(back * unit, axis=0)
        sums_ref[1] += jnp.sum(back, axis=0)
        res = norm_back(back, unit, inv_ref[k].reshape(half * half, imgs, 1), gain)
        res_ref[k] = res.reshape(half, half, imgs, D)
        kept = res * keep
        sums_ref[2] += jnp.sum(kept * branch_ref[k].reshape(shape).astype(F32), axis=0)
        bb = (res * scale).astype(BF16)
        bb_ref[k] = bb.reshape(half, half, imgs, D)
        start(leave(k))
        sums_ref[3] += jnp.sum(bb.astype(F32), axis=0)
        return 0

    lax.fori_loop(0, 4, part, 0)
    out_ref[...] = acc[...].astype(BF16).reshape(out_ref.shape)
    for k in range(4):
        wait(leave(k))


def down_both(origin, norm, unit, inv, branch, wd, dy, small, keep, db, after=()):
    half, _, _, _, imgs, _ = norm.shape
    rows = half * half * imgs
    four = lambda width, dtype: pltpu.VMEM((4, half, half, imgs, width), dtype)
    return kernel_call(
        down_kernel,
        [near((half, half, imgs, 2 * D), BF16), far(norm.shape, BF16), near((4, imgs, D), F32), far(norm.shape, F32)],
        [SMEM] + [HBM] * 8 + [VMEM] * 2,
        [pltpu.VMEM(wd[0].shape, BF16)] * 2
        + [pltpu.VMEM(dy.shape, BF16), pltpu.VMEM(small.shape, F32)]
        + [four(D, BF16), four(D, BF16), four(1, F32), four(D, BF16), four(D, BF16), four(D, F32)]
        + [pltpu.VMEM((rows, 2 * D), F32), pltpu.VMEM((6, 4 * D, 128), F32), pltpu.VMEM((4, D, 2 * D), BF16)]
        + [pltpu.SemaphoreType.DMA((4,)), pltpu.SemaphoreType.DMA((4, 4)), pltpu.SemaphoreType.DMA((2, 4))],
        (origin, norm, unit, inv, branch, *wd, dy, small, keep, db),
        after,
        13,
        44,
    )


def pair_grad_kernel(block, bb_hbm, act_hbm, dg_hbm, norm_hbm, near_hbm, far_hbm, *rest):
    gnear_ref, gfar_ref, hb_ref, p_hbm, near_ref, far_ref, acc, bb_ref, act_ref, dg_ref, norm_ref, p_ref, sem, wsem = rest[-14:]
    rows = bb_hbm.shape[0]
    imgs = hb_ref.shape[0]
    steps = rows // block
    wide = near_ref.shape[0]

    def spot(i):
        return pl.ds(pl.multiple_of(i * block, block), block)

    def enter(i):
        s = i % 2
        pairs = ((act_hbm, act_ref), (dg_hbm, dg_ref), (norm_hbm, norm_ref), (bb_hbm, bb_ref))
        return [dma(a.at[spot(i), :], b.at[s], sem.at[k, s]) for k, (a, b) in enumerate(pairs)]

    def leave(i):
        return dma(p_ref.at[i % 2], p_hbm.at[spot(i), :], sem.at[4, i % 2])

    loads = [dma(near_hbm.at[:, pl.ds(D, D)], near_ref, wsem.at[0]), dma(far_hbm.at[:, pl.ds(D, D)], far_ref, wsem.at[1])]
    start(loads)
    start(enter(0))
    hb_ref[...] = jnp.zeros(hb_ref.shape, F32)
    acc[...] = jnp.zeros(acc.shape, F32)
    wait(loads)

    def body(i, _):
        s = i % 2

        @pl.when(i + 1 < steps)
        def _():
            start(enter(i + 1))

        @pl.when(i >= 2)
        def _():
            leave(i - 2).wait()

        wait(enter(i))
        b = bb_ref[s]
        x = norm_ref[s]
        for j, out_ref in enumerate((near_ref, far_ref)):
            cols = pl.ds(j * wide, wide)
            back = lax.dot_general(b, out_ref[...], COLS, preferred_element_type=F32)
            p = (back * dg_ref[s, :, cols].astype(F32)).astype(BF16)
            p_ref[s, :, cols] = p
            hb_ref[:, cols] += jnp.sum(p.astype(F32).reshape(block // imgs, imgs, wide), axis=0)
            acc[cols, D:] += lax.dot_general(act_ref[s, :, cols], b, ROWS, preferred_element_type=F32)
            acc[cols, :D] += lax.dot_general(p, x, ROWS, preferred_element_type=F32)
        leave(i).start()
        return 0

    lax.fori_loop(0, steps, body, 0)
    gnear_ref[...] = acc[:wide].astype(BF16)
    gfar_ref[...] = acc[wide:].astype(BF16)
    for i in range(max(steps - 2, 0), steps):
        leave(i).wait()


def pair_grad(bb, act, dg, norm, pair, imgs, after=(), block=784):
    rows = bb.shape[0]
    two = lambda width: pltpu.VMEM((2, block, width), BF16)
    return kernel_call(
        functools.partial(pair_grad_kernel, block),
        [near((FF // 2, 2 * D), BF16)] * 2 + [near((imgs, FF), F32), far((rows, FF), BF16)],
        [HBM] * 6,
        [pltpu.VMEM((FF // 2, D), BF16)] * 2
        + [pltpu.VMEM((FF, 2 * D), F32), two(D), two(FF), two(FF), two(D), two(FF)]
        + [pltpu.SemaphoreType.DMA((5, 2)), pltpu.SemaphoreType.DMA((2,))],
        (bb, act, dg, norm, *pair),
        after,
        23,
        44,
    )


def back_one_kernel(block, p_hbm, unit_hbm, inv_hbm, near_hbm, far_hbm, small_hbm, *rest):
    conv_hbm, sums_ref, near_ref, far_ref, small_ref, p_ref, unit_ref, inv_ref, conv_ref, sem, wsem = rest[-11:]
    rows = p_hbm.shape[0]
    imgs = sums_ref.shape[1]
    steps = rows // block
    shape = (block // imgs, imgs, D)
    wide = near_ref.shape[0]

    def spot(i):
        return pl.ds(pl.multiple_of(i * block, block), block)

    def enter(i):
        s = i % 2
        pairs = ((p_hbm, p_ref), (unit_hbm, unit_ref), (inv_hbm, inv_ref))
        return [dma(a.at[spot(i), :], b.at[s], sem.at[k, s]) for k, (a, b) in enumerate(pairs)]

    def leave(i):
        return dma(conv_ref.at[i % 2], conv_hbm.at[spot(i), :], sem.at[3, i % 2])

    loads = [dma(near_hbm.at[:, pl.ds(0, D)], near_ref, wsem.at[0]), dma(far_hbm.at[:, pl.ds(0, D)], far_ref, wsem.at[1]), dma(small_hbm, small_ref, wsem.at[2])]
    start(loads)
    start(enter(0))
    sums_ref[...] = jnp.zeros(sums_ref.shape, F32)
    wait(loads)
    gain = small_ref[GAIN_ONE : GAIN_ONE + 1, :][None]

    def body(i, _):
        s = i % 2

        @pl.when(i + 1 < steps)
        def _():
            start(enter(i + 1))

        @pl.when(i >= 2)
        def _():
            leave(i - 2).wait()

        wait(enter(i))
        back = jnp.dot(p_ref[s, :, :wide], near_ref[...], preferred_element_type=F32)
        back = back + jnp.dot(p_ref[s, :, wide:], far_ref[...], preferred_element_type=F32)
        back = back.reshape(shape)
        unit = unit_ref[s].reshape(shape).astype(F32)
        sums_ref[0] += jnp.sum(back * unit, axis=0)
        sums_ref[1] += jnp.sum(back, axis=0)
        out = norm_back(back, unit, inv_ref[s].reshape(shape[:2] + (1,)), gain)
        sums_ref[2] += jnp.sum(out, axis=0)
        conv_ref[s] = out.reshape(block, D)
        leave(i).start()
        return 0

    lax.fori_loop(0, steps, body, 0)
    for i in range(max(steps - 2, 0), steps):
        leave(i).wait()


def back_one(p, unit, inv, pair, small, imgs, after=(), block=448):
    rows = p.shape[0]
    two = lambda width, dtype: pltpu.VMEM((2, block, width), dtype)
    return kernel_call(
        functools.partial(back_one_kernel, block),
        [far((rows, D), F32), near((3, imgs, D), F32)],
        [HBM] * 6,
        [pltpu.VMEM((FF // 2, D), BF16)] * 2
        + [pltpu.VMEM(small.shape, F32), two(FF, BF16), two(D, BF16), two(1, F32), two(D, F32)]
        + [pltpu.SemaphoreType.DMA((4, 2)), pltpu.SemaphoreType.DMA((3,))],
        (p, unit, inv, *pair, small),
        after,
        10,
        24,
    )


def taps_kernel(groups, conv_hbm, mixed_hbm, *rest):
    g_ref, conv_ref, mixed_ref, sem = rest[-4:]
    side, _, imgs, _ = conv_hbm.shape

    def enter(k):
        lanes = pl.ds(groups[k] * 128, 128)
        return (
            dma(mixed_hbm.at[:, :, :, lanes], mixed_ref.at[k], sem.at[0, k]),
            dma(conv_hbm.at[:, :, :, lanes], conv_ref.at[k], sem.at[1, k]),
        )

    for k in range(len(groups)):
        start(enter(k))
    for k in range(len(groups)):
        wait(enter(k))

        def per_ky(ky, _):
            first = jnp.maximum(3 - ky, 0)
            last = jnp.minimum(side, side + 3 - ky)

            def row(h, acc):
                acc = list(acc)
                for t in range(imgs // 8):
                    at = pl.ds(t * 8, 8)
                    x = [mixed_ref[k, h + ky - 3, w, at] for w in range(side)]
                    for w in range(side):
                        d = conv_ref[k, h, w, at]
                        for kx in range(7):
                            if 0 <= w + kx - 3 < side:
                                acc[kx] = acc[kx] + x[w + kx - 3] * d
                return tuple(acc)

            acc = lax.fori_loop(first, last, row, (jnp.zeros((8, 128), F32),) * 7)
            for kx in range(7):
                g_ref[ky * 7 + kx, :, pl.ds(k * 128, 128)] = jnp.sum(acc[kx], axis=0, keepdims=True)
            return 0

        lax.fori_loop(0, 7, per_ky, 0)


def taps_grad(conv, mixed, groups, after=()):
    lanes = pltpu.VMEM((len(groups),) + conv.shape[:3] + (128,), F32)
    return kernel_call(
        functools.partial(taps_kernel, groups),
        [near((49, 1, 128 * len(groups)), F32)],
        [HBM] * 2,
        [lanes, lanes, pltpu.SemaphoreType.DMA((2, len(groups)))],
        (conv, mixed),
        after,
        4.7 * len(groups),
        20,
    )[0]


def images_kernel(begin, end, conv_hbm, small_hbm, mix_ref, sel_ref, res_hbm, *rest):
    g_hbm, small_ref, conv_ref, taps, res_ref, out_ref, sem, csem = rest[-8:]
    side, _, imgs, _ = conv_hbm.shape
    low = max(begin - 3, 0)
    high = min(end + 3, side)
    load = dma(small_hbm, small_ref, csem.at[side])
    load.start()

    def bring(h):
        return dma(conv_hbm.at[h], conv_ref.at[h], csem.at[h])

    def enter(h):
        return dma(res_hbm.at[h], res_ref.at[h % 2], sem.at[0, h % 2])

    def leave(h):
        return dma(out_ref.at[h % 2], g_hbm.at[h], sem.at[1, h % 2])

    for h in range(low, high):
        bring(h).start()
        if h == min(begin + 3, high - 1):
            enter(begin).start()
    load.wait()
    for t in range(49):
        taps[t] = jnp.broadcast_to(small_ref[t : t + 1, :], (8, D))
    mix = mix_ref[...][None]
    others = 1.0 - mix
    for h in range(low, min(begin + 3, high)):
        bring(h).wait()

    def row(h, _):
        s = h % 2

        @pl.when(h + 1 < end)
        def _():
            enter(h + 1).start()

        @pl.when(h + 3 < high)
        def _():
            bring(h + 3).wait()

        @pl.when(h >= begin + 2)
        def _():
            leave(h - 2).wait()

        enter(h).wait()
        for t in range(imgs // 8):
            at = pl.ds(t * 8, 8)
            for g in range(D // 128):
                lanes = pl.ds(g * 128, 128)
                base = [res_ref[s, w, at, lanes] for w in range(side)]
                acc = conv_rows(conv_ref, taps, h, at, lanes, side, base, True)
                for w in range(side):
                    out_ref[s, w, at, lanes] = acc[w]
        v = out_ref[s]
        part = (others * v).reshape(side * imgs, D)
        upper = part.astype(BF16)
        lower = (part - upper.astype(F32)).astype(BF16)
        back = jnp.dot(sel_ref[...], upper, preferred_element_type=F32)
        back = back + jnp.dot(sel_ref[...], lower, preferred_element_type=F32)
        out_ref[s] = mix * v + back.reshape(side, imgs, D)
        leave(h).start()
        return 0

    lax.fori_loop(begin, end, row, 0)
    for h in range(end - 2, end):
        leave(h).wait()


def images_back(conv, small, mix, sel, res, begin, end, so_far=(), after=()):
    side, _, imgs, _ = conv.shape
    return kernel_call(
        functools.partial(images_kernel, begin, end),
        [far(conv.shape, F32)],
        [HBM, HBM, VMEM, VMEM, HBM] + [HBM] * len(so_far),
        [
            pltpu.VMEM(small.shape, F32),
            pltpu.VMEM(conv.shape, F32),
            pltpu.VMEM((49, 8, D), F32),
            pltpu.VMEM((2, side, imgs, D), F32),
            pltpu.VMEM((2, side, imgs, D), F32),
            pltpu.SemaphoreType.DMA((2, 2)),
            pltpu.SemaphoreType.DMA((side + 1,)),
        ],
        (conv, small, mix, sel, res) + tuple(so_far),
        after,
        22 * (end - begin) / side,
        16,
        {5: 0} if so_far else {},
    )[0]


def join_kernel(first_ref, second_ref, *rest):
    out_ref = rest[-1]
    k = first_ref.shape[0]
    out_ref[:k] = first_ref[...]
    out_ref[k:] = second_ref[...]


def join(first, second, after=()):
    return kernel_call(
        join_kernel,
        [near((2 * first.shape[0],) + first.shape[1:], first.dtype)],
        [VMEM] * 2,
        [],
        (first, second),
        after,
        0.5,
        8,
    )[0]


def fold_kernel(keep_ref, come_ref, *rest):
    stay_ref, leave_ref = rest[-2:]
    k = stay_ref.shape[0]
    stay_ref[...] = keep_ref[:k].astype(F32) + come_ref[:k].astype(F32)
    leave_ref[...] = (keep_ref[k:].astype(F32) + come_ref[k:].astype(F32)).astype(BF16)


def last_kernel(keep_ref, come_ref, *rest):
    sum_ref, square_ref = rest[-2:]
    total = keep_ref[...].astype(F32) + come_ref[...].astype(F32)
    sum_ref[...] = total
    square_ref[...] = jnp.sum(total[0] * total[0], axis=0, keepdims=True)


def fold(keep, come, after=()):
    slots = keep.shape[0]
    rest = keep.shape[1:]
    if slots == 1:
        body = last_kernel
        out = [near(keep.shape, F32), near((1, rest[1]), F32)]
    else:
        body = fold_kernel
        out = [near((slots // 2,) + rest, F32), near((slots // 2,) + rest, BF16)]
    return kernel_call(body, out, [VMEM] * 2, [], (keep, come), after, 0.5, 12)


def swap(x, bit, n):
    return lax.ppermute(x, "dp", [(i, i ^ bit) for i in range(n)])


def is_set(bit):
    return (lax.axis_index("dp") & bit) != 0


def gather_natural(shard, n, order):
    have = shard
    met = []
    for bit in order:
        other = swap(have, bit, n)
        axis = sum(1 for b in met if b > bit)
        mine = is_set(bit)
        have = jnp.stack([jnp.where(mine, other, have), jnp.where(mine, have, other)], axis=axis)
        met.append(bit)
    return have.reshape((n,) + shard.shape)


def scatter_natural(total, n, order):
    left = sorted(order, reverse=True)
    have = total.reshape((2,) * len(left) + total.shape[1:])
    for bit in order:
        axis = left.index(bit)
        mine = is_set(bit).astype(jnp.int32)
        keep = lax.dynamic_index_in_dim(have, mine, axis, keepdims=False)
        send = lax.dynamic_index_in_dim(have, 1 - mine, axis, keepdims=False)
        have = keep.astype(F32) + swap(send.astype(BF16), bit, n).astype(F32)
        left.remove(bit)
    return have


def masks_of(n, order):
    masks = np.zeros(n, np.int32)
    for k, bit in enumerate(order):
        masks += ((np.arange(n, dtype=np.int32) >> k) & 1) * bit
    return masks


def adamw_step(weight, first_mom, second, gradient, step_rate, decay_rate):
    first_mom = BETA_ONE * first_mom + (1.0 - BETA_ONE) * gradient
    second = BETA_TWO * second + (1.0 - BETA_TWO) * gradient * gradient
    first_hat = first_mom / (1.0 - BETA_ONE**STEP)
    second_hat = second / (1.0 - BETA_TWO**STEP)
    weight = weight - step_rate * (first_hat / (jnp.sqrt(second_hat) + ADAM_EPS) + decay_rate * weight)
    return (first_mom, second, weight)


def local(n, images, mix_weight, partner, keep_mask, cotangent, weight_in, weight_out, weight_down, small_params,
          first_in, second_in, first_out, second_out, first_down, second_down, first_small, second_small):
    imgs, side = images.shape[:2]
    half = side // 2
    pixels = side * side * imgs
    me = lax.axis_index("dp")
    bits = [1 << k for k in range(n.bit_length() - 1)]
    deep = FF // n
    aligned = deep % 16 == 0
    p_order = bits[::-1]
    w_order = bits[:2:-1] + [2, 4, 1]
    p_masks = masks_of(n, p_order)
    w_masks = masks_of(n, w_order)

    small = small_params.astype(BF16)
    pair = jnp.concatenate([weight_in, weight_out], axis=1).astype(BF16)[None]
    down = weight_down.astype(BF16)[None]
    small = gather_natural(small, n, bits[1:] + bits[:1]).reshape(-1, D).astype(F32)
    hb = jnp.take(small[HIDDEN_BIAS:OUT_BIAS].reshape(n, deep), me ^ p_masks, axis=0).reshape(1, FF)
    db = small[DOWN_BIAS:].reshape(1, 2 * D)
    spot = jnp.arange(side * imgs, dtype=jnp.int32)
    target = jnp.tile(partner - me * imgs, side) + (spot // imgs) * imgs
    sel = (target[:, None] == spot[None, :]).astype(BF16)
    selt = (target[None, :] == spot[:, None]).astype(BF16)
    mix = jnp.broadcast_to(mix_weight[:, None], (imgs, D))
    keep = jnp.broadcast_to((keep_mask.astype(F32) / (1.0 - DROP_RATE))[:, None], (imgs, D))

    img = images.transpose(1, 2, 0, 3)
    dy = cotangent.transpose(1, 2, 0, 3)
    flat = lambda a: a.reshape(pixels, a.shape[-1])
    paired = lambda a: a.reshape(half, 2, half, 2, imgs, a.shape[-1])
    square = lambda a: a.reshape(side, side, imgs, a.shape[-1])
    def grow(have, order, hop, after=()):
        return join(have, swap(have, order[hop], n), after)

    last = len(bits) - 1
    for hop in range(last - 1):
        pair = grow(pair, p_order, hop)
    for hop in range(last - 2):
        down = grow(down, w_order, hop)
    mixed, *first = conv_forward(small, (img, sel, mix), 0, half)
    pair = grow(pair, p_order, last - 1, first[2:3])
    down = grow(down, w_order, last - 2, first[2:3])
    unit1, inv1, norm1 = conv_forward(small, (mixed,), half, side, tuple(first), (pair, down))
    pair = tuple(x.reshape(FF // 2, 2 * D) for x in (pair, swap(pair, 1, n)))
    act, dg, branch, unit2, inv2, norm2 = hidden_forward(flat(norm1), flat(mixed), pair, small, hb, keep)
    down = grow(down, w_order, last - 1, (norm2,))
    far_down = swap(down, 1, n)
    if aligned:
        origin = me ^ w_masks
        down = tuple(x.reshape(2 * D, 2 * D) for x in (down, far_down))
    else:
        origin = jnp.arange(32, dtype=jnp.int32)
        down = jnp.take(jnp.concatenate([down, far_down]), jnp.asarray(np.argsort(w_masks))[me ^ np.arange(n, dtype=np.int32)], axis=0)
        down = down.reshape(2, 2 * D, 2 * D)

    gd_near, gd_far, gdb = grad_down(origin, paired(norm2), dy, (down[0],))
    out, bb, sums2, res = down_both(
        origin, paired(norm2), paired(unit2), paired(inv2), paired(branch), down, dy, small, keep, db, (gd_near,)
    )
    shards = (n // 2, deep, 2 * D)
    if aligned:
        d_keep = gd_near.reshape(shards)
        d_come = swap(gd_far.reshape(shards), 1, n)
        d_keep, d_send = fold(d_keep, d_come, (bb,))
        d_come = swap(d_send, w_order[-2], n)
    g_near, g_far, ghb, p = pair_grad(flat(bb), act, dg, flat(norm1), pair, imgs, (d_send,) if aligned else ())
    p_keep = g_near.reshape(shards)
    p_come = swap(g_far.reshape(shards), 1, n)
    gate = ()
    if aligned:
        d_keep, d_send = fold(d_keep, d_come, (g_near,))
        d_come = swap(d_send, w_order[-3], n)
        gate = (d_send,)
    back_conv, sums1 = back_one(p, flat(unit1), flat(inv1), pair, small, imgs, gate)
    back_conv = square(back_conv)
    p_keep, p_send = fold(p_keep, p_come, (sums1,))
    p_come = swap(p_send, p_order[-2], n)
    gate = (p_send,)
    if aligned:
        d_keep, d_send = fold(d_keep, d_come, (sums1,))
        d_come = swap(d_send, w_order[-4], n)
        gate = (p_send, d_send)
    part = images_back(back_conv, small, mix, selt, square(res), 0, half, (), gate)
    p_keep, p_send = fold(p_keep, p_come, (part,))
    p_come = swap(p_send, p_order[-3], n)
    gate = (p_send,)
    if aligned:
        d_keep, d_send = fold(d_keep, d_come, (part,))
        d_come = swap(d_send, w_order[-5], n)
        gate = (p_send, d_send)
    images_grad = images_back(back_conv, small, mix, selt, square(res), half, side, (part,), gate)
    p_keep, p_send = fold(p_keep, p_come, (images_grad,))
    p_come = swap(p_send, p_order[-4], n)
    gate = (p_send,)
    if aligned:
        gd, gd_squares = fold(d_keep, d_come, (images_grad,))
        gate = (p_send, gd)
    gk1 = taps_grad(back_conv, mixed, (0, 1), gate)
    p_keep, p_send = fold(p_keep, p_come, (gk1,))
    p_come = swap(p_send, p_order[-5], n)
    gk2 = taps_grad(back_conv, mixed, (2,), (p_send,))
    for bit in p_order[-6::-1]:
        p_keep, p_send = fold(p_keep, p_come)
        p_come = swap(p_send, bit, n)
    gp, gp_squares = fold(p_keep, p_come, (gk2,))
    if not aligned:
        gd = jnp.concatenate([gd_near, gd_far]).reshape(n, deep, 2 * D)
        gd = scatter_natural(gd, n, w_order[::-1])[None]
        gd_squares = jnp.sum(gd[0] * gd[0], axis=0, keepdims=True)
    gd = gd[0]
    gi, go = gp[0, :, :D], gp[0, :, D:]

    one = jnp.sum(sums1, axis=1)
    two = jnp.sum(sums2, axis=1)
    ghb = jnp.take(jnp.sum(ghb, axis=0).reshape(n, deep), jnp.asarray(p_masks)[me ^ np.arange(n, dtype=np.int32)], axis=0)
    total = jnp.concatenate(
        [
            jnp.concatenate([gk1, gk2], axis=2).reshape(49, D),
            one[2:3],
            one[0:2],
            ghb.reshape(4, D),
            two[3:4],
            two[2:3],
            two[0:2],
            jnp.sum(gdb, axis=0).reshape(2, D),
            (gp_squares + gd_squares).reshape(2, D),
        ],
        axis=0,
    )
    for bit in p_order:
        total = total + swap(total, bit, n)
    used = DOWN_BIAS + 2
    gs = total[:used]
    grad_norm = jnp.sqrt(jnp.sum(gs * gs) + jnp.sum(total[used:]))
    factor = CLIP_NORM / jnp.maximum(grad_norm, CLIP_NORM)
    shard_len = small_params.shape[0]
    gs = lax.dynamic_slice_in_dim(gs.reshape(-1), me * shard_len, shard_len)
    position = me * shard_len + jnp.arange(shard_len, dtype=jnp.int32)
    small_rate = jnp.where(position < 54 * D + FF, LAYER_DECAY * RATE_VECTOR, RATE_VECTOR)
    small_decay = jnp.where(position < 49 * D, WEIGHT_DECAY, 0.0)
    new_in = adamw_step(weight_in, first_in, second_in, gi * factor, LAYER_DECAY * RATE_MATRIX, WEIGHT_DECAY)
    new_out = adamw_step(weight_out, first_out, second_out, go * factor, LAYER_DECAY * RATE_MATRIX, WEIGHT_DECAY)
    new_down = adamw_step(weight_down, first_down, second_down, gd * factor, RATE_MATRIX, WEIGHT_DECAY)
    new_small = adamw_step(small_params, first_small, second_small, gs * factor, small_rate, small_decay)
    return (
        out.transpose(2, 0, 1, 3),
        images_grad.transpose(2, 0, 1, 3),
        grad_norm,
        *new_in,
        *new_out,
        *new_down,
        *new_small,
    )


def solution(mesh):
    four = P("dp", None, None, None)
    two = P("dp", None)
    one = P("dp")
    return jax.shard_map(
        functools.partial(local, mesh.shape["dp"]),
        mesh=mesh,
        in_specs=(four, one, one, one, four, two, two, two, one) + (two,) * 6 + (one,) * 2,
        out_specs=(four, four, P()) + (two,) * 9 + (one,) * 3,
        check_vma=False,
    )
```

time: 350 us -> 248 us (0.71)
  waiting for transfers between devices: 82.9 us -> 33.4 us
  local copies, waits for them, and re-layouts: 55.4 us -> 13.1 us
  Pallas kernels: 131 us -> 152 us
  between operations: 21.7 us -> 4.03 us
  other arithmetic: 18.4 us -> 9.64 us
  starting transfers between devices: 40.6 us -> 35.5 us
    ppermute x35 -> x30, waiting for transfers between devices: 82.9 us -> 33.4 us  [swap(): return lax.ppermute(x, 'dp', [(i, i ^ bit) for i in range(n)])]
    unnamed x101 -> x81, local copies, waits for them, and re-layouts: 37.6 us -> 8.34 us
    pallas_call x7 -> x29, Pallas kernels: 131 us -> 152 us  [kernel_call(): pl.pallas_call(body, out_shape=tuple(out), in_specs=specs, out_specs=tupl...]
    reshape x3 -> x6, local copies, waits for them, and re-layouts: 7.29 us -> 0.34 us  [the longest x1 0.08 us: local(): jnp.take(small[HIDDEN_BIAS:OUT_BIAS].reshape(n, deep), me ^ p_masks, axis=0)]
    another operation x20 -> x8, other arithmetic: 6.02 us -> 0.23 us  [gather_natural(): jnp.stack([jnp.where(mine, other, have), jnp.where(mine, have, other)], a...]
    another operation x7 -> x4, local copies, waits for them, and re-layouts: 5.68 us -> 0.1 us  [the longest x2 0.09 us: local(): target = jnp.tile(partner - me * imgs, side) + spot // imgs * imgs]
    ppermute x35 -> x30, starting transfers between devices: 40.5 us -> 35.5 us  [swap(): return lax.ppermute(x, 'dp', [(i, i ^ bit) for i in range(n)])]
  transfers between devices with their start and end apart: 36 -> 30, of which waited for: 22 -> 12; matrix products, arithmetic and copies ran while one was open for 7% -> 4% of each run, Pallas kernels for 23% -> 58%
where the time goes in v2:
time: 248 us; the launch traced here: 247 us
  Pallas kernels  152 us (61%)
  starting transfers between devices  35.5 us (14%)
  waiting for transfers between devices  33.4 us (13%)
  local copies, waits for them, and re-layouts  13.1 us (5%)
  other arithmetic  9.64 us (4%)
  between operations  4.03 us (2%)
    pallas_call x29, Pallas kernels, kernel_call(): pl.pallas_call(body, out_shape=tuple(out), in_specs=specs, out_specs=tupl...  152 us
    ppermute x30, starting transfers between devices, swap(): return lax.ppermute(x, 'dp', [(i, i ^ bit) for i in range(n)])  35.5 us
    ppermute x30, waiting for transfers between devices, swap(): return lax.ppermute(x, 'dp', [(i, i ^ bit) for i in range(n)])  33.4 us
    unnamed x81, local copies, waits for them, and re-layouts  8.34 us
  transfers between devices with their start and end apart: 30, of which 12 were waited for; matrix products, arithmetic and copies ran while one was open for 4% of the time, Pallas kernels for 58%

profile of v2, /device:TPU:0, one launch (start us, length us, event | category | flops | bytes accessed | tf_op | source)
XLA Modules:
  0.0 247.3 jit_solution(8800218249897213433)
XLA Ops:
  1.3 2.9 %collective-permute-start = (bf16[744]{0:T(1024)(128)(2,1)S(1)}, bf16[744]{0:T(1024)(128)(2,1)S(1)}, u32[]{:S(2)}, u32[]{:S(2)}) collective-permute-start(bf16[744]{0:T(1024)(128)(2,1)S(1)} %convert_element_type.28), channel_id=1, source_target_pairs={{0,2},{1,3},{2,0},{3,1},{4,6},{5,7},{6,4},{7,5},{8,10},{9,11},{10,... | collective-permute-start | bytes 4472 | tf_op jit(solution)/shard_map/ppermute | solution.py:789
  4.3 0.9 convert_bitcast_fusion.1
  5.2 2.7 %collective-permute-start.5 = (bf16[1,48,768]{2,1,0:T(8,128)(2,1)S(1)}, bf16[1,48,768]{2,1,0:T(8,128)(2,1)S(1)}, u32[]{:S(2)}, u32[]{:S(2)}) collective-permute-start(bf16[1,48,768]{2,1,0:T(8,128)(2,1)S(1)} %pad_maximum_fusion.1.first_ref), channel_id=1, source_target_pairs={{0,16},{1,17},{2,18},{3,19},{4,20},{5,21},{6,22},{7,23},{8,24},{9,... | collective-permute-start | bytes 221192 | tf_op jit(solution)/shard_map/ppermute | solution.py:789
  7.9 0.9 convert_bitcast_fusion.first_ref
  9.9 1.4 gather_fusion
  12.9 1.6 collective-permute-start.1
  15.1 1.4 collective-permute-done.1
  16.6 1.6 collective-permute-start.2
  18.2 2.0 collective-permute-done.2
  20.3 2.7 %collective-permute-start.3 = (bf16[2,2,2,744]{3,2,1,0:T(2,128)(2,1)S(1)}, bf16[2,2,2,744]{3,2,1,0:T(2,128)(2,1)S(1)}, u32[]{:S(2)}, u32[]{:S(2)}) collective-permute-start(bf16[2,2,2,744]{3,2,1,0:T(2,128)(2,1)S(1)} %pad_maximum_fusion.3), channel_id=1, source_target_pairs={{0,16},{1,17},{2,18},{3,19},{4,20},{5,21},{6,22},{7,23},{8,24},{9,... | collective-permute-start | bytes 35720 | tf_op jit(solution)/shard_map/ppermute | solution.py:789
  23.0 2.0 collective-permute-done.3
  25.1 1.6 collective-permute-start.6
  27.4 3.4 %collective-permute-done.6.second_ref = bf16[2,48,768]{2,1,0:T(8,128)(2,1)S(1)} collective-permute-done((bf16[2,48,768]{2,1,0:T(8,128)(2,1)S(1)}, bf16[2,48,768]{2,1,0:T(8,128)(2,1)S(1)}, u32[]{:S(2)}, u32[]{:S(2)}) %collective-permute-start.6) | collective-permute-done | bytes 147488 | tf_op jit(solution)/shard_map/ppermute | solution.py:789
  30.8 1.6 collective-permute-start.7
  34.1 3.5 %collective-permute-done.7.second_ref = bf16[4,48,768]{2,1,0:T(8,128)(2,1)S(1)} collective-permute-done((bf16[4,48,768]{2,1,0:T(8,128)(2,1)S(1)}, bf16[4,48,768]{2,1,0:T(8,128)(2,1)S(1)}, u32[]{:S(2)}, u32[]{:S(2)}) %collective-permute-start.7) | collective-permute-done | bytes 294944 | tf_op jit(solution)/shard_map/ppermute | solution.py:789
  38.5 14.7 %shard_map.307 = (f32[14,14,16,384]{3,2,1,0:T(8,128)}, bf16[14,14,16,384]{3,2,1,0:T(8,128)(2,1)}, f32[14,14,16,1]{3,2,1,0:T(8,128)}, bf16[14,14,16,384]{3,2,1,0:T(8,128)(2,1)}) custom-call(f32[62,384]{1,0:T(8,128)} %reshape.230.refs_0_.small_hbm, bf16[14,14,16,384]{3,2,1,0:T(8,128)(2,1)} %bitcast.90, bf16[224,224]{1,0:T(8,128)(2,1)S(1)} %get-tuple-element.140.refs_2_, ...), custom_call_target="tpu_custom_call" | custom-call | flops 13500000256 | tf_op jit(solution)/shard_map/pallas_call | solution.py:63
  55.3 0.9 shard_map.314.refs_6_.first_ref
  56.3 1.5 collective-permute-start.13
  57.8 12.3 %shard_map.315 = (bf16[14,14,16,384]{3,2,1,0:T(8,128)(2,1)}, f32[14,14,16,1]{3,2,1,0:T(8,128)}, bf16[14,14,16,384]{3,2,1,0:T(8,128)(2,1)}) custom-call(f32[62,384]{1,0:T(8,128)} %reshape.230.refs_0_.small_hbm, f32[14,14,16,384]{3,2,1,0:T(8,128)} %get-tuple-element.62.refs_1_.mixed_hbm, ...), custom_call_target="tpu_custom_call", output_to_operand_aliasing={{0}: (2, {}), {1}: (3, {}), {2}: (4, {})} | custom-call | flops 10499999744 | tf_op jit(solution)/shard_map/pallas_call | solution.py:63
  70.2 0.9 copy-done.37
  71.1 20.0 %shard_map.316 = (bf16[3136,1536]{1,0:T(8,128)(2,1)}, bf16[3136,1536]{1,0:T(8,128)(2,1)}, bf16[3136,384]{1,0:T(8,128)(2,1)}, bf16[3136,384]{1,0:T(8,128)(2,1)}, ...) custom-call(bf16[3136,384]{1,0:T(8,128)(2,1)} %bitcast.84, f32[3136,384]{1,0:T(8,128)} %bitcast.96, ...), custom_call_target="tpu_custom_call" | custom-call | flops 16999999488 | tf_op jit(solution)/shard_map/pallas_call | solution.py:63
  91.2 1.1 shard_map.317
  93.3 7.7 %shard_map.318 = (bf16[768,768]{1,0:T(8,128)(2,1)S(1)}, bf16[768,768]{1,0:T(8,128)(2,1)S(1)}, f32[16,768]{1,0:T(8,128)S(1)}) custom-call(s32[32]{0:T(128)S(1)} %broadcast_xor_fusion.origin_ref, bf16[7,2,7,2,16,384]{5,4,3,2,1,0:T(8,128)(2,1)} %bitcast.86, bf16[7,7,16,768]{3,2,1,0:T(8,128)(2,1)} %bitcast.91, bf16[768,768]{1,0:T(8,128)(2,1)} %bitcast.77), custom_call_target="tpu_custom_call" | custom-call | flops 8000000000 | tf_op jit(solution)/shard_map/pallas_call | solution.py:63
  101.0 1.0 copy-done.4
  102.4 14.2 %shard_map.319 = (bf16[7,7,16,768]{3,2,1,0:T(8,128)(2,1)}, bf16[7,2,7,2,16,384]{5,4,3,2,1,0:T(8,128)(2,1)}, f32[4,16,384]{2,1,0:T(8,128)S(1)}, f32[7,2,7,2,16,384]{5,4,3,2,1,0:T(8,128)}) custom-call(s32[32]{0:T(128)S(1)} %broadcast_xor_fusion.origin_ref, bf16[7,2,7,2,16,384]{5,4,3,2,1,0:T(8,128)(2,1)} %bitcast.87, bf16[7,2,7,2,16,384]{5,4,3,2,1,0:T(8,128)(2,1)} %bitcast.104, ...), custom_call_target="tpu_custom_call" | custom-call | flops 12999999488 | tf_op jit(solution)/shard_map/pallas_call | solution.py:63
  116.7 1.0 shard_map.320
  118.2 22.5 %shard_map.321 = (bf16[768,768]{1,0:T(8,128)(2,1)S(1)}, bf16[768,768]{1,0:T(8,128)(2,1)S(1)}, f32[16,1536]{1,0:T(8,128)S(1)}, bf16[3136,1536]{1,0:T(8,128)(2,1)}) custom-call(bf16[3136,384]{1,0:T(8,128)(2,1)} %bitcast.88, bf16[3136,1536]{1,0:T(8,128)(2,1)} %get-tuple-element.74.act_hbm, bf16[3136,1536]{1,0:T(8,128)(2,1)} %get-tuple-element.75.dg_hbm, ...), custom_call_target="tpu_custom_call" | custom-call | flops 23000000512 | tf_op jit(solution)/shard_map/pallas_call | solution.py:63
  140.8 1.0 copy-done
  141.8 1.1 copy-done.12
  145.4 0.9 collective-permute-start.18
  146.4 12.5 %shard_map.323 = (f32[3136,384]{1,0:T(8,128)}, f32[3,16,384]{2,1,0:T(8,128)S(1)}) custom-call(bf16[3136,1536]{1,0:T(8,128)(2,1)} %get-tuple-element.78.p_hbm, bf16[3136,384]{1,0:T(8,128)(2,1)} %bitcast.105, f32[3136,1]{1,0:T(8,128)} %bitcast.107, bf16[768,768]{1,0:T(8,128)(2,1)} %bitcast.76, bf16[768,768]{1,0:T(8,128)(2,1)} %bitcast.95, ...), custom_call_target="tpu_custom_call" | custom-call | flops 10000000000 | tf_op jit(solution)/shard_map/pallas_call | solution.py:63
  159.6 2.5 %collective-permute-start.20 = (bf16[2,48,768]{2,1,0:T(8,128)(2,1)S(1)}, bf16[2,48,768]{2,1,0:T(8,128)(2,1)S(1)}, u32[]{:S(2)}, u32[]{:S(2)}) collective-permute-start(bf16[2,48,768]{2,1,0:T(8,128)(2,1)S(1)} %get-tuple-element.90.rest_1_), channel_id=1, source_target_pairs={{0,8},{1,9},{2,10},{3,11},{4,12},{5,13},{6,14},{7,15},{8,0},{9,1},... | collective-permute-start | bytes 442376 | tf_op jit(solution)/shard_map/ppermute | solution.py:789
  163.3 12.9 %shard_map.326.rest_0_ = f32[14,14,16,384]{3,2,1,0:T(8,128)} custom-call(f32[14,14,16,384]{3,2,1,0:T(8,128)} %bitcast.99, f32[62,384]{1,0:T(8,128)} %reshape.230.refs_0_.small_hbm, f32[16,384]{1,0:T(8,128)S(1)} %broadcast_in_dim.46.refs_3_.mix_ref, bf16[224,224]{1,0:T(8,128)(2,1)S(1)} %get-tuple-element.139.sel_ref, f32[14,14,16,384]{3,2,1,0:T(8,128)} %bitcast.97, ...), custom_call_target="tpu_custom_call" | custom-call | flops 11000000512 | tf_op jit(solution)/shard_map/pallas_call | solution.py:63
  176.3 2.6 %collective-permute-start.22 = (bf16[1,48,768]{2,1,0:T(8,128)(2,1)S(1)}, bf16[1,48,768]{2,1,0:T(8,128)(2,1)S(1)}, u32[]{:S(2)}, u32[]{:S(2)}) collective-permute-start(bf16[1,48,768]{2,1,0:T(8,128)(2,1)S(1)} %get-tuple-element.94.rest_2_), channel_id=1, source_target_pairs={{0,16},{1,17},{2,18},{3,19},{4,20},{5,21},{6,22},{7,23},{8,24},{9,... | collective-permute-start | bytes 221192 | tf_op jit(solution)/shard_map/ppermute | solution.py:789
  179.0 1.6 collective-permute-start.21
  180.6 12.9 %shard_map.329.rest_0_ = f32[14,14,16,384]{3,2,1,0:T(8,128)} custom-call(f32[14,14,16,384]{3,2,1,0:T(8,128)} %bitcast.100, f32[62,384]{1,0:T(8,128)} %reshape.230.refs_0_.small_hbm, f32[16,384]{1,0:T(8,128)S(1)} %broadcast_in_dim.46.refs_3_.mix_ref, bf16[224,224]{1,0:T(8,128)(2,1)S(1)} %get-tuple-element.139.sel_ref, ...), custom_call_target="tpu_custom_call", output_to_operand_aliasing={{}: (5, {})} | custom-call | flops 11000000512 | tf_op jit(solution)/shard_map/pallas_call | solution.py:63
  194.9 10.7 %shard_map.332.rest_0_ = f32[49,1,256]{2,1,0:T(1,128)S(1)} custom-call(f32[14,14,16,384]{3,2,1,0:T(8,128)} %bitcast.101, f32[14,14,16,384]{3,2,1,0:T(8,128)} %get-tuple-element.62.refs_1_.mixed_hbm, bf16[2,48,768]{2,1,0:T(8,128)(2,1)} %copy-done.18, f32[1,48,768]{2,1,0:T(8,128)} %copy-done.7), custom_call_target="tpu_custom_call" | custom-call | flops 9400000512 | tf_op jit(solution)/shard_map/pallas_call | solution.py:63
  207.0 6.4 %shard_map.334.rest_0_ = f32[49,1,128]{2,1,0:T(1,128)S(1)} custom-call(f32[14,14,16,384]{3,2,1,0:T(8,128)} %bitcast.102, f32[14,14,16,384]{3,2,1,0:T(8,128)} %get-tuple-element.62.refs_1_.mixed_hbm, bf16[1,48,768]{2,1,0:T(8,128)(2,1)} %copy-done.20), custom_call_target="tpu_custom_call" | custom-call | flops 4700000256 | tf_op jit(solution)/shard_map/pallas_call | solution.py:63
  213.4 1.6 collective-permute-start.24
  215.1 3.7 %collective-permute-done.24.come_ref = bf16[1,48,768]{2,1,0:T(8,128)(2,1)S(1)} collective-permute-done((bf16[1,48,768]{2,1,0:T(8,128)(2,1)S(1)}, bf16[1,48,768]{2,1,0:T(8,128)(2,1)S(1)}, u32[]{:S(2)}, u32[]{:S(2)}) %collective-permute-start.24) | collective-permute-done | bytes 73760 | tf_op jit(solution)/shard_map/ppermute | solution.py:789
  219.0 1.7 collective-permute-start.25
  220.6 5.0 %collective-permute-done.25 = f32[64,384]{1,0:T(8,128)S(1)} collective-permute-done((f32[64,384]{1,0:T(8,128)S(1)}, f32[64,384]{1,0:T(8,128)S(1)}, u32[]{:S(2)}, u32[]{:S(2)}) %collective-permute-start.25) | collective-permute-done | bytes 98336 | tf_op jit(solution)/shard_map/ppermute | solution.py:789
  226.1 4.2 %collective-permute-done.26 = f32[64,384]{1,0:T(8,128)S(1)} collective-permute-done((f32[64,384]{1,0:T(8,128)S(1)}, f32[64,384]{1,0:T(8,128)S(1)}, u32[]{:S(2)}, u32[]{:S(2)}) %collective-permute-start.26) | collective-permute-done | bytes 98336 | tf_op jit(solution)/shard_map/ppermute | solution.py:789
  230.3 1.6 collective-permute-start.27
  231.9 3.1 %collective-permute-done.27 = f32[64,384]{1,0:T(8,128)S(1)} collective-permute-done((f32[64,384]{1,0:T(8,128)S(1)}, f32[64,384]{1,0:T(8,128)S(1)}, u32[]{:S(2)}, u32[]{:S(2)}) %collective-permute-start.27) | collective-permute-done | bytes 98336 | tf_op jit(solution)/shard_map/ppermute | solution.py:789
  235.0 1.3 collective-permute-start.28
  236.3 3.3 %collective-permute-done.28 = f32[64,384]{1,0:T(8,128)S(1)} collective-permute-done((f32[64,384]{1,0:T(8,128)S(1)}, f32[64,384]{1,0:T(8,128)S(1)}, u32[]{:S(2)}, u32[]{:S(2)}) %collective-permute-start.28) | collective-permute-done | bytes 98336 | tf_op jit(solution)/shard_map/ppermute | solution.py:789
  239.8 1.3 collective-permute-done.29
  (192 shorter events, 23.0 us)
Async XLA Ops:
  1.3 10.8 %collective-permute-start = (bf16[744]{0:T(1024)(128)(2,1)S(1)}, bf16[744]{0:T(1024)(128)(2,1)S(1)}, u32[]{:S(2)}, u32[]{:S(2)}) collective-permute-start(bf16[744]{0:T(1024)(128)(2,1)S(1)} %convert_element_type.28), channel_id=1, source_target_pairs={{0,2},{1,3},{2,0},{3,1},{4,6},{5,7},{6,4},{7,5},{8,10},{9,11},{10,... | collective-permute-start | bytes 4472 | tf_op jit(solution)/shard_map/ppermute | solution.py:789
  5.2 19.9 %collective-permute-start.5 = (bf16[1,48,768]{2,1,0:T(8,128)(2,1)S(1)}, bf16[1,48,768]{2,1,0:T(8,128)(2,1)S(1)}, u32[]{:S(2)}, u32[]{:S(2)}) collective-permute-start(bf16[1,48,768]{2,1,0:T(8,128)(2,1)S(1)} %pad_maximum_fusion.1.first_ref), channel_id=1, source_target_pairs={{0,16},{1,17},{2,18},{3,19},{4,20},{5,21},{6,22},{7,23},{8,24},{9,... | collective-permute-start | bytes 221192 | tf_op jit(solution)/shard_map/ppermute | solution.py:789
  8.8 18.1 %collective-permute-start.9 = (bf16[1,48,768]{2,1,0:T(8,128)(2,1)S(1)}, bf16[1,48,768]{2,1,0:T(8,128)(2,1)S(1)}, u32[]{:S(2)}, u32[]{:S(2)}) collective-permute-start(bf16[1,48,768]{2,1,0:T(8,128)(2,1)S(1)} %convert_bitcast_fusion.first_ref), channel_id=1, source_target_pairs={{0,16},{1,17},{2,18},{3,19},{4,20},{5,21},{6,22},{7,23},{8,24},{9,... | collective-permute-start | bytes 221192 | tf_op jit(solution)/shard_map/ppermute | solution.py:789
  12.9 3.7 %collective-permute-start.1 = (bf16[2,744]{1,0:T(2,128)(2,1)S(1)}, bf16[2,744]{1,0:T(2,128)(2,1)S(1)}, u32[]{:S(2)}, u32[]{:S(2)}) collective-permute-start(bf16[2,744]{1,0:T(2,128)(2,1)S(1)} %pad_maximum_fusion.5), channel_id=1, source_target_pairs={{0,4},{1,5},{2,6},{3,7},{4,0},{5,1},{6,2},{7,3},{8,12},{9,13},{10,... | collective-permute-start | bytes 8936 | tf_op jit(solution)/shard_map/ppermute | solution.py:789
  16.6 3.7 %collective-permute-start.2 = (bf16[2,2,744]{2,1,0:T(2,128)(2,1)S(1)}, bf16[2,2,744]{2,1,0:T(2,128)(2,1)S(1)}, u32[]{:S(2)}, u32[]{:S(2)}) collective-permute-start(bf16[2,2,744]{2,1,0:T(2,128)(2,1)S(1)} %pad_maximum_fusion.4), channel_id=1, source_target_pairs={{0,8},{1,9},{2,10},{3,11},{4,12},{5,13},{6,14},{7,15},{8,0},{9,1},... | collective-permute-start | bytes 17864 | tf_op jit(solution)/shard_map/ppermute | solution.py:789
  20.3 4.7 %collective-permute-start.3 = (bf16[2,2,2,744]{3,2,1,0:T(2,128)(2,1)S(1)}, bf16[2,2,2,744]{3,2,1,0:T(2,128)(2,1)S(1)}, u32[]{:S(2)}, u32[]{:S(2)}) collective-permute-start(bf16[2,2,2,744]{3,2,1,0:T(2,128)(2,1)S(1)} %pad_maximum_fusion.3), channel_id=1, source_target_pairs={{0,16},{1,17},{2,18},{3,19},{4,20},{5,21},{6,22},{7,23},{8,24},{9,... | collective-permute-start | bytes 35720 | tf_op jit(solution)/shard_map/ppermute | solution.py:789
  25.1 5.7 %collective-permute-start.6 = (bf16[2,48,768]{2,1,0:T(8,128)(2,1)S(1)}, bf16[2,48,768]{2,1,0:T(8,128)(2,1)S(1)}, u32[]{:S(2)}, u32[]{:S(2)}) collective-permute-start(bf16[2,48,768]{2,1,0:T(8,128)(2,1)S(1)} %shard_map.308.first_ref), channel_id=1, source_target_pairs={{0,8},{1,9},{2,10},{3,11},{4,12},{5,13},{6,14},{7,15},{8,0},{9,1},... | collective-permute-start | bytes 442376 | tf_op jit(solution)/shard_map/ppermute | solution.py:789
  26.8 5.6 %collective-permute-start.4 = (bf16[2,2,2,2,744]{4,3,2,1,0:T(2,128)(2,1)S(1)}, bf16[2,2,2,2,744]{4,3,2,1,0:T(2,128)(2,1)S(1)}, u32[]{:S(2)}, u32[]{:S(2)}) collective-permute-start(bf16[2,2,2,2,744]{4,3,2,1,0:T(2,128)(2,1)S(1)} %pad_maximum_fusion.2), channel_id=1, source_target_pairs={{0,1},{1,0},{2,3},{3,2},{4,5},{5,4},{6,7},{7,6},{8,9},{9,8},{10,11... | collective-permute-start | bytes 71432 | tf_op jit(solution)/shard_map/ppermute | solution.py:789
  26.9 6.6 %collective-permute-start.10 = (bf16[2,48,768]{2,1,0:T(8,128)(2,1)S(1)}, bf16[2,48,768]{2,1,0:T(8,128)(2,1)S(1)}, u32[]{:S(2)}, u32[]{:S(2)}) collective-permute-start(bf16[2,48,768]{2,1,0:T(8,128)(2,1)S(1)} %shard_map.312.first_ref), channel_id=1, source_target_pairs={{0,8},{1,9},{2,10},{3,11},{4,12},{5,13},{6,14},{7,15},{8,0},{9,1},... | collective-permute-start | bytes 442376 | tf_op jit(solution)/shard_map/ppermute | solution.py:789
  30.8 6.8 %collective-permute-start.7 = (bf16[4,48,768]{2,1,0:T(8,128)(2,1)S(1)}, bf16[4,48,768]{2,1,0:T(8,128)(2,1)S(1)}, u32[]{:S(2)}, u32[]{:S(2)}) collective-permute-start(bf16[4,48,768]{2,1,0:T(8,128)(2,1)S(1)} %shard_map.309.first_ref), channel_id=1, source_target_pairs={{0,4},{1,5},{2,6},{3,7},{4,0},{5,1},{6,2},{7,3},{8,12},{9,13},{10,... | collective-permute-start | bytes 884744 | tf_op jit(solution)/shard_map/ppermute | solution.py:789
  33.5 21.8 %collective-permute-start.11 = (bf16[4,48,768]{2,1,0:T(8,128)(2,1)S(1)}, bf16[4,48,768]{2,1,0:T(8,128)(2,1)S(1)}, u32[]{:S(2)}, u32[]{:S(2)}) collective-permute-start(bf16[4,48,768]{2,1,0:T(8,128)(2,1)S(1)} %shard_map.313.first_ref), channel_id=1, source_target_pairs={{0,2},{1,3},{2,0},{3,1},{4,6},{5,7},{6,4},{7,5},{8,10},{9,11},{10,... | collective-permute-start | bytes 884744 | tf_op jit(solution)/shard_map/ppermute | solution.py:789
  37.7 17.3 %collective-permute-start.8 = (bf16[8,48,768]{2,1,0:T(8,128)(2,1)S(1)}, bf16[8,48,768]{2,1,0:T(8,128)(2,1)S(1)}, u32[]{:S(2)}, u32[]{:S(2)}) collective-permute-start(bf16[8,48,768]{2,1,0:T(8,128)(2,1)S(1)} %shard_map.310.first_ref), channel_id=1, source_target_pairs={{0,2},{1,3},{2,0},{3,1},{4,6},{5,7},{6,4},{7,5},{8,10},{9,11},{10,... | collective-permute-start | bytes 1769480 | tf_op jit(solution)/shard_map/ppermute | solution.py:789
  55.1 15.0 %collective-permute-start.12 = (bf16[16,48,768]{2,1,0:T(8,128)(2,1)S(1)}, bf16[16,48,768]{2,1,0:T(8,128)(2,1)S(1)}, u32[]{:S(2)}, u32[]{:S(2)}) collective-permute-start(bf16[16,48,768]{2,1,0:T(8,128)(2,1)S(1)} %shard_map.311.refs_5_), channel_id=1, source_target_pairs={{0,1},{1,0},{2,3},{3,2},{4,5},{5,4},{6,7},{7,6},{8,9},{9,8},{10,11... | collective-permute-start | bytes 3538952 | tf_op jit(solution)/shard_map/ppermute | solution.py:789
  56.3 34.9 %collective-permute-start.13 = (bf16[8,48,768]{2,1,0:T(8,128)(2,1)}, bf16[8,48,768]{2,1,0:T(8,128)(2,1)S(1)}, u32[]{:S(2)}, u32[]{:S(2)}) collective-permute-start(bf16[8,48,768]{2,1,0:T(8,128)(2,1)} %shard_map.314.refs_6_.first_ref), channel_id=1, source_target_pairs={{0,4},{1,5},{2,6},{3,7},{4,0},{5,1},{6,2},{7,3},{8,12},{9,13},{10,... | collective-permute-start | bytes 1769480 | tf_op jit(solution)/shard_map/ppermute | solution.py:789
  92.3 10.1 %collective-permute-start.14 = (bf16[16,48,768]{2,1,0:T(8,128)(2,1)S(1)}, bf16[16,48,768]{2,1,0:T(8,128)(2,1)}, u32[]{:S(2)}, u32[]{:S(2)}) collective-permute-start(bf16[16,48,768]{2,1,0:T(8,128)(2,1)S(1)} %shard_map.317), channel_id=1, source_target_pairs={{0,1},{1,0},{2,3},{3,2},{4,5},{5,4},{6,7},{7,6},{8,9},{9,8},{10,11... | collective-permute-start | bytes 3538952 | tf_op jit(solution)/shard_map/ppermute | solution.py:789
  102.0 14.6 %collective-permute-start.15 = (bf16[16,48,768]{2,1,0:T(8,128)(2,1)S(1)}, bf16[16,48,768]{2,1,0:T(8,128)(2,1)S(1)}, u32[]{:S(2)}, u32[]{:S(2)}) collective-permute-start(bf16[16,48,768]{2,1,0:T(8,128)(2,1)S(1)} %bitcast.82), channel_id=1, source_target_pairs={{0,1},{1,0},{2,3},{3,2},{4,5},{5,4},{6,7},{7,6},{8,9},{9,8},{10,11... | collective-permute-start | bytes 3538952 | tf_op jit(solution)/shard_map/ppermute | solution.py:789
  102.4 14.3 %copy-start.5 = (bf16[768,768]{1,0:T(8,128)(2,1)S(1)}, bf16[768,768]{1,0:T(8,128)(2,1)}, u32[]{:S(2)}) copy-start(bf16[768,768]{1,0:T(8,128)(2,1)} %copy-done.4) | copy-start | bytes 3538948
  117.7 26.1 %collective-permute-start.16 = (bf16[8,48,768]{2,1,0:T(8,128)(2,1)}, bf16[8,48,768]{2,1,0:T(8,128)(2,1)S(1)}, u32[]{:S(2)}, u32[]{:S(2)}) collective-permute-start(bf16[8,48,768]{2,1,0:T(8,128)(2,1)} %get-tuple-element.77.rest_0_), channel_id=1, source_target_pairs={{0,4},{1,5},{2,6},{3,7},{4,0},{5,1},{6,2},{7,3},{8,12},{9,13},{10,... | collective-permute-start | bytes 1769480 | tf_op jit(solution)/shard_map/ppermute | solution.py:789
  142.9 16.0 %copy-start.32 = (f32[4,384]{1,0:T(4,128)}, f32[4,384]{1,0:T(4,128)S(1)}, u32[]{:S(2)}) copy-start(f32[4,384]{1,0:T(4,128)S(1)} %reduce_sum.56) | copy-start | bytes 18436
  143.7 18.4 %collective-permute-start.17 = (bf16[16,48,768]{2,1,0:T(8,128)(2,1)}, bf16[16,48,768]{2,1,0:T(8,128)(2,1)S(1)}, u32[]{:S(2)}, u32[]{:S(2)}) collective-permute-start(bf16[16,48,768]{2,1,0:T(8,128)(2,1)} %bitcast.81), channel_id=1, source_target_pairs={{0,1},{1,0},{2,3},{3,2},{4,5},{5,4},{6,7},{7,6},{8,9},{9,8},{10,11... | collective-permute-start | bytes 3538952 | tf_op jit(solution)/shard_map/ppermute | solution.py:789
  145.4 13.6 %collective-permute-start.18 = (bf16[4,48,768]{2,1,0:T(8,128)(2,1)}, bf16[4,48,768]{2,1,0:T(8,128)(2,1)S(1)}, u32[]{:S(2)}, u32[]{:S(2)}) collective-permute-start(bf16[4,48,768]{2,1,0:T(8,128)(2,1)} %get-tuple-element.83.rest_0_), channel_id=1, source_target_pairs={{0,2},{1,3},{2,0},{3,1},{4,6},{5,7},{6,4},{7,5},{8,10},{9,11},{10,... | collective-permute-start | bytes 884744 | tf_op jit(solution)/shard_map/ppermute | solution.py:789
  146.4 13.2 %copy-start.14 = (f32[4,48,768]{2,1,0:T(8,128)S(1)}, f32[4,48,768]{2,1,0:T(8,128)}, u32[]{:S(2)}) copy-start(f32[4,48,768]{2,1,0:T(8,128)} %copy-done.13) | copy-start | bytes 1769476
  159.0 17.2 %copy-start.33 = (f32[3,384]{1,0:T(4,128)}, f32[3,384]{1,0:T(4,128)S(1)}, u32[]{:S(2)}) copy-start(f32[3,384]{1,0:T(4,128)S(1)} %reduce_sum.54) | copy-start | bytes 13828
  159.6 16.6 %collective-permute-start.20 = (bf16[2,48,768]{2,1,0:T(8,128)(2,1)S(1)}, bf16[2,48,768]{2,1,0:T(8,128)(2,1)S(1)}, u32[]{:S(2)}, u32[]{:S(2)}) collective-permute-start(bf16[2,48,768]{2,1,0:T(8,128)(2,1)S(1)} %get-tuple-element.90.rest_1_), channel_id=1, source_target_pairs={{0,8},{1,9},{2,10},{3,11},{4,12},{5,13},{6,14},{7,15},{8,0},{9,1},... | collective-permute-start | bytes 442376 | tf_op jit(solution)/shard_map/ppermute | solution.py:789
  162.4 16.5 %collective-permute-start.19 = (bf16[8,48,768]{2,1,0:T(8,128)(2,1)S(1)}, bf16[8,48,768]{2,1,0:T(8,128)(2,1)S(1)}, u32[]{:S(2)}, u32[]{:S(2)}) collective-permute-start(bf16[8,48,768]{2,1,0:T(8,128)(2,1)S(1)} %get-tuple-element.88.rest_0_), channel_id=1, source_target_pairs={{0,2},{1,3},{2,0},{3,1},{4,6},{5,7},{6,4},{7,5},{8,10},{9,11},{10,... | collective-permute-start | bytes 1769480 | tf_op jit(solution)/shard_map/ppermute | solution.py:789
  176.3 17.3 %collective-permute-start.22 = (bf16[1,48,768]{2,1,0:T(8,128)(2,1)S(1)}, bf16[1,48,768]{2,1,0:T(8,128)(2,1)S(1)}, u32[]{:S(2)}, u32[]{:S(2)}) collective-permute-start(bf16[1,48,768]{2,1,0:T(8,128)(2,1)S(1)} %get-tuple-element.94.rest_2_), channel_id=1, source_target_pairs={{0,16},{1,17},{2,18},{3,19},{4,20},{5,21},{6,22},{7,23},{8,24},{9,... | collective-permute-start | bytes 221192 | tf_op jit(solution)/shard_map/ppermute | solution.py:789
  179.0 14.6 %collective-permute-start.21 = (bf16[4,48,768]{2,1,0:T(8,128)(2,1)S(1)}, bf16[4,48,768]{2,1,0:T(8,128)(2,1)S(1)}, u32[]{:S(2)}, u32[]{:S(2)}) collective-permute-start(bf16[4,48,768]{2,1,0:T(8,128)(2,1)S(1)} %get-tuple-element.92.rest_1_), channel_id=1, source_target_pairs={{0,4},{1,5},{2,6},{3,7},{4,0},{5,1},{6,2},{7,3},{8,12},{9,13},{10,... | collective-permute-start | bytes 884744 | tf_op jit(solution)/shard_map/ppermute | solution.py:789
  194.3 12.0 %collective-permute-start.23 = (bf16[2,48,768]{2,1,0:T(8,128)(2,1)S(1)}, bf16[2,48,768]{2,1,0:T(8,128)(2,1)S(1)}, u32[]{:S(2)}, u32[]{:S(2)}) collective-permute-start(bf16[2,48,768]{2,1,0:T(8,128)(2,1)S(1)} %get-tuple-element.96.rest_0_), channel_id=1, source_target_pairs={{0,8},{1,9},{2,10},{3,11},{4,12},{5,13},{6,14},{7,15},{8,0},{9,1},... | collective-permute-start | bytes 442376 | tf_op jit(solution)/shard_map/ppermute | solution.py:789
  207.0 11.9 %slice-start.1 = ((f32[3,384]{1,0:T(4,128)}), f32[2,384]{1,0:T(2,128)S(1)}, s32[]{:S(2)}) async-start(f32[3,384]{1,0:T(4,128)} %copy-done.33), calls=%async_computation.1 | async-start | bytes 6144 | tf_op jit(solution)/shard_map/slice | solution.py:957
  213.4 30.4 %copy-start.8 = (f32[1,48,768]{2,1,0:T(8,128)S(1)}, f32[1,48,768]{2,1,0:T(8,128)}, u32[]{:S(2)}) copy-start(f32[1,48,768]{2,1,0:T(8,128)} %copy-done.7) | copy-start | bytes 442372
  213.4 30.4 %copy-start.22 = (f32[48,768]{1,0:T(8,128)S(1)}, f32[48,768]{1,0:T(8,128)}, u32[]{:S(2)}) copy-start(f32[48,768]{1,0:T(8,128)} %param.29) | copy-start | bytes 442372
  213.4 30.4 %copy-start.25 = (f32[48,768]{1,0:T(8,128)S(1)}, f32[48,768]{1,0:T(8,128)}, u32[]{:S(2)}) copy-start(f32[48,768]{1,0:T(8,128)} %param.36) | copy-start | bytes 442372
  213.4 30.4 %copy-start.26 = (f32[48,768]{1,0:T(8,128)S(1)}, f32[48,768]{1,0:T(8,128)}, u32[]{:S(2)}) copy-start(f32[48,768]{1,0:T(8,128)} %param.35) | copy-start | bytes 442372
  213.4 5.3 %collective-permute-start.24 = (bf16[1,48,768]{2,1,0:T(8,128)(2,1)S(1)}, bf16[1,48,768]{2,1,0:T(8,128)(2,1)S(1)}, u32[]{:S(2)}, u32[]{:S(2)}) collective-permute-start(bf16[1,48,768]{2,1,0:T(8,128)(2,1)S(1)} %copy-done.21), channel_id=1, source_target_pairs={{0,16},{1,17},{2,18},{3,19},{4,20},{5,21},{6,22},{7,23},{8,24},{9,... | collective-permute-start | bytes 221192 | tf_op jit(solution)/shard_map/ppermute | solution.py:789
  218.7 25.9 %copy-start.31 = (f32[744]{0:T(1024)S(1)}, f32[744]{0:T(1024)}, u32[]{:S(2)}) copy-start(f32[744]{0:T(1024)} %param.30) | copy-start | bytes 8932
  218.7 25.9 %copy-start.34 = (f32[744]{0:T(1024)S(1)}, f32[744]{0:T(1024)}, u32[]{:S(2)}) copy-start(f32[744]{0:T(1024)} %param.38) | copy-start | bytes 8932
  218.7 25.9 %copy-start.35 = (f32[744]{0:T(1024)S(1)}, f32[744]{0:T(1024)}, u32[]{:S(2)}) copy-start(f32[744]{0:T(1024)} %param.37) | copy-start | bytes 8932
  218.7 26.6 %copy-start.23 = (f32[48,384]{1,0:T(8,128)S(1)}, f32[48,384]{1,0:T(8,128)}, u32[]{:S(2)}) copy-start(f32[48,384]{1,0:T(8,128)} %param.28) | copy-start | bytes 221188
  218.8 26.6 %copy-start.24 = (f32[48,384]{1,0:T(8,128)S(1)}, f32[48,384]{1,0:T(8,128)}, u32[]{:S(2)}) copy-start(f32[48,384]{1,0:T(8,128)} %param.27) | copy-start | bytes 221188
  218.8 26.5 %copy-start.27 = (f32[48,384]{1,0:T(8,128)S(1)}, f32[48,384]{1,0:T(8,128)}, u32[]{:S(2)}) copy-start(f32[48,384]{1,0:T(8,128)} %param.34) | copy-start | bytes 221188
  218.8 26.5 %copy-start.28 = (f32[48,384]{1,0:T(8,128)S(1)}, f32[48,384]{1,0:T(8,128)}, u32[]{:S(2)}) copy-start(f32[48,384]{1,0:T(8,128)} %param.33) | copy-start | bytes 221188
  218.8 26.5 %copy-start.29 = (f32[48,384]{1,0:T(8,128)S(1)}, f32[48,384]{1,0:T(8,128)}, u32[]{:S(2)}) copy-start(f32[48,384]{1,0:T(8,128)} %param.32) | copy-start | bytes 221188
  218.8 26.5 %copy-start.30 = (f32[48,384]{1,0:T(8,128)S(1)}, f32[48,384]{1,0:T(8,128)}, u32[]{:S(2)}) copy-start(f32[48,384]{1,0:T(8,128)} %param.31) | copy-start | bytes 221188
  219.0 6.6 %collective-permute-start.25 = (f32[64,384]{1,0:T(8,128)S(1)}, f32[64,384]{1,0:T(8,128)S(1)}, u32[]{:S(2)}, u32[]{:S(2)}) collective-permute-start(f32[64,384]{1,0:T(8,128)S(1)} %concatenate.25), channel_id=1, source_target_pairs={{0,16},{1,17},{2,18},{3,19},{4,20},{5,21},{6,22},{7,23},{8,24},{9,... | collective-permute-start | bytes 294920 | tf_op jit(solution)/shard_map/ppermute | solution.py:789
  225.6 4.7 %collective-permute-start.26 = (f32[64,384]{1,0:T(8,128)S(1)}, f32[64,384]{1,0:T(8,128)S(1)}, u32[]{:S(2)}, u32[]{:S(2)}) collective-permute-start(f32[64,384]{1,0:T(8,128)S(1)} %add.120), channel_id=1, source_target_pairs={{0,8},{1,9},{2,10},{3,11},{4,12},{5,13},{6,14},{7,15},{8,0},{9,1},... | collective-permute-start | bytes 294920 | tf_op jit(solution)/shard_map/ppermute | solution.py:789
  230.3 4.7 %collective-permute-start.27 = (f32[64,384]{1,0:T(8,128)S(1)}, f32[64,384]{1,0:T(8,128)S(1)}, u32[]{:S(2)}, u32[]{:S(2)}) collective-permute-start(f32[64,384]{1,0:T(8,128)S(1)} %add.121), channel_id=1, source_target_pairs={{0,4},{1,5},{2,6},{3,7},{4,0},{5,1},{6,2},{7,3},{8,12},{9,13},{10,... | collective-permute-start | bytes 294920 | tf_op jit(solution)/shard_map/ppermute | solution.py:789
  235.0 4.7 %collective-permute-start.28 = (f32[64,384]{1,0:T(8,128)S(1)}, f32[64,384]{1,0:T(8,128)S(1)}, u32[]{:S(2)}, u32[]{:S(2)}) collective-permute-start(f32[64,384]{1,0:T(8,128)S(1)} %add.122), channel_id=1, source_target_pairs={{0,2},{1,3},{2,0},{3,1},{4,6},{5,7},{6,4},{7,5},{8,10},{9,11},{10,... | collective-permute-start | bytes 294920 | tf_op jit(solution)/shard_map/ppermute | solution.py:789
  239.7 1.4 collective-permute-start.29
  (23 other events, 64.6 us)

commit v3 on v2

v3 whole, which is shorter than its diff:
```python
import functools
import jax
import jax.numpy as jnp
import numpy as np
from jax import lax
from jax.experimental import pallas as pl
from jax.experimental.pallas import tpu as pltpu
from jax.sharding import PartitionSpec as P

STEP = 10
DROP_RATE = 0.2
RATE_MATRIX = 0.05
RATE_VECTOR = 0.3
LAYER_DECAY = 0.8
BETA_ONE = 0.9
BETA_TWO = 0.999
ADAM_EPS = 1e-08
WEIGHT_DECAY = 0.05
CLIP_NORM = 1.0
D = 384
FF = 1536
LN_EPS = 1e-06
F32 = jnp.float32
BF16 = jnp.bfloat16
VMEM = pl.BlockSpec(memory_space=pltpu.VMEM)
SMEM = pl.BlockSpec(memory_space=pltpu.SMEM)
HBM = pl.BlockSpec(memory_space=pltpu.HBM)
ROWS = (((0,), (0,)), ((), ()))
COLS = (((1,), (1,)), ((), ()))
DEPTH_BIAS, GAIN_ONE, BIAS_ONE, HIDDEN_BIAS, OUT_BIAS, LAYER_SCALE, GAIN_TWO, BIAS_TWO, DOWN_BIAS = 49, 50, 51, 52, 56, 57, 58, 59, 60
SQUARES = 62


def near(shape, dtype):
    return jax.ShapeDtypeStruct(shape, dtype)


def far(shape, dtype):
    return pltpu.HBM(shape, dtype)


def held(x):
    return pltpu.with_memory_space_constraint(x, pltpu.HBM)


def dma(src, dst, sem):
    return pltpu.make_async_copy(src, dst, sem)


def start(copies):
    for copy in copies:
        copy.start()


def wait(copies):
    for copy in copies:
        copy.wait()


def kernel_call(body, out, specs, scratch, args, after, us, mib, aliases=None):
    specs = specs + [HBM] * len(after)
    args = tuple(args) + tuple(after)
    args = [held(x) if spec is HBM else x for spec, x in zip(specs, args)]
    return pl.pallas_call(
        body,
        out_shape=tuple(out),
        in_specs=specs,
        out_specs=tuple(HBM if isinstance(x, type(far((8, 128), F32))) else VMEM for x in out),
        scratch_shapes=scratch,
        input_output_aliases=aliases or {},
        cost_estimate=pl.CostEstimate(flops=int(us * 1e9), bytes_accessed=0, transcendentals=0),
        compiler_params=pltpu.CompilerParams(vmem_limit_bytes=mib << 20),
    )(*args)


def norm_of(v):
    c = v - jnp.mean(v, axis=-1, keepdims=True)
    inv = lax.rsqrt(jnp.mean(c * c, axis=-1, keepdims=True) + LN_EPS)
    return c * inv, inv


def norm_back(back, unit, inv, gain):
    scaled = back * gain
    m1 = jnp.mean(scaled, axis=-1, keepdims=True)
    m2 = jnp.mean(scaled * unit, axis=-1, keepdims=True)
    return inv * (scaled - m1 - unit * m2)


def conv_rows(src, taps, h, t, lanes, side, base, flip):
    def one(ky, acc):
        acc = list(acc)
        x = [src[h + ky - 3, w, t, lanes] for w in range(side)]
        for kx in range(7):
            tap = taps[48 - (ky * 7 + kx) if flip else ky * 7 + kx, :, lanes]
            for w in range(side):
                if 0 <= w + kx - 3 < side:
                    acc[w] = acc[w] + x[w + kx - 3] * tap
        return tuple(acc)

    first = jnp.maximum(3 - h, 0)
    last = jnp.minimum(7, side + 3 - h)
    return lax.fori_loop(first, last, one, tuple(base))


def spread(scalars_ref, rows_ref):
    for i in range(rows_ref.shape[0]):
        rows_ref[i : i + 1, :] = jnp.full((1, rows_ref.shape[1]), scalars_ref[i], F32)


def select(row_ref, sel_ref):
    imgs, wide = row_ref.shape
    lane = lax.broadcasted_iota(jnp.int32, (imgs, wide), 1)
    for w in range(wide // imgs):
        sel_ref[w * imgs : (w + 1) * imgs, :] = (lane == row_ref[...] + w * imgs).astype(F32).astype(BF16)


def conv_kernel(begin, end, fresh, *refs):
    if fresh:
        small_hbm, img_hbm, partner_ref, weight_ref = refs[:4]
        mixed_hbm, unit_hbm, inv_hbm, norm_hbm, small_ref, mixed_ref, taps, conv_ref, unit_ref, inv_ref, norm_ref, sem, img_ref, mix_ref, row_ref, sel_ref = refs[-16:]
    else:
        small_hbm, mixed_hbm = refs[:2]
        unit_hbm, inv_hbm, norm_hbm, small_ref, mixed_ref, taps, conv_ref, unit_ref, inv_ref, norm_ref, sem = refs[-11:]
    side, _, imgs, _ = mixed_ref.shape
    low = max(begin - 3, 0)
    high = side if fresh else min(end + 3, side)
    rows = end - begin
    load = dma(small_hbm, small_ref, sem.at[4, 0])
    load.start()

    def enter(h):
        if fresh:
            return dma(img_hbm.at[h], img_ref.at[h], sem.at[3, h])
        return dma(mixed_hbm.at[h], mixed_ref.at[h], sem.at[3, h])

    def store(h):
        return dma(mixed_ref.at[h], mixed_hbm.at[h], sem.at[5, h])

    for h in range(low, high):
        enter(h).start()
    if fresh:
        spread(weight_ref, mix_ref)
        for i in range(imgs):
            row_ref[i : i + 1, :] = jnp.full((1, row_ref.shape[1]), lax.rem(partner_ref[i], imgs), jnp.int32)
        select(row_ref, sel_ref)
    load.wait()
    for t in range(49):
        taps[t] = jnp.broadcast_to(small_ref[t : t + 1, :], (8, D))
    if fresh:
        mix = mix_ref[...][None]
        rest = 1.0 - mix

        def blend(h, _):
            enter(h).wait()
            x = img_ref[h].reshape(side * imgs, D)
            other = jnp.dot(sel_ref[...], x, preferred_element_type=F32).reshape(side, imgs, D)
            mixed_ref[h] = mix * x.reshape(side, imgs, D).astype(F32) + rest * other
            store(h).start()
            return 0

        lax.fori_loop(0, side, blend, 0)
    else:
        for h in range(low, min(begin + 3, high)):
            enter(h).wait()

    def conv(r, _):
        h = r + begin
        if not fresh:

            @pl.when(h + 3 < high)
            def _():
                enter(h + 3).wait()

        for t in range(imgs // 8):
            at = pl.ds(t * 8, 8)
            for g in range(D // 128):
                lanes = pl.ds(g * 128, 128)
                base = jnp.broadcast_to(small_ref[DEPTH_BIAS : DEPTH_BIAS + 1, lanes], (8, 128))
                acc = conv_rows(mixed_ref, taps, h, at, lanes, side, [base] * side, False)
                for w in range(side):
                    conv_ref[r, w, at, lanes] = acc[w]
        return 0

    lax.fori_loop(0, rows, conv, 0)
    gain = small_ref[GAIN_ONE : GAIN_ONE + 1, :][None]
    bias = small_ref[BIAS_ONE : BIAS_ONE + 1, :][None]

    def leave(r):
        return (
            dma(unit_ref.at[r], unit_hbm.at[r + begin], sem.at[0, r]),
            dma(inv_ref.at[r], inv_hbm.at[r + begin], sem.at[1, r]),
            dma(norm_ref.at[r], norm_hbm.at[r + begin], sem.at[2, r]),
        )

    def norm(r, _):
        unit, inv = norm_of(conv_ref[r])
        unit_ref[r] = unit.astype(BF16)
        inv_ref[r] = inv
        norm_ref[r] = (unit * gain + bias).astype(BF16)
        start(leave(r))
        return 0

    lax.fori_loop(0, rows, norm, 0)
    for r in range(rows):
        wait(leave(r))
    if fresh:
        for h in range(side):
            store(h).wait()


def conv_forward(small, inputs, begin, end, so_far=(), after=()):
    fresh = not so_far
    full = inputs[0].shape
    side = full[0]
    thin = full[:3] + (1,)
    rows = end - begin
    out = [far(full, BF16), far(thin, F32), far(full, BF16)]
    scratch = [
        pltpu.VMEM(small.shape, F32),
        pltpu.VMEM(full, F32),
        pltpu.VMEM((49, 8, D), F32),
        pltpu.VMEM((rows,) + full[1:], F32),
        pltpu.VMEM((rows,) + full[1:], BF16),
        pltpu.VMEM((rows,) + thin[1:], F32),
        pltpu.VMEM((rows,) + full[1:], BF16),
        pltpu.SemaphoreType.DMA((6, side)),
    ]
    specs = [HBM] * 2
    if fresh:
        out = [far(full, F32)] + out
        wide = side * full[2]
        scratch += [pltpu.VMEM(full, BF16), pltpu.VMEM((full[2], D), F32), pltpu.VMEM((full[2], wide), jnp.int32), pltpu.VMEM((wide, wide), BF16)]
        specs = [HBM] * 2 + [SMEM] * 2
    return kernel_call(
        functools.partial(conv_kernel, begin, end, fresh),
        out,
        specs + [HBM] * len(so_far),
        scratch,
        (small,) + tuple(inputs) + tuple(so_far),
        after,
        21 * rows / side + 3 * fresh,
        28,
        {2 + k: k for k in range(len(so_far))},
    )


def assembly(origin_ref, near_hbm, far_hbm, whole_ref, sem):
    pieces = origin_ref.shape[0]
    deep = whole_ref.shape[0] // pieces

    def copy(j, src, k):
        to = pl.ds(pl.multiple_of(origin_ref[j] * deep, 16), deep)
        return dma(src.at[pl.ds(k * deep, deep), :], whole_ref.at[to, :], sem)

    return [copy(j, near_hbm if j < pieces // 2 else far_hbm, j % (pieces // 2)) for j in range(pieces)]


def keep_rows(mask_ref, keep_ref):
    for i in range(keep_ref.shape[0]):
        keep_ref[i : i + 1, :] = jnp.full((1, D), mask_ref[i], jnp.int32).astype(F32) / (1.0 - DROP_RATE)


def hidden_kernel(block, origin_ref, norm_hbm, mixed_hbm, near_hbm, far_hbm, small_hbm, mask_ref, *rest):
    act_hbm, dg_hbm, branch_hbm, unit_hbm, inv_hbm, out_hbm = rest[-20:-14]
    pair_ref, small_ref, keep_ref, norm_ref, mixed_ref, act_ref, dg_ref, branch_ref, unit_ref, inv_ref, out_ref, isem, osem, wsem = rest[-14:]
    rows = norm_hbm.shape[0]
    steps = rows // block
    imgs = keep_ref.shape[0]
    shape = (block // imgs, imgs, D)
    wide = FF // 2

    def spot(i):
        return pl.ds(pl.multiple_of(i * block, block), block)

    def enter(i):
        s = i % 2
        return (
            dma(norm_hbm.at[spot(i), :], norm_ref.at[s], isem.at[0, s]),
            dma(mixed_hbm.at[spot(i), :], mixed_ref.at[s], isem.at[1, s]),
        )

    def leave(i):
        s = i % 2
        pairs = ((act_ref, act_hbm), (dg_ref, dg_hbm), (branch_ref, branch_hbm), (unit_ref, unit_hbm), (inv_ref, inv_hbm), (out_ref, out_hbm))
        return [dma(a.at[s], b.at[spot(i), :], osem.at[k, s]) for k, (a, b) in enumerate(pairs)]

    load = dma(small_hbm, small_ref, wsem.at[0])
    start(enter(0))
    load.start()
    pieces_in = assembly(origin_ref, near_hbm, far_hbm, pair_ref, wsem.at[1])
    start(pieces_in)
    wait(pieces_in)
    load.wait()
    keep_rows(mask_ref, keep_ref)
    scale = (keep_ref[...] * small_ref[LAYER_SCALE : LAYER_SCALE + 1, :])[None]
    gain = small_ref[GAIN_TWO : GAIN_TWO + 1, :][None]
    bias = small_ref[BIAS_TWO : BIAS_TWO + 1, :][None]

    def body(i, _):
        s = i % 2

        @pl.when(i + 1 < steps)
        def _():
            start(enter(i + 1))

        @pl.when(i >= 2)
        def _():
            wait(leave(i - 2))

        wait(enter(i))
        x = norm_ref[s]
        branch = jnp.broadcast_to(small_ref[OUT_BIAS : OUT_BIAS + 1, :], (block, D))
        for j in range(2):
            cols = pl.ds(j * wide, wide)
            bias_row = jnp.concatenate([small_ref[HIDDEN_BIAS + 2 * j + k : HIDDEN_BIAS + 2 * j + k + 1, :] for k in range(2)], axis=1)
            pre = lax.dot_general(x, pair_ref[cols, :D], COLS, preferred_element_type=F32) + bias_row
            phi = 0.5 + 0.5 * lax.erf(pre * 0.7071067811865476)
            bell = jnp.exp2(pre * pre * -0.7213475204444817) * 0.3989422804014327
            act = (pre * phi).astype(BF16)
            act_ref[s, :, cols] = act
            dg_ref[s, :, cols] = (phi + pre * bell).astype(BF16)
            branch = branch + jnp.dot(act, pair_ref[cols, D:], preferred_element_type=F32)
        branch_ref[s] = branch.astype(BF16)
        unit, inv = norm_of(mixed_ref[s].reshape(shape) + scale * branch.reshape(shape))
        unit_ref[s] = unit.astype(BF16).reshape(block, D)
        inv_ref[s] = inv.reshape(block, 1)
        out_ref[s] = (unit * gain + bias).astype(BF16).reshape(block, D)
        start(leave(i))
        return 0

    lax.fori_loop(0, steps, body, 0)
    for i in range(max(steps - 2, 0), steps):
        wait(leave(i))


def hidden_forward(origin, norm, mixed, pair, small, mask, after=(), block=448):
    rows = norm.shape[0]
    two = lambda width, dtype: pltpu.VMEM((2, block, width), dtype)
    return kernel_call(
        functools.partial(hidden_kernel, block),
        [far((rows, FF), BF16)] * 2 + [far((rows, D), BF16)] * 2 + [far((rows, 1), F32), far((rows, D), BF16)],
        [SMEM] + [HBM] * 5 + [SMEM],
        [pltpu.VMEM((FF, 2 * D), BF16), pltpu.VMEM(small.shape, F32), pltpu.VMEM((mask.shape[0], D), F32)]
        + [two(D, BF16), two(D, F32), two(FF, BF16), two(FF, BF16)]
        + [two(D, BF16), two(D, BF16), two(1, F32), two(D, BF16)]
        + [pltpu.SemaphoreType.DMA((2, 2)), pltpu.SemaphoreType.DMA((6, 2)), pltpu.SemaphoreType.DMA((3,))],
        (origin, norm, mixed, *pair, small, mask),
        after,
        17,
        32,
    )


def deal(origin_ref, near_ref, far_ref, read):
    pieces = origin_ref.shape[0]
    deep = 2 * near_ref.shape[0] // pieces
    for half_ref, first in ((near_ref, 0), (far_ref, pieces // 2)):

        def move(j, _):
            begin = pl.multiple_of(origin_ref[first + j] * deep, 16)
            to = pl.multiple_of(j * deep, 16)
            for g in range(half_ref.shape[1] // 128):
                half_ref[pl.ds(to, deep), pl.ds(g * 128, 128)] = read(pl.ds(begin, deep), g).astype(BF16)
            return 0

        lax.fori_loop(0, pieces // 2, move, 0)


def down_kernel(home_ref, origin_ref, norm_hbm, unit_hbm, inv_hbm, branch_hbm, near_hbm, far_hbm, dy_hbm, small_hbm, mask_ref, *rest):
    gnear_ref, gfar_ref, gdb_ref, out_ref, bb_hbm, sums_ref, res_hbm = rest[-23:-16]
    wd_ref, dy_ref, small_ref, keep_ref, norm_ref, unit_ref, inv_ref, branch_ref, bb_ref, res_ref, acc, wide, wk, wsem, isem, osem = rest[-16:]
    half, _, _, _, imgs, _ = norm_hbm.shape
    rows = half * half * imgs
    loads = [dma(dy_hbm, dy_ref, wsem.at[1]), dma(small_hbm, small_ref, wsem.at[2])]
    pieces_in = assembly(home_ref, near_hbm, far_hbm, wd_ref, wsem.at[0])
    start(pieces_in)
    start(loads)

    def enter(k):
        pairs = ((norm_hbm, norm_ref), (unit_hbm, unit_ref), (inv_hbm, inv_ref), (branch_hbm, branch_ref))
        return [dma(a.at[:, k // 2, :, k % 2], b.at[k], isem.at[j, k]) for j, (a, b) in enumerate(pairs)]

    def leave(k):
        pairs = ((bb_ref, bb_hbm), (res_ref, res_hbm))
        return [dma(a.at[k], b.at[:, k // 2, :, k % 2], osem.at[j, k]) for j, (a, b) in enumerate(pairs)]

    for k in range(4):
        start(enter(k))
    wait(pieces_in)
    for g in range(6):
        wide[g] = wd_ref[:, pl.ds(g * 128, 128)].astype(F32)
        for k in range(4):
            wk[k, :, pl.ds(g * 128, 128)] = wide[g, pl.ds(k, D, stride=4), :].astype(BF16)
    sums_ref[...] = jnp.zeros(sums_ref.shape, F32)
    shape = (half * half, imgs, D)
    wait(loads)
    keep_rows(mask_ref, keep_ref)
    for k in range(2):
        acc[:, k * D : (k + 1) * D] = jnp.broadcast_to(small_ref[DOWN_BIAS + k : DOWN_BIAS + k + 1, :], (rows, D))
    gdb_ref[...] = jnp.sum(dy_ref[...].astype(F32).reshape(half * half, imgs, 2 * D), axis=0)
    gain = small_ref[GAIN_TWO : GAIN_TWO + 1, :][None]
    keep = keep_ref[...][None]
    scale = keep * small_ref[LAYER_SCALE : LAYER_SCALE + 1, :][None]

    for k in range(4):
        wait(enter(k))
        dy = dy_ref[...].reshape(rows, 2 * D)
        x = norm_ref[k].reshape(rows, D)
        acc[...] += jnp.dot(x, wk[k], preferred_element_type=F32)
        for g in range(6):
            wide[g, pl.ds(k, D, stride=4), :] = lax.dot_general(
                x, dy[:, g * 128 : (g + 1) * 128], ROWS, preferred_element_type=F32
            )
        back = lax.dot_general(dy, wk[k], COLS, preferred_element_type=F32).reshape(shape)
        unit = unit_ref[k].reshape(shape).astype(F32)
        sums_ref[0] += jnp.sum(back * unit, axis=0)
        sums_ref[1] += jnp.sum(back, axis=0)
        res = norm_back(back, unit, inv_ref[k].reshape(half * half, imgs, 1), gain)
        res_ref[k] = res.reshape(half, half, imgs, D)
        kept = res * keep
        sums_ref[2] += jnp.sum(kept * branch_ref[k].reshape(shape).astype(F32), axis=0)
        bb = (res * scale).astype(BF16)
        bb_ref[k] = bb.reshape(half, half, imgs, D)
        start(leave(k))
        sums_ref[3] += jnp.sum(bb.astype(F32), axis=0)

    out_ref[...] = acc[...].astype(BF16).reshape(out_ref.shape)
    deal(origin_ref, gnear_ref, gfar_ref, lambda at, g: wide[g, at, :])
    for k in range(4):
        wait(leave(k))


def down_both(home, origin, norm, unit, inv, branch, wd, dy, small, mask, after=()):
    half, _, _, _, imgs, _ = norm.shape
    rows = half * half * imgs
    four = lambda width, dtype: pltpu.VMEM((4, half, half, imgs, width), dtype)
    return kernel_call(
        down_kernel,
        [near((2 * D, 2 * D), BF16)] * 2
        + [near((imgs, 2 * D), F32), near((half, half, imgs, 2 * D), BF16), far(norm.shape, BF16), near((4, imgs, D), F32), far(norm.shape, F32)],
        [SMEM] * 2 + [HBM] * 8 + [SMEM],
        [pltpu.VMEM((4 * D, 2 * D), BF16), pltpu.VMEM(dy.shape, BF16), pltpu.VMEM(small.shape, F32), pltpu.VMEM((imgs, D), F32)]
        + [four(D, BF16), four(D, BF16), four(1, F32), four(D, BF16), four(D, BF16), four(D, F32)]
        + [pltpu.VMEM((rows, 2 * D), F32), pltpu.VMEM((6, 4 * D, 128), F32), pltpu.VMEM((4, D, 2 * D), BF16)]
        + [pltpu.SemaphoreType.DMA((3,)), pltpu.SemaphoreType.DMA((4, 4)), pltpu.SemaphoreType.DMA((2, 4))],
        (home, origin, norm, unit, inv, branch, *wd, dy, small, mask),
        after,
        20,
        48,
    )


def pair_grad_kernel(block, origin_ref, bb_hbm, act_hbm, dg_hbm, norm_hbm, unit_hbm, inv_hbm, near_hbm, far_hbm, small_hbm, *rest):
    gnear_ref, gfar_ref, hb_ref, sums_ref, conv_hbm = rest[-17:-12]
    pair_ref, small_ref, acc, bb_ref, act_ref, dg_ref, norm_ref, unit_ref, inv_ref, conv_ref, sem, wsem = rest[-12:]
    rows = bb_hbm.shape[0]
    imgs = hb_ref.shape[0]
    steps = rows // block
    wide = FF // 2
    shape = (block // imgs, imgs, D)

    def spot(i):
        return pl.ds(pl.multiple_of(i * block, block), block)

    def enter(i):
        s = i % 2
        pairs = ((act_hbm, act_ref), (dg_hbm, dg_ref), (norm_hbm, norm_ref), (bb_hbm, bb_ref), (unit_hbm, unit_ref), (inv_hbm, inv_ref))
        return [dma(a.at[spot(i), :], b.at[s], sem.at[k, s]) for k, (a, b) in enumerate(pairs)]

    def leave(i):
        return dma(conv_ref.at[i % 2], conv_hbm.at[spot(i), :], sem.at[6, i % 2])

    load = dma(small_hbm, small_ref, wsem.at[0])
    start(enter(0))
    load.start()
    hb_ref[...] = jnp.zeros(hb_ref.shape, F32)
    sums_ref[...] = jnp.zeros(sums_ref.shape, F32)
    acc[...] = jnp.zeros(acc.shape, F32)
    pieces_in = assembly(origin_ref, near_hbm, far_hbm, pair_ref, wsem.at[1])
    start(pieces_in)
    wait(pieces_in)
    load.wait()
    gain = small_ref[GAIN_ONE : GAIN_ONE + 1, :][None]

    def body(i, _):
        s = i % 2

        @pl.when(i + 1 < steps)
        def _():
            start(enter(i + 1))

        @pl.when(i >= 2)
        def _():
            leave(i - 2).wait()

        wait(enter(i))
        b = bb_ref[s]
        x = norm_ref[s]
        back_one = None
        for j in range(2):
            cols = pl.ds(j * wide, wide)
            back = lax.dot_general(b, pair_ref[cols, D:], COLS, preferred_element_type=F32)
            p = (back * dg_ref[s, :, cols].astype(F32)).astype(BF16)
            hb_ref[:, cols] += jnp.sum(p.astype(F32).reshape(block // imgs, imgs, wide), axis=0)
            acc[cols, D:] += lax.dot_general(act_ref[s, :, cols], b, ROWS, preferred_element_type=F32)
            acc[cols, :D] += lax.dot_general(p, x, ROWS, preferred_element_type=F32)
            term = jnp.dot(p, pair_ref[cols, :D], preferred_element_type=F32)
            back_one = term if back_one is None else back_one + term
        back = back_one.reshape(shape)
        unit = unit_ref[s].reshape(shape).astype(F32)
        sums_ref[0] += jnp.sum(back * unit, axis=0)
        sums_ref[1] += jnp.sum(back, axis=0)
        out = norm_back(back, unit, inv_ref[s].reshape(shape[:2] + (1,)), gain)
        sums_ref[2] += jnp.sum(out, axis=0)
        conv_ref[s] = out.reshape(block, D)
        leave(i).start()
        return 0

    lax.fori_loop(0, steps, body, 0)
    deal(origin_ref, gnear_ref, gfar_ref, lambda at, g: acc[at, pl.ds(g * 128, 128)])
    for i in range(max(steps - 2, 0), steps):
        leave(i).wait()


def pair_grad(origin, bb, act, dg, norm, unit, inv, pair, small, imgs, after=(), block=448):
    rows = bb.shape[0]
    two = lambda width, dtype=BF16: pltpu.VMEM((2, block, width), dtype)
    return kernel_call(
        functools.partial(pair_grad_kernel, block),
        [near((FF // 2, 2 * D), BF16)] * 2 + [near((imgs, FF), F32), near((3, imgs, D), F32), far((rows, D), F32)],
        [SMEM] + [HBM] * 9,
        [pltpu.VMEM((FF, 2 * D), BF16), pltpu.VMEM(small.shape, F32), pltpu.VMEM((FF, 2 * D), F32)]
        + [two(D), two(FF), two(FF), two(D), two(D), two(1, F32), two(D, F32)]
        + [pltpu.SemaphoreType.DMA((7, 2)), pltpu.SemaphoreType.DMA((3,))],
        (origin, bb, act, dg, norm, unit, inv, *pair, small),
        after,
        32,
        40,
    )


def taps_kernel(groups, conv_hbm, mixed_hbm, *rest):
    g_ref, conv_ref, mixed_ref, sem = rest[-4:]
    side, _, imgs, _ = conv_hbm.shape

    def enter(k):
        lanes = pl.ds(groups[k] * 128, 128)
        return (
            dma(mixed_hbm.at[:, :, :, lanes], mixed_ref.at[k], sem.at[0, k]),
            dma(conv_hbm.at[:, :, :, lanes], conv_ref.at[k], sem.at[1, k]),
        )

    for k in range(len(groups)):
        start(enter(k))
    for k in range(len(groups)):
        wait(enter(k))

        def per_ky(ky, _):
            first = jnp.maximum(3 - ky, 0)
            last = jnp.minimum(side, side + 3 - ky)

            def row(h, acc):
                acc = list(acc)
                for t in range(imgs // 8):
                    at = pl.ds(t * 8, 8)
                    x = [mixed_ref[k, h + ky - 3, w, at] for w in range(side)]
                    for w in range(side):
                        d = conv_ref[k, h, w, at]
                        for kx in range(7):
                            if 0 <= w + kx - 3 < side:
                                acc[kx] = acc[kx] + x[w + kx - 3] * d
                return tuple(acc)

            acc = lax.fori_loop(first, last, row, (jnp.zeros((8, 128), F32),) * 7)
            for kx in range(7):
                g_ref[ky * 7 + kx, :, pl.ds(k * 128, 128)] = acc[kx]
            return 0

        lax.fori_loop(0, 7, per_ky, 0)


def taps_grad(conv, mixed, groups, after=()):
    lanes = pltpu.VMEM((len(groups),) + conv.shape[:3] + (128,), F32)
    return kernel_call(
        functools.partial(taps_kernel, groups),
        [near((49, 8, 128 * len(groups)), F32)],
        [HBM] * 2,
        [lanes, lanes, pltpu.SemaphoreType.DMA((2, len(groups)))],
        (conv, mixed),
        after,
        4.7 * len(groups),
        20,
    )[0]


def images_kernel(begin, end, conv_hbm, small_hbm, partner_ref, weight_ref, res_hbm, *rest):
    g_hbm, small_ref, conv_ref, taps, res_ref, out_ref, mix_ref, row_ref, sel_ref, sem, csem = rest[-11:]
    side, _, imgs, _ = conv_hbm.shape
    low = max(begin - 3, 0)
    high = min(end + 3, side)
    load = dma(small_hbm, small_ref, csem.at[side])
    load.start()

    def bring(h):
        return dma(conv_hbm.at[h], conv_ref.at[h], csem.at[h])

    def enter(h):
        return dma(res_hbm.at[h], res_ref.at[h % 2], sem.at[0, h % 2])

    def leave(h):
        return dma(out_ref.at[h % 2], g_hbm.at[h], sem.at[1, h % 2])

    for h in range(low, high):
        bring(h).start()
        if h == min(begin + 3, high - 1):
            enter(begin).start()
    spread(weight_ref, mix_ref)
    for i in range(imgs):
        row_ref[pl.ds(lax.rem(partner_ref[i], imgs), 1), :] = jnp.full((1, row_ref.shape[1]), i, jnp.int32)
    select(row_ref, sel_ref)
    load.wait()
    for t in range(49):
        taps[t] = jnp.broadcast_to(small_ref[t : t + 1, :], (8, D))
    mix = mix_ref[...][None]
    others = 1.0 - mix
    for h in range(low, min(begin + 3, high)):
        bring(h).wait()

    def row(h, _):
        s = h % 2

        @pl.when(h + 1 < end)
        def _():
            enter(h + 1).start()

        @pl.when(h + 3 < high)
        def _():
            bring(h + 3).wait()

        @pl.when(h >= begin + 2)
        def _():
            leave(h - 2).wait()

        enter(h).wait()
        for t in range(imgs // 8):
            at = pl.ds(t * 8, 8)
            for g in range(D // 128):
                lanes = pl.ds(g * 128, 128)
                base = [res_ref[s, w, at, lanes] for w in range(side)]
                acc = conv_rows(conv_ref, taps, h, at, lanes, side, base, True)
                for w in range(side):
                    out_ref[s, w, at, lanes] = acc[w]
        v = out_ref[s]
        part = (others * v).reshape(side * imgs, D)
        upper = part.astype(BF16)
        lower = (part - upper.astype(F32)).astype(BF16)
        back = jnp.dot(sel_ref[...], upper, preferred_element_type=F32)
        back = back + jnp.dot(sel_ref[...], lower, preferred_element_type=F32)
        out_ref[s] = mix * v + back.reshape(side, imgs, D)
        leave(h).start()
        return 0

    lax.fori_loop(begin, end, row, 0)
    for h in range(end - 2, end):
        leave(h).wait()


def images_back(conv, small, partner, weight, res, begin, end, so_far=(), after=()):
    side, _, imgs, _ = conv.shape
    return kernel_call(
        functools.partial(images_kernel, begin, end),
        [far(conv.shape, F32)],
        [HBM, HBM, SMEM, SMEM, HBM] + [HBM] * len(so_far),
        [
            pltpu.VMEM(small.shape, F32),
            pltpu.VMEM(conv.shape, F32),
            pltpu.VMEM((49, 8, D), F32),
            pltpu.VMEM((2, side, imgs, D), F32),
            pltpu.VMEM((2, side, imgs, D), F32),
            pltpu.VMEM((imgs, D), F32),
            pltpu.VMEM((imgs, side * imgs), jnp.int32),
            pltpu.VMEM((side * imgs, side * imgs), BF16),
            pltpu.SemaphoreType.DMA((2, 2)),
            pltpu.SemaphoreType.DMA((side + 1,)),
        ],
        (conv, small, partner, weight, res) + tuple(so_far),
        after,
        22 * (end - begin) / side,
        16,
        {5: 0} if so_far else {},
    )[0]


def ready_kernel(in_hbm, out_hbm, down_hbm, *rest):
    pair_ref, low_ref, in_ref, out_ref, down_ref, sem = rest[-6:]
    pairs = ((in_hbm, in_ref), (out_hbm, out_ref), (down_hbm, down_ref))
    copies = [dma(a, b, sem.at[k]) for k, (a, b) in enumerate(pairs)]
    start(copies)
    wait(copies)
    pair_ref[0, :, :D] = in_ref[...].astype(BF16)
    pair_ref[0, :, D:] = out_ref[...].astype(BF16)
    low_ref[0] = down_ref[...].astype(BF16)


def ready(weight_in, weight_out, weight_down, after=()):
    deep = weight_in.shape[0]
    return kernel_call(
        ready_kernel,
        [near((1, deep, 2 * D), BF16)] * 2,
        [HBM] * 3,
        [pltpu.VMEM(x.shape, F32) for x in (weight_in, weight_out, weight_down)] + [pltpu.SemaphoreType.DMA((3,))],
        (weight_in, weight_out, weight_down),
        after,
        0.5,
        8,
    )


def join_kernel(first_ref, second_ref, *rest):
    out_ref = rest[-1]
    k = first_ref.shape[0]
    out_ref[:k] = first_ref[...]
    out_ref[k:] = second_ref[...]


def join(first, second, after=()):
    return kernel_call(
        join_kernel,
        [near((2 * first.shape[0],) + first.shape[1:], first.dtype)],
        [VMEM] * 2,
        [],
        (first, second),
        after,
        0.5,
        8,
    )[0]


def fold_kernel(count, *refs):
    ins, (stay_ref, leave_ref) = refs[: 2 * count], refs[-2:]
    k = stay_ref.shape[0] // count
    for i in range(count):
        keep_ref, come_ref = ins[2 * i], ins[2 * i + 1]
        stay_ref[i * k : (i + 1) * k] = keep_ref[:k].astype(F32) + come_ref[:k].astype(F32)
        leave_ref[i * k : (i + 1) * k] = (keep_ref[k:].astype(F32) + come_ref[k:].astype(F32)).astype(BF16)


def fold(*arrays, after=()):
    slots, deep, wide = arrays[0].shape
    count = len(arrays) // 2
    return kernel_call(
        functools.partial(fold_kernel, count),
        [near((count * slots // 2, deep, wide), F32), near((count * slots // 2, deep, wide), BF16)],
        [VMEM] * len(arrays),
        [],
        arrays,
        after,
        0.5,
        12,
    )


def small_kernel(gk1_ref, gk2_ref, sums1_ref, sums2_ref, hb_ref, db_ref, keep_ref, come_ref, sum_ref, send_ref, total):
    grads = keep_ref[...] + come_ref[...].astype(F32)
    sum_ref[...] = grads
    rows = lambda x: jnp.sum(x, axis=0, keepdims=True)
    for t in range(49):
        total[t : t + 1, :128] = rows(gk1_ref[t])
        total[t : t + 1, 128:] = rows(gk2_ref[t])
    for row, value in (
        (DEPTH_BIAS, sums1_ref[2]),
        (GAIN_ONE, sums1_ref[0]),
        (BIAS_ONE, sums1_ref[1]),
        (OUT_BIAS, sums2_ref[3]),
        (LAYER_SCALE, sums2_ref[2]),
        (GAIN_TWO, sums2_ref[0]),
        (BIAS_TWO, sums2_ref[1]),
    ):
        total[row : row + 1, :] = rows(value)
    for k in range(4):
        total[HIDDEN_BIAS + k : HIDDEN_BIAS + k + 1, :] = rows(hb_ref[:, k * D : (k + 1) * D])
    for k in range(2):
        total[DOWN_BIAS + k : DOWN_BIAS + k + 1, :] = rows(db_ref[:, k * D : (k + 1) * D])
    square = jnp.full((1, D), jnp.sum(grads * grads), F32)
    upper = square.astype(BF16).astype(F32)
    total[SQUARES : SQUARES + 1, :] = upper
    total[SQUARES + 1 : SQUARES + 2, :] = square - upper
    send_ref[...] = total[...].astype(BF16)


def small_total(gk1, gk2, sums1, sums2, hb, db, keep, come):
    return kernel_call(
        small_kernel,
        [near(keep.shape, F32), near((SQUARES + 2, D), BF16)],
        [VMEM] * 8,
        [pltpu.VMEM((SQUARES + 2, D), F32)],
        (gk1, gk2, sums1, sums2, hb, db, keep, come),
        (),
        1,
        8,
    )


def meet_kernel(mine_ref, come_ref, out_ref):
    total = mine_ref[...].astype(F32) + come_ref[...].astype(F32)
    square = total[SQUARES : SQUARES + 1] + total[SQUARES + 1 : SQUARES + 2]
    upper = square.astype(BF16).astype(F32)
    out_ref[...] = total.astype(out_ref.dtype)
    out_ref[SQUARES : SQUARES + 2, :] = jnp.concatenate([upper, square - upper], axis=0).astype(out_ref.dtype)


def meet(mine, come, dtype):
    return kernel_call(meet_kernel, [near(mine.shape, dtype)], [VMEM] * 2, [], (mine, come), (), 0.3, 8)[0]


def adam(weight, first, second, grad, rate, decay):
    first = BETA_ONE * first + (1.0 - BETA_ONE) * grad
    second = BETA_TWO * second + (1.0 - BETA_TWO) * grad * grad
    first_hat = first / (1.0 - BETA_ONE**STEP)
    second_hat = second / (1.0 - BETA_TWO**STEP)
    weight = weight - rate * (first_hat / (jnp.sqrt(second_hat) + ADAM_EPS) + decay * weight)
    return first, second, weight


def adam_kernel(total_ref, grads_ref, *refs):
    ins, outs = refs[:9], refs[9:18]
    norm_ref = refs[18]
    gs = total_ref[:SQUARES]
    norm = jnp.sqrt(jnp.sum(gs * gs) + jnp.sum(total_ref[SQUARES : SQUARES + 2, 0:1]))
    norm_ref[0, 0] = norm
    factor = CLIP_NORM / jnp.maximum(norm, CLIP_NORM)
    grads = (grads_ref[0, :, :D], grads_ref[0, :, D:], grads_ref[1])
    rates = (LAYER_DECAY * RATE_MATRIX, LAYER_DECAY * RATE_MATRIX, RATE_MATRIX)
    for k in range(3):
        new = adam(ins[3 * k][...], ins[3 * k + 1][...], ins[3 * k + 2][...], grads[k] * factor, rates[k], WEIGHT_DECAY)
        for out_ref, value in zip(outs[3 * k : 3 * k + 3], new):
            out_ref[...] = value


def adam_all(total, grads, states):
    return pl.pallas_call(
        adam_kernel,
        out_shape=tuple(near(x.shape, F32) for x in states) + (near((1, 1), F32),),
        in_specs=[VMEM] * 11,
        out_specs=(VMEM,) * 9 + (SMEM,),
        cost_estimate=pl.CostEstimate(flops=int(2e9), bytes_accessed=0, transcendentals=0),
        compiler_params=pltpu.CompilerParams(vmem_limit_bytes=12 << 20),
    )(total, grads, *states)


def swap(x, bit, n):
    return lax.ppermute(x, "dp", [(i, i ^ bit) for i in range(n)])


def is_set(bit):
    return (lax.axis_index("dp") & bit) != 0


def gather_natural(shard, n, order, gates=None):
    have = shard
    met = []
    for hop, bit in enumerate(order):
        if gates and hop in gates:
            have, _ = lax.optimization_barrier((have, gates[hop]))
        other = swap(have, bit, n)
        axis = sum(1 for b in met if b > bit)
        mine = is_set(bit)
        have = jnp.stack([jnp.where(mine, other, have), jnp.where(mine, have, other)], axis=axis)
        met.append(bit)
    return have.reshape((n,) + shard.shape)


def masks_of(n, order):
    masks = np.zeros(n, np.int32)
    for k, bit in enumerate(order):
        masks += ((np.arange(n, dtype=np.int32) >> k) & 1) * bit
    return masks


def local(n, images, mix_weight, partner, keep_mask, cotangent, weight_in, weight_out, weight_down, small_params,
          first_in, second_in, first_out, second_out, first_down, second_down, first_small, second_small):
    imgs, side = images.shape[:2]
    half = side // 2
    pixels = side * side * imgs
    me = lax.axis_index("dp")
    bits = [1 << k for k in range(n.bit_length() - 1)]
    deep = FF // n
    by_hops = n == 32

    pair, down = ready(weight_in, weight_out, weight_down)
    p_origin = d_origin = w_origin = jnp.arange(32, dtype=jnp.int32)
    if by_hops:
        p_order = [16, 8, 4, 2, 1]
        w_order = [16, 8, 2, 4, 1]
        d_order = [16, 2, 8, 4, 1]
        p_origin = me ^ masks_of(n, p_order)
        w_origin = me ^ masks_of(n, w_order)
        d_origin = me ^ masks_of(n, d_order)

    img = images.transpose(1, 2, 0, 3)
    dy = cotangent.transpose(1, 2, 0, 3)
    flat = lambda a: a.reshape(pixels, a.shape[-1])
    paired = lambda a: a.reshape(half, 2, half, 2, imgs, a.shape[-1])
    square = lambda a: a.reshape(side, side, imgs, a.shape[-1])

    cut = [0, 3, 10, side]
    gates = None
    if by_hops:
        gates = {1: pair}
        pair = join(pair, swap(pair, p_order[0], n))
        gates[2] = pair
        down = join(down, swap(down, w_order[0], n))
        gates[3] = down
        pair = join(pair, swap(pair, p_order[1], n))
        gates[4] = pair
    small = gather_natural(small_params.astype(BF16), n, bits[1:] + bits[:1], gates).reshape(-1, D).astype(F32)
    if by_hops:
        down = join(down, swap(down, w_order[1], n))
    mixed, *made = conv_forward(small, (img, partner, mix_weight), cut[0], cut[1])
    for part in (1, 2):
        if by_hops:
            pair = join(pair, swap(pair, p_order[part + 1], n), made[2:3])
            down = join(down, swap(down, w_order[part + 1], n), made[2:3])
        made = conv_forward(small, (mixed,), cut[part], cut[part + 1], tuple(made), (pair, down))
    unit1, inv1, norm1 = made
    if by_hops:
        pair = (pair, swap(pair, p_order[4], n))
        down = (down, swap(down, w_order[4], n))
    else:
        pair, down = (lax.all_gather(x[0], "dp", axis=0, tiled=True).reshape(2, FF // 2, 2 * D) for x in (pair, down))
    pair = tuple(x.reshape(FF // 2, 2 * D) for x in pair)
    down = tuple(x.reshape(FF // 2, 2 * D) for x in down)
    act, dg, branch, unit2, inv2, norm2 = hidden_forward(p_origin, flat(norm1), flat(mixed), pair, small, keep_mask)
    d_near, d_far, gdb, out, bb, sums2, res = down_both(
        w_origin, d_origin, paired(norm2), paired(unit2), paired(inv2), paired(branch), down, dy, small, keep_mask
    )
    shards = (n // 2, deep, 2 * D)
    if by_hops:
        d_keep = d_near.reshape(shards)
        d_come = swap(d_far.reshape(shards), d_order[4], n)
    p_near, p_far, ghb, sums1, back_conv = pair_grad(
        p_origin, flat(bb), act, dg, flat(norm1), flat(unit1), flat(inv1), pair, small, imgs
    )
    back_conv = square(back_conv)
    res = square(res)
    back = functools.partial(images_back, back_conv, small, partner, mix_weight, res)
    if by_hops:
        p_keep = p_near.reshape(shards)
        p_come = swap(p_far.reshape(shards), p_order[4], n)
        d_keep, d_send = fold(d_keep, d_come, after=(sums1,))
        d_come = swap(d_send, d_order[3], n)
        cut = [0, 4, 10, side]
        grad = ()
        for part in range(3):
            grad = (back(cut[part], cut[part + 1], grad, (p_send, d_send) if part else (d_send,)),)
            p_keep, p_send = fold(p_keep, p_come, after=grad)
            p_come = swap(p_send, p_order[3 - part], n)
            if part < 2:
                d_keep, d_send = fold(d_keep, d_come, after=grad)
                d_come = swap(d_send, d_order[2 - part], n)
        gk1 = taps_grad(back_conv, mixed, (0,), (p_send,))
        keep, send = fold(p_keep, p_come, d_keep, d_come, after=(gk1,))
        come = swap(send, p_order[0], n)
        gk2 = taps_grad(back_conv, mixed, (1, 2), (send,))
    else:
        grad = (back(0, side),)
        gk1 = taps_grad(back_conv, mixed, (0,), grad)
        gk2 = taps_grad(back_conv, mixed, (1, 2))
        keep = jnp.stack(
            [
                lax.psum_scatter(jnp.concatenate(x).astype(F32), "dp", scatter_dimension=0, tiled=True)
                for x in ((p_near, p_far), (d_near, d_far))
            ]
        )
        come = jnp.zeros(keep.shape, BF16)

    grads, total = small_total(gk1, gk2, sums1, sums2, ghb, gdb, keep, come)
    for bit in bits[::-1]:
        total = meet(total, swap(total, bit, n), F32 if bit == 1 else BF16)
    states = (weight_in, first_in, second_in, weight_out, first_out, second_out, weight_down, first_down, second_down)
    *news, norm = adam_all(total, grads, states)
    grad_norm = norm[0, 0]
    factor = CLIP_NORM / jnp.maximum(grad_norm, CLIP_NORM)
    shard_len = small_params.shape[0]
    gs = lax.dynamic_slice_in_dim(total[:SQUARES].reshape(-1), me * shard_len, shard_len)
    position = me * shard_len + jnp.arange(shard_len, dtype=jnp.int32)
    small_rate = jnp.where(position < 54 * D + FF, LAYER_DECAY * RATE_VECTOR, RATE_VECTOR)
    small_decay = jnp.where(position < 49 * D, WEIGHT_DECAY, 0.0)
    new_small = adam(small_params, first_small, second_small, gs * factor, small_rate, small_decay)
    return (
        out.transpose(2, 0, 1, 3),
        grad[0].transpose(2, 0, 1, 3),
        grad_norm,
        *news,
        *new_small,
    )


def solution(mesh):
    four = P("dp", None, None, None)
    two = P("dp", None)
    one = P("dp")
    return jax.shard_map(
        functools.partial(local, mesh.shape["dp"]),
        mesh=mesh,
        in_specs=(four, one, one, one, four, two, two, two, one) + (two,) * 6 + (one,) * 2,
        out_specs=(four, four, P()) + (two,) * 9 + (one,) * 3,
        check_vma=False,
    )
```

time: 248 us -> 223 us (0.90)
  other arithmetic: 9.64 us -> 2.35 us
  local copies, waits for them, and re-layouts: 13.1 us -> 6.48 us
  starting transfers between devices: 35.5 us -> 31.3 us
  waiting for transfers between devices: 33.4 us -> 30.1 us
    ppermute x30 -> x29, starting transfers between devices: 35.5 us -> 31.3 us  [swap(): return lax.ppermute(x, 'dp', [(i, i ^ bit) for i in range(n)])]
    ppermute x30 -> x29, waiting for transfers between devices: 33.4 us -> 30.1 us  [swap(): return lax.ppermute(x, 'dp', [(i, i ^ bit) for i in range(n)])]
    unnamed x81 -> x74, local copies, waits for them, and re-layouts: 8.34 us -> 5.56 us
    pallas_call x29 -> x33, Pallas kernels: 152 us -> 149 us  [kernel_call(): pl.pallas_call(body, out_shape=tuple(out), in_specs=specs, out_specs=tupl...]
    gather x3 -> x0, local copies, waits for them, and re-layouts: 2.51 us -> none  [the longest x1 1.36 us: local(): jnp.asarray(p_masks)[me ^ np.arange(n, dtype=np.int32)]]
  transfers between devices with their start and end apart: 30 -> 29, of which waited for: 12 -> 13; matrix products, arithmetic and copies ran while one was open for 4% -> 0% of each run, Pallas kernels for 58% -> 58%
where the time goes in v3:
time: 223 us
  Pallas kernels  150 us (67%)
  starting transfers between devices  31.3 us (14%)
  waiting for transfers between devices  30.1 us (13%)
  local copies, waits for them, and re-layouts  6.48 us (3%)
  other arithmetic  2.35 us (1%)
    pallas_call x33, Pallas kernels, kernel_call(): pl.pallas_call(body, out_shape=tuple(out), in_specs=specs, out_specs=tupl...  149 us
    ppermute x29, starting transfers between devices, swap(): return lax.ppermute(x, 'dp', [(i, i ^ bit) for i in range(n)])  31.3 us
    ppermute x29, waiting for transfers between devices, swap(): return lax.ppermute(x, 'dp', [(i, i ^ bit) for i in range(n)])  30.1 us
    unnamed x74, local copies, waits for them, and re-layouts  5.56 us
  transfers between devices with their start and end apart: 29, of which 13 were waited for; matrix products, arithmetic and copies ran while one was open for 0% of the time, Pallas kernels for 58%

profile of v3, /device:TPU:0, one launch (start us, length us, event | category | flops | bytes accessed | tf_op | source)
XLA Modules:
  0.0 222.6 jit_solution(7938862658518146840)
XLA Ops:
  0.6 0.7 convert_element_type.8
  1.3 2.9 %collective-permute-start = (bf16[744]{0:T(1024)(128)(2,1)S(1)}, bf16[744]{0:T(1024)(128)(2,1)S(1)}, u32[]{:S(2)}, u32[]{:S(2)}) collective-permute-start(bf16[744]{0:T(1024)(128)(2,1)S(1)} %convert_element_type.8), channel_id=1, source_target_pairs={{0,2},{1,3},{2,0},{3,1},{4,6},{5,7},{6,4},{7,5},{8,10},{9,11},{10,... | collective-permute-start | bytes 4472 | tf_op jit(solution)/shard_map/ppermute | solution.py:852
  4.3 1.0 shard_map.307
  5.8 0.7 broadcast_select_fusion.9
  6.6 2.1 collective-permute-start.1
  8.7 2.6 %collective-permute-start.2 = (bf16[1,48,768]{2,1,0:T(8,128)(2,1)S(1)}, bf16[1,48,768]{2,1,0:T(8,128)(2,1)S(1)}, u32[]{:S(2)}, u32[]{:S(2)}) collective-permute-start(bf16[1,48,768]{2,1,0:T(8,128)(2,1)S(1)} %get-tuple-element.75.first_ref), channel_id=1, source_target_pairs={{0,16},{1,17},{2,18},{3,19},{4,20},{5,21},{6,22},{7,23},{8,24},{9,... | collective-permute-start | bytes 221192 | tf_op jit(solution)/shard_map/ppermute | solution.py:852
  11.7 4.4 %collective-permute-done.2.second_ref = bf16[1,48,768]{2,1,0:T(8,128)(2,1)S(1)} collective-permute-done((bf16[1,48,768]{2,1,0:T(8,128)(2,1)S(1)}, bf16[1,48,768]{2,1,0:T(8,128)(2,1)S(1)}, u32[]{:S(2)}, u32[]{:S(2)}) %collective-permute-start.2) | collective-permute-done | bytes 73760 | tf_op jit(solution)/shard_map/ppermute | solution.py:852
  16.1 0.8 collective-permute-start.3
  16.9 2.9 %collective-permute-done.3 = bf16[2,2,744]{2,1,0:T(2,128)(2,1)S(1)} collective-permute-done((bf16[2,2,744]{2,1,0:T(2,128)(2,1)S(1)}, bf16[2,2,744]{2,1,0:T(2,128)(2,1)S(1)}, u32[]{:S(2)}, u32[]{:S(2)}) %collective-permute-start.3) | collective-permute-done | bytes 5984 | tf_op jit(solution)/shard_map/ppermute | solution.py:852
  19.8 2.2 collective-permute-start.5
  22.0 2.1 collective-permute-start.6
  24.6 2.7 %collective-permute-done.6.second_ref = bf16[2,48,768]{2,1,0:T(8,128)(2,1)S(1)} collective-permute-done((bf16[2,48,768]{2,1,0:T(8,128)(2,1)S(1)}, bf16[2,48,768]{2,1,0:T(8,128)(2,1)S(1)}, u32[]{:S(2)}, u32[]{:S(2)}) %collective-permute-start.6) | collective-permute-done | bytes 147488 | tf_op jit(solution)/shard_map/ppermute | solution.py:852
  27.8 1.4 collective-permute-done.9.second_ref
  29.3 1.6 collective-permute-start.10
  31.0 0.8 reshape.113.refs_0_.small_hbm
  31.9 9.4 %shard_map.311 = (f32[14,14,16,384]{3,2,1,0:T(8,128)}, bf16[14,14,16,384]{3,2,1,0:T(8,128)(2,1)}, f32[14,14,16,1]{3,2,1,0:T(8,128)}, bf16[14,14,16,384]{3,2,1,0:T(8,128)(2,1)}) custom-call(f32[62,384]{1,0:T(8,128)} %reshape.113.refs_0_.small_hbm, bf16[14,14,16,384]{3,2,1,0:T(8,128)(2,1)} %bitcast.52, s32[16]{0:T(128)S(1)} %copy-done.25, f32[16]{0:T(128)S(1)} %copy-done.26), custom_call_target="tpu_custom_call" | custom-call | flops 7500000256 | tf_op jit(solution)/shard_map/pallas_call | solution.py:64
  42.0 0.8 collective-permute-start.11
  42.8 13.3 %shard_map.315 = (bf16[14,14,16,384]{3,2,1,0:T(8,128)(2,1)}, f32[14,14,16,1]{3,2,1,0:T(8,128)}, bf16[14,14,16,384]{3,2,1,0:T(8,128)(2,1)}) custom-call(f32[62,384]{1,0:T(8,128)} %reshape.113.refs_0_.small_hbm, f32[14,14,16,384]{3,2,1,0:T(8,128)} %get-tuple-element.81.refs_1_.mixed_hbm, ...), custom_call_target="tpu_custom_call", output_to_operand_aliasing={{0}: (2, {}), {1}: (3, {}), {2}: (4, {})} | custom-call | flops 10499999744 | tf_op jit(solution)/shard_map/pallas_call | solution.py:64
  56.2 0.7 collective-permute-done.11.second_ref
  56.8 1.1 copy-done.3
  59.4 8.0 %shard_map.318 = (bf16[14,14,16,384]{3,2,1,0:T(8,128)(2,1)}, f32[14,14,16,1]{3,2,1,0:T(8,128)}, bf16[14,14,16,384]{3,2,1,0:T(8,128)(2,1)}) custom-call(f32[62,384]{1,0:T(8,128)} %reshape.113.refs_0_.small_hbm, f32[14,14,16,384]{3,2,1,0:T(8,128)} %get-tuple-element.81.refs_1_.mixed_hbm, ...), custom_call_target="tpu_custom_call", output_to_operand_aliasing={{0}: (2, {}), {1}: (3, {}), {2}: (4, {})} | custom-call | flops 6000000000 | tf_op jit(solution)/shard_map/pallas_call | solution.py:64
  67.4 1.0 copy-done.34
  68.4 20.5 %shard_map.319 = (bf16[3136,1536]{1,0:T(8,128)(2,1)}, bf16[3136,1536]{1,0:T(8,128)(2,1)}, bf16[3136,384]{1,0:T(8,128)(2,1)}, bf16[3136,384]{1,0:T(8,128)(2,1)}, ...) custom-call(s32[32]{0:T(128)S(1)} %broadcast_xor_fusion.origin_ref, bf16[3136,384]{1,0:T(8,128)(2,1)} %bitcast.50, ...), custom_call_target="tpu_custom_call" | custom-call | flops 16999999488 | tf_op jit(solution)/shard_map/pallas_call | solution.py:64
  88.9 1.0 copy-done.35
  89.9 19.0 %shard_map.320 = (bf16[768,768]{1,0:T(8,128)(2,1)S(1)}, bf16[768,768]{1,0:T(8,128)(2,1)S(1)}, f32[16,768]{1,0:T(8,128)S(1)}, bf16[7,7,16,768]{3,2,1,0:T(8,128)(2...) custom-call(s32[32]{0:T(128)S(1)} %get-tuple-element.149.home_ref, ...), custom_call_target="tpu_custom_call" | custom-call | flops 20000000000 | tf_op jit(solution)/shard_map/pallas_call | solution.py:64
  109.3 29.0 %shard_map.321 = (bf16[768,768]{1,0:T(8,128)(2,1)S(1)}, bf16[768,768]{1,0:T(8,128)(2,1)S(1)}, f32[16,1536]{1,0:T(8,128)S(1)}, f32[3,16,384]{2,1,0:T(8,128)S(1)}, f32[3136,384]{1,0:T(8,128)}) custom-call(s32[32]{0:T(128)S(1)} %broadcast_xor_fusion.origin_ref, bf16[3136,384]{1,0:T(8,128)(2,1)} %bitcast.66, bf16[3136,1536]{1,0:T(8,128)(2,1)} %get-tuple-element.95.act_hbm, ...), custom_call_target="tpu_custom_call" | custom-call | flops 32000000000 | tf_op jit(solution)/shard_map/pallas_call | solution.py:64
  139.4 1.0 collective-permute-start.17
  140.4 8.4 %shard_map.323.refs_2_.rest_0_ = f32[14,14,16,384]{3,2,1,0:T(8,128)} custom-call(f32[14,14,16,384]{3,2,1,0:T(8,128)} %bitcast.58, f32[62,384]{1,0:T(8,128)} %reshape.113.refs_0_.small_hbm, s32[16]{0:T(128)S(1)} %copy-done.25, f32[16]{0:T(128)S(1)} %copy-done.26, f32[14,14,16,384]{3,2,1,0:T(8,128)} %bitcast.63, bf16[8,48,768]{2,1,0:T(8,128)(2,1)} %copy-done.9), custom_call_target="tpu_custom_call" | custom-call | flops 6285714432 | tf_op jit(solution)/shard_map/pallas_call | solution.py:64
  149.2 1.4 collective-permute-start.18
  150.5 4.6 %collective-permute-done.17.refs_1_ = bf16[8,48,768]{2,1,0:T(8,128)(2,1)S(1)} collective-permute-done((bf16[8,48,768]{2,1,0:T(8,128)(2,1)S(1)}, bf16[8,48,768]{2,1,0:T(8,128)(2,1)S(1)}, u32[]{:S(2)}, u32[]{:S(2)}) %collective-permute-start.17) | collective-permute-done | bytes 589856 | tf_op jit(solution)/shard_map/ppermute | solution.py:852
  155.2 2.1 collective-permute-start.19
  157.3 13.1 %shard_map.326.refs_2_.rest_0_ = f32[14,14,16,384]{3,2,1,0:T(8,128)} custom-call(f32[14,14,16,384]{3,2,1,0:T(8,128)} %bitcast.59, f32[62,384]{1,0:T(8,128)} %reshape.113.refs_0_.small_hbm, s32[16]{0:T(128)S(1)} %copy-done.25, f32[16]{0:T(128)S(1)} %copy-done.26, f32[14,14,16,384]{3,2,1,0:T(8,128)} %bitcast.64, ...), custom_call_target="tpu_custom_call", output_to_operand_aliasing={{}: (5, {})} | custom-call | flops 9428571136 | tf_op jit(solution)/shard_map/pallas_call | solution.py:64
  171.3 1.3 collective-permute-start.22
  172.6 8.5 %shard_map.329.refs_2_ = f32[14,14,16,384]{3,2,1,0:T(8,128)} custom-call(f32[14,14,16,384]{3,2,1,0:T(8,128)} %bitcast.60, f32[62,384]{1,0:T(8,128)} %reshape.113.refs_0_.small_hbm, s32[16]{0:T(128)S(1)} %copy-done.25, f32[16]{0:T(128)S(1)} %copy-done.26, f32[14,14,16,384]{3,2,1,0:T(8,128)} %bitcast.65, ...), custom_call_target="tpu_custom_call", output_to_operand_aliasing={{}: (5, {})} | custom-call | flops 6285714432 | tf_op jit(solution)/shard_map/pallas_call | solution.py:64
  181.2 0.7 collective-permute-start.21
  181.9 6.3 %shard_map.331.refs_4_.gk1_ref = f32[49,8,128]{2,1,0:T(8,128)S(1)} custom-call(f32[14,14,16,384]{3,2,1,0:T(8,128)} %bitcast.61, f32[14,14,16,384]{3,2,1,0:T(8,128)} %get-tuple-element.81.refs_1_.mixed_hbm, bf16[2,48,768]{2,1,0:T(8,128)(2,1)} %copy-done.17), custom_call_target="tpu_custom_call" | custom-call | flops 4700000256 | tf_op jit(solution)/shard_map/pallas_call | solution.py:64
  189.6 10.7 %shard_map.333.gk2_ref = f32[49,8,256]{2,1,0:T(8,128)S(1)} custom-call(f32[14,14,16,384]{3,2,1,0:T(8,128)} %bitcast.62, f32[14,14,16,384]{3,2,1,0:T(8,128)} %get-tuple-element.81.refs_1_.mixed_hbm, bf16[2,48,768]{2,1,0:T(8,128)(2,1)} %copy-done.16), custom_call_target="tpu_custom_call" | custom-call | flops 9400000512 | tf_op jit(solution)/shard_map/pallas_call | solution.py:64
  200.7 2.4 %collective-permute-start.24 = (bf16[64,384]{1,0:T(8,128)(2,1)S(1)}, bf16[64,384]{1,0:T(8,128)(2,1)S(1)}, u32[]{:S(2)}, u32[]{:S(2)}) collective-permute-start(bf16[64,384]{1,0:T(8,128)(2,1)S(1)} %get-tuple-element.123.mine_ref), channel_id=1, source_target_pairs={{0,16},{1,17},{2,18},{3,19},{4,20},{5,21},{6,22},{7,23},{8,24},{9,... | collective-permute-start | bytes 147464 | tf_op jit(solution)/shard_map/ppermute | solution.py:852
  203.2 2.6 %collective-permute-done.24.come_ref = bf16[64,384]{1,0:T(8,128)(2,1)S(1)} collective-permute-done((bf16[64,384]{1,0:T(8,128)(2,1)S(1)}, bf16[64,384]{1,0:T(8,128)(2,1)S(1)}, u32[]{:S(2)}, u32[]{:S(2)}) %collective-permute-start.24) | collective-permute-done | bytes 49184 | tf_op jit(solution)/shard_map/ppermute | solution.py:852
  205.9 1.4 collective-permute-start.25
  207.4 2.7 %collective-permute-done.25.come_ref = bf16[64,384]{1,0:T(8,128)(2,1)S(1)} collective-permute-done((bf16[64,384]{1,0:T(8,128)(2,1)S(1)}, bf16[64,384]{1,0:T(8,128)(2,1)S(1)}, u32[]{:S(2)}, u32[]{:S(2)}) %collective-permute-start.25) | collective-permute-done | bytes 49184 | tf_op jit(solution)/shard_map/ppermute | solution.py:852
  210.1 1.4 collective-permute-start.26
  211.5 2.8 %collective-permute-done.26.come_ref = bf16[64,384]{1,0:T(8,128)(2,1)S(1)} collective-permute-done((bf16[64,384]{1,0:T(8,128)(2,1)S(1)}, bf16[64,384]{1,0:T(8,128)(2,1)S(1)}, u32[]{:S(2)}, u32[]{:S(2)}) %collective-permute-start.26) | collective-permute-done | bytes 49184 | tf_op jit(solution)/shard_map/ppermute | solution.py:852
  214.3 0.9 collective-permute-start.27
  215.2 3.3 %collective-permute-done.27.come_ref = bf16[64,384]{1,0:T(8,128)(2,1)S(1)} collective-permute-done((bf16[64,384]{1,0:T(8,128)(2,1)S(1)}, bf16[64,384]{1,0:T(8,128)(2,1)S(1)}, u32[]{:S(2)}, u32[]{:S(2)}) %collective-permute-start.27) | collective-permute-done | bytes 49184 | tf_op jit(solution)/shard_map/ppermute | solution.py:852
  218.5 1.2 collective-permute-done.28.come_ref
  219.9 1.3 shard_map.340
  221.9 0.7 multiply_subtract_fusion
  (137 shorter events, 9.2 us)
Async XLA Ops:
  1.3 4.5 %collective-permute-start = (bf16[744]{0:T(1024)(128)(2,1)S(1)}, bf16[744]{0:T(1024)(128)(2,1)S(1)}, u32[]{:S(2)}, u32[]{:S(2)}) collective-permute-start(bf16[744]{0:T(1024)(128)(2,1)S(1)} %convert_element_type.8), channel_id=1, source_target_pairs={{0,2},{1,3},{2,0},{3,1},{4,6},{5,7},{6,4},{7,5},{8,10},{9,11},{10,... | collective-permute-start | bytes 4472 | tf_op jit(solution)/shard_map/ppermute | solution.py:852
  6.6 5.0 %collective-permute-start.1 = (bf16[2,744]{1,0:T(2,128)(2,1)S(1)}, bf16[2,744]{1,0:T(2,128)(2,1)S(1)}, u32[]{:S(2)}, u32[]{:S(2)}) collective-permute-start(bf16[2,744]{1,0:T(2,128)(2,1)S(1)} %pad_maximum_fusion.3), channel_id=1, source_target_pairs={{0,4},{1,5},{2,6},{3,7},{4,0},{5,1},{6,2},{7,3},{8,12},{9,13},{10,... | collective-permute-start | bytes 8936 | tf_op jit(solution)/shard_map/ppermute | solution.py:852
  8.7 7.4 %collective-permute-start.2 = (bf16[1,48,768]{2,1,0:T(8,128)(2,1)S(1)}, bf16[1,48,768]{2,1,0:T(8,128)(2,1)S(1)}, u32[]{:S(2)}, u32[]{:S(2)}) collective-permute-start(bf16[1,48,768]{2,1,0:T(8,128)(2,1)S(1)} %get-tuple-element.75.first_ref), channel_id=1, source_target_pairs={{0,16},{1,17},{2,18},{3,19},{4,20},{5,21},{6,22},{7,23},{8,24},{9,... | collective-permute-start | bytes 221192 | tf_op jit(solution)/shard_map/ppermute | solution.py:852
  11.3 5.6 %collective-permute-start.4 = (bf16[1,48,768]{2,1,0:T(8,128)(2,1)S(1)}, bf16[1,48,768]{2,1,0:T(8,128)(2,1)S(1)}, u32[]{:S(2)}, u32[]{:S(2)}) collective-permute-start(bf16[1,48,768]{2,1,0:T(8,128)(2,1)S(1)} %get-tuple-element.78.first_ref), channel_id=1, source_target_pairs={{0,16},{1,17},{2,18},{3,19},{4,20},{5,21},{6,22},{7,23},{8,24},{9,... | collective-permute-start | bytes 221192 | tf_op jit(solution)/shard_map/ppermute | solution.py:852
  16.1 3.7 %collective-permute-start.3 = (bf16[2,2,744]{2,1,0:T(2,128)(2,1)S(1)}, bf16[2,2,744]{2,1,0:T(2,128)(2,1)S(1)}, u32[]{:S(2)}, u32[]{:S(2)}) collective-permute-start(bf16[2,2,744]{2,1,0:T(2,128)(2,1)S(1)} %pad_maximum_fusion.2), channel_id=1, source_target_pairs={{0,8},{1,9},{2,10},{3,11},{4,12},{5,13},{6,14},{7,15},{8,0},{9,1},... | collective-permute-start | bytes 17864 | tf_op jit(solution)/shard_map/ppermute | solution.py:852
  16.9 15.0 %copy-start.25 = (s32[16]{0:T(128)S(1)}, s32[16]{0:T(128)}, u32[]{:S(2)}) copy-start(s32[16]{0:T(128)} %partner_ref.5) | copy-start | bytes 196
  16.9 15.0 %copy-start.26 = (f32[16]{0:T(128)S(1)}, f32[16]{0:T(128)}, u32[]{:S(2)}) copy-start(f32[16]{0:T(128)} %weight_ref.5) | copy-start | bytes 196
  19.8 4.7 %collective-permute-start.5 = (bf16[2,2,2,744]{3,2,1,0:T(2,128)(2,1)S(1)}, bf16[2,2,2,744]{3,2,1,0:T(2,128)(2,1)S(1)}, u32[]{:S(2)}, u32[]{:S(2)}) collective-permute-start(bf16[2,2,2,744]{3,2,1,0:T(2,128)(2,1)S(1)} %pad_maximum_fusion.1), channel_id=1, source_target_pairs={{0,16},{1,17},{2,18},{3,19},{4,20},{5,21},{6,22},{7,23},{8,24},{9,... | collective-permute-start | bytes 35720 | tf_op jit(solution)/shard_map/ppermute | solution.py:852
  22.0 5.2 %collective-permute-start.6 = (bf16[2,48,768]{2,1,0:T(8,128)(2,1)S(1)}, bf16[2,48,768]{2,1,0:T(8,128)(2,1)S(1)}, u32[]{:S(2)}, u32[]{:S(2)}) collective-permute-start(bf16[2,48,768]{2,1,0:T(8,128)(2,1)S(1)} %shard_map.308.first_ref), channel_id=1, source_target_pairs={{0,8},{1,9},{2,10},{3,11},{4,12},{5,13},{6,14},{7,15},{8,0},{9,1},... | collective-permute-start | bytes 442376 | tf_op jit(solution)/shard_map/ppermute | solution.py:852
  24.1 5.1 %collective-permute-start.9 = (bf16[2,48,768]{2,1,0:T(8,128)(2,1)S(1)}, bf16[2,48,768]{2,1,0:T(8,128)(2,1)S(1)}, u32[]{:S(2)}, u32[]{:S(2)}) collective-permute-start(bf16[2,48,768]{2,1,0:T(8,128)(2,1)S(1)} %shard_map.309.first_ref), channel_id=1, source_target_pairs={{0,8},{1,9},{2,10},{3,11},{4,12},{5,13},{6,14},{7,15},{8,0},{9,1},... | collective-permute-start | bytes 442376 | tf_op jit(solution)/shard_map/ppermute | solution.py:852
  27.2 14.7 %collective-permute-start.8 = (bf16[4,48,768]{2,1,0:T(8,128)(2,1)S(1)}, bf16[4,48,768]{2,1,0:T(8,128)(2,1)S(1)}, u32[]{:S(2)}, u32[]{:S(2)}) collective-permute-start(bf16[4,48,768]{2,1,0:T(8,128)(2,1)S(1)} %shard_map.310.first_ref), channel_id=1, source_target_pairs={{0,4},{1,5},{2,6},{3,7},{4,0},{5,1},{6,2},{7,3},{8,12},{9,13},{10,... | collective-permute-start | bytes 884744 | tf_op jit(solution)/shard_map/ppermute | solution.py:852
  27.8 3.0 %collective-permute-start.7 = (bf16[2,2,2,2,744]{4,3,2,1,0:T(2,128)(2,1)S(1)}, bf16[2,2,2,2,744]{4,3,2,1,0:T(2,128)(2,1)S(1)}, u32[]{:S(2)}, u32[]{:S(2)}) collective-permute-start(bf16[2,2,2,2,744]{4,3,2,1,0:T(2,128)(2,1)S(1)} %pad_maximum_fusion), channel_id=1, source_target_pairs={{0,1},{1,0},{2,3},{3,2},{4,5},{5,4},{6,7},{7,6},{8,9},{9,8},{10,11... | collective-permute-start | bytes 71432 | tf_op jit(solution)/shard_map/ppermute | solution.py:852
  29.3 12.0 %collective-permute-start.10 = (bf16[4,48,768]{2,1,0:T(8,128)(2,1)S(1)}, bf16[4,48,768]{2,1,0:T(8,128)(2,1)S(1)}, u32[]{:S(2)}, u32[]{:S(2)}) collective-permute-start(bf16[4,48,768]{2,1,0:T(8,128)(2,1)S(1)} %shard_map.313.first_ref), channel_id=1, source_target_pairs={{0,2},{1,3},{2,0},{3,1},{4,6},{5,7},{6,4},{7,5},{8,10},{9,11},{10,... | collective-permute-start | bytes 884744 | tf_op jit(solution)/shard_map/ppermute | solution.py:852
  41.4 16.8 %collective-permute-start.12 = (bf16[8,48,768]{2,1,0:T(8,128)(2,1)S(1)}, bf16[8,48,768]{2,1,0:T(8,128)(2,1)S(1)}, u32[]{:S(2)}, u32[]{:S(2)}) collective-permute-start(bf16[8,48,768]{2,1,0:T(8,128)(2,1)S(1)} %shard_map.314.refs_6_.first_ref), channel_id=1, source_target_pairs={{0,4},{1,5},{2,6},{3,7},{4,0},{5,1},{6,2},{7,3},{8,12},{9,13},{10,... | collective-permute-start | bytes 1769480 | tf_op jit(solution)/shard_map/ppermute | solution.py:852
  42.0 14.8 %collective-permute-start.11 = (bf16[8,48,768]{2,1,0:T(8,128)(2,1)S(1)}, bf16[8,48,768]{2,1,0:T(8,128)(2,1)S(1)}, u32[]{:S(2)}, u32[]{:S(2)}) collective-permute-start(bf16[8,48,768]{2,1,0:T(8,128)(2,1)S(1)} %shard_map.312.refs_5_.first_ref), channel_id=1, source_target_pairs={{0,2},{1,3},{2,0},{3,1},{4,6},{5,7},{6,4},{7,5},{8,10},{9,11},{10,... | collective-permute-start | bytes 1769480 | tf_op jit(solution)/shard_map/ppermute | solution.py:852
  42.8 15.3 %copy-start.36 = (s32[32]{0:T(128)S(1)}, s32[32]{0:T(128)}, u32[]{:S(2)}) copy-start(s32[32]{0:T(128)} %constant.56.clone) | copy-start | bytes 388
  42.8 15.3 %copy-start.32 = (s32[32]{0:T(128)S(1)}, s32[32]{0:T(128)}, u32[]{:S(2)}) copy-start(s32[32]{0:T(128)} %constant.57.clone) | copy-start | bytes 388
  42.8 15.3 %copy-start.33 = (s32[32]{0:T(128)S(1)}, s32[32]{0:T(128)}, u32[]{:S(2)}) copy-start(s32[32]{0:T(128)} %constant.58.clone) | copy-start | bytes 388
  58.0 9.3 %collective-permute-start.13 = (bf16[16,48,768]{2,1,0:T(8,128)(2,1)S(1)}, bf16[16,48,768]{2,1,0:T(8,128)(2,1)S(1)}, u32[]{:S(2)}, u32[]{:S(2)}) collective-permute-start(bf16[16,48,768]{2,1,0:T(8,128)(2,1)S(1)} %shard_map.316.refs_5_), channel_id=1, source_target_pairs={{0,1},{1,0},{2,3},{3,2},{4,5},{5,4},{6,7},{7,6},{8,9},{9,8},{10,11... | collective-permute-start | bytes 3538952 | tf_op jit(solution)/shard_map/ppermute | solution.py:852
  58.2 30.6 %collective-permute-start.14 = (bf16[16,48,768]{2,1,0:T(8,128)(2,1)S(1)}, bf16[16,48,768]{2,1,0:T(8,128)(2,1)S(1)}, u32[]{:S(2)}, u32[]{:S(2)}) collective-permute-start(bf16[16,48,768]{2,1,0:T(8,128)(2,1)S(1)} %shard_map.317.refs_6_), channel_id=1, source_target_pairs={{0,1},{1,0},{2,3},{3,2},{4,5},{5,4},{6,7},{7,6},{8,9},{9,8},{10,11... | collective-permute-start | bytes 3538952 | tf_op jit(solution)/shard_map/ppermute | solution.py:852
  59.4 9.0 %copy-start.24 = (s32[16]{0:T(128)S(1)}, s32[16]{0:T(128)}, u32[]{:S(2)}) copy-start(s32[16]{0:T(128)} %mask_ref.3) | copy-start | bytes 196
  108.9 30.2 %collective-permute-start.15 = (bf16[16,48,768]{2,1,0:T(8,128)(2,1)S(1)}, bf16[16,48,768]{2,1,0:T(8,128)(2,1)S(1)}, u32[]{:S(2)}, u32[]{:S(2)}) collective-permute-start(bf16[16,48,768]{2,1,0:T(8,128)(2,1)S(1)} %bitcast.47), channel_id=1, source_target_pairs={{0,1},{1,0},{2,3},{3,2},{4,5},{5,4},{6,7},{7,6},{8,9},{9,8},{10,11... | collective-permute-start | bytes 3538952 | tf_op jit(solution)/shard_map/ppermute | solution.py:852
  139.0 9.8 %collective-permute-start.16 = (bf16[16,48,768]{2,1,0:T(8,128)(2,1)S(1)}, bf16[16,48,768]{2,1,0:T(8,128)(2,1)S(1)}, u32[]{:S(2)}, u32[]{:S(2)}) collective-permute-start(bf16[16,48,768]{2,1,0:T(8,128)(2,1)S(1)} %bitcast.48), channel_id=1, source_target_pairs={{0,1},{1,0},{2,3},{3,2},{4,5},{5,4},{6,7},{7,6},{8,9},{9,8},{10,11... | collective-permute-start | bytes 3538952 | tf_op jit(solution)/shard_map/ppermute | solution.py:852
  139.4 15.7 %collective-permute-start.17 = (bf16[8,48,768]{2,1,0:T(8,128)(2,1)S(1)}, bf16[8,48,768]{2,1,0:T(8,128)(2,1)S(1)}, u32[]{:S(2)}, u32[]{:S(2)}) collective-permute-start(bf16[8,48,768]{2,1,0:T(8,128)(2,1)S(1)} %get-tuple-element.104.rest_0_), channel_id=1, source_target_pairs={{0,4},{1,5},{2,6},{3,7},{4,0},{5,1},{6,2},{7,3},{8,12},{9,13},{10,... | collective-permute-start | bytes 1769480 | tf_op jit(solution)/shard_map/ppermute | solution.py:852
  149.2 6.1 %copy-start.8 = (bf16[8,48,768]{2,1,0:T(8,128)(2,1)}, bf16[8,48,768]{2,1,0:T(8,128)(2,1)S(1)}, u32[]{:S(2)}) copy-start(bf16[8,48,768]{2,1,0:T(8,128)(2,1)S(1)} %get-tuple-element.107.rest_1_) | copy-start | bytes 1769476
  149.2 21.3 %collective-permute-start.18 = (bf16[8,48,768]{2,1,0:T(8,128)(2,1)S(1)}, bf16[8,48,768]{2,1,0:T(8,128)(2,1)S(1)}, u32[]{:S(2)}, u32[]{:S(2)}) collective-permute-start(bf16[8,48,768]{2,1,0:T(8,128)(2,1)S(1)} %get-tuple-element.107.rest_1_), channel_id=1, source_target_pairs={{0,2},{1,3},{2,0},{3,1},{4,6},{5,7},{6,4},{7,5},{8,10},{9,11},{10,... | collective-permute-start | bytes 1769480 | tf_op jit(solution)/shard_map/ppermute | solution.py:852
  155.2 2.1 copy-start.11
  155.2 16.0 %collective-permute-start.19 = (bf16[4,48,768]{2,1,0:T(8,128)(2,1)S(1)}, bf16[4,48,768]{2,1,0:T(8,128)(2,1)S(1)}, u32[]{:S(2)}, u32[]{:S(2)}) collective-permute-start(bf16[4,48,768]{2,1,0:T(8,128)(2,1)S(1)} %get-tuple-element.109.rest_2_), channel_id=1, source_target_pairs={{0,8},{1,9},{2,10},{3,11},{4,12},{5,13},{6,14},{7,15},{8,0},{9,1},... | collective-permute-start | bytes 884744 | tf_op jit(solution)/shard_map/ppermute | solution.py:852
  170.6 10.5 %collective-permute-start.20 = (bf16[4,48,768]{2,1,0:T(8,128)(2,1)S(1)}, bf16[4,48,768]{2,1,0:T(8,128)(2,1)S(1)}, u32[]{:S(2)}, u32[]{:S(2)}) collective-permute-start(bf16[4,48,768]{2,1,0:T(8,128)(2,1)S(1)} %get-tuple-element.111.rest_1_), channel_id=1, source_target_pairs={{0,4},{1,5},{2,6},{3,7},{4,0},{5,1},{6,2},{7,3},{8,12},{9,13},{10,... | collective-permute-start | bytes 884744 | tf_op jit(solution)/shard_map/ppermute | solution.py:852
  171.3 17.6 %collective-permute-start.22 = (bf16[2,48,768]{2,1,0:T(8,128)(2,1)S(1)}, bf16[2,48,768]{2,1,0:T(8,128)(2,1)S(1)}, u32[]{:S(2)}, u32[]{:S(2)}) collective-permute-start(bf16[2,48,768]{2,1,0:T(8,128)(2,1)S(1)} %get-tuple-element.113.rest_2_), channel_id=1, source_target_pairs={{0,2},{1,3},{2,0},{3,1},{4,6},{5,7},{6,4},{7,5},{8,10},{9,11},{10,... | collective-permute-start | bytes 442376 | tf_op jit(solution)/shard_map/ppermute | solution.py:852
  181.2 7.7 %collective-permute-start.21 = (bf16[2,48,768]{2,1,0:T(8,128)(2,1)S(1)}, bf16[2,48,768]{2,1,0:T(8,128)(2,1)S(1)}, u32[]{:S(2)}, u32[]{:S(2)}) collective-permute-start(bf16[2,48,768]{2,1,0:T(8,128)(2,1)S(1)} %get-tuple-element.115.rest_0_), channel_id=1, source_target_pairs={{0,8},{1,9},{2,10},{3,11},{4,12},{5,13},{6,14},{7,15},{8,0},{9,1},... | collective-permute-start | bytes 442376 | tf_op jit(solution)/shard_map/ppermute | solution.py:852
  188.9 11.4 %copy-start.7 = (f32[3,16,384]{2,1,0:T(8,128)S(1)}, f32[3,16,384]{2,1,0:T(8,128)}, u32[]{:S(2)}) copy-start(f32[3,16,384]{2,1,0:T(8,128)} %copy-done.6) | copy-start | bytes 221188
  189.0 11.4 %copy-start.28 = (f32[49,8,128]{2,1,0:T(8,128)S(1)}, f32[49,8,128]{2,1,0:T(8,128)}, u32[]{:S(2)}) copy-start(f32[49,8,128]{2,1,0:T(8,128)} %copy-done.27) | copy-start | bytes 602116
  189.0 11.3 %collective-permute-start.23 = (bf16[2,48,768]{2,1,0:T(8,128)(2,1)S(1)}, bf16[2,48,768]{2,1,0:T(8,128)(2,1)S(1)}, u32[]{:S(2)}, u32[]{:S(2)}) collective-permute-start(bf16[2,48,768]{2,1,0:T(8,128)(2,1)S(1)} %get-tuple-element.118.rest_0_), channel_id=1, source_target_pairs={{0,16},{1,17},{2,18},{3,19},{4,20},{5,21},{6,22},{7,23},{8,24},{9,... | collective-permute-start | bytes 442376 | tf_op jit(solution)/shard_map/ppermute | solution.py:852
  200.7 5.1 %collective-permute-start.24 = (bf16[64,384]{1,0:T(8,128)(2,1)S(1)}, bf16[64,384]{1,0:T(8,128)(2,1)S(1)}, u32[]{:S(2)}, u32[]{:S(2)}) collective-permute-start(bf16[64,384]{1,0:T(8,128)(2,1)S(1)} %get-tuple-element.123.mine_ref), channel_id=1, source_target_pairs={{0,16},{1,17},{2,18},{3,19},{4,20},{5,21},{6,22},{7,23},{8,24},{9,... | collective-permute-start | bytes 147464 | tf_op jit(solution)/shard_map/ppermute | solution.py:852
  205.8 14.0 %copy-start.12 = (f32[48,768]{1,0:T(8,128)S(1)}, f32[48,768]{1,0:T(8,128)}, u32[]{:S(2)}) copy-start(f32[48,768]{1,0:T(8,128)} %refs_6_.1) | copy-start | bytes 442372
  205.8 14.0 %copy-start.13 = (f32[48,768]{1,0:T(8,128)S(1)}, f32[48,768]{1,0:T(8,128)}, u32[]{:S(2)}) copy-start(f32[48,768]{1,0:T(8,128)} %refs_7_.1) | copy-start | bytes 442372
  205.8 14.0 %copy-start.14 = (f32[48,768]{1,0:T(8,128)S(1)}, f32[48,768]{1,0:T(8,128)}, u32[]{:S(2)}) copy-start(f32[48,768]{1,0:T(8,128)} %refs_8_.1) | copy-start | bytes 442372
  205.9 14.0 %copy-start.18 = (f32[48,384]{1,0:T(8,128)S(1)}, f32[48,384]{1,0:T(8,128)}, u32[]{:S(2)}) copy-start(f32[48,384]{1,0:T(8,128)} %refs_0_.1) | copy-start | bytes 221188
  205.9 14.0 %copy-start.19 = (f32[48,384]{1,0:T(8,128)S(1)}, f32[48,384]{1,0:T(8,128)}, u32[]{:S(2)}) copy-start(f32[48,384]{1,0:T(8,128)} %refs_3_.3) | copy-start | bytes 221188
  205.9 14.0 %copy-start.20 = (f32[48,384]{1,0:T(8,128)S(1)}, f32[48,384]{1,0:T(8,128)}, u32[]{:S(2)}) copy-start(f32[48,384]{1,0:T(8,128)} %refs_1_.1) | copy-start | bytes 221188
  205.9 14.0 %copy-start.21 = (f32[48,384]{1,0:T(8,128)S(1)}, f32[48,384]{1,0:T(8,128)}, u32[]{:S(2)}) copy-start(f32[48,384]{1,0:T(8,128)} %refs_2_.3) | copy-start | bytes 221188
  205.9 14.0 %copy-start.22 = (f32[48,384]{1,0:T(8,128)S(1)}, f32[48,384]{1,0:T(8,128)}, u32[]{:S(2)}) copy-start(f32[48,384]{1,0:T(8,128)} %refs_4_.1) | copy-start | bytes 221188
  205.9 14.0 %copy-start.23 = (f32[48,384]{1,0:T(8,128)S(1)}, f32[48,384]{1,0:T(8,128)}, u32[]{:S(2)}) copy-start(f32[48,384]{1,0:T(8,128)} %refs_5_.1) | copy-start | bytes 221188
  205.9 4.2 %collective-permute-start.25 = (bf16[64,384]{1,0:T(8,128)(2,1)S(1)}, bf16[64,384]{1,0:T(8,128)(2,1)S(1)}, u32[]{:S(2)}, u32[]{:S(2)}) collective-permute-start(bf16[64,384]{1,0:T(8,128)(2,1)S(1)} %shard_map.335.mine_ref), channel_id=1, source_target_pairs={{0,8},{1,9},{2,10},{3,11},{4,12},{5,13},{6,14},{7,15},{8,0},{9,1},... | collective-permute-start | bytes 147464 | tf_op jit(solution)/shard_map/ppermute | solution.py:852
  210.1 4.2 %collective-permute-start.26 = (bf16[64,384]{1,0:T(8,128)(2,1)S(1)}, bf16[64,384]{1,0:T(8,128)(2,1)S(1)}, u32[]{:S(2)}, u32[]{:S(2)}) collective-permute-start(bf16[64,384]{1,0:T(8,128)(2,1)S(1)} %shard_map.336.mine_ref), channel_id=1, source_target_pairs={{0,4},{1,5},{2,6},{3,7},{4,0},{5,1},{6,2},{7,3},{8,12},{9,13},{10,... | collective-permute-start | bytes 147464 | tf_op jit(solution)/shard_map/ppermute | solution.py:852
  214.3 4.2 %collective-permute-start.27 = (bf16[64,384]{1,0:T(8,128)(2,1)S(1)}, bf16[64,384]{1,0:T(8,128)(2,1)S(1)}, u32[]{:S(2)}, u32[]{:S(2)}) collective-permute-start(bf16[64,384]{1,0:T(8,128)(2,1)S(1)} %shard_map.337.mine_ref), channel_id=1, source_target_pairs={{0,2},{1,3},{2,0},{3,1},{4,6},{5,7},{6,4},{7,5},{8,10},{9,11},{10,... | collective-permute-start | bytes 147464 | tf_op jit(solution)/shard_map/ppermute | solution.py:852
  218.5 1.3 collective-permute-start.28
  (18 other events, 21.2 us)
